TPU v7x, 256 devices: a whole 4x4x8 slice. The times are simulated.
256 devices in a mesh: row: 8 (over x, y_lo), col: 32 (over z, y_hi, core).
Axes of the slice: x: 4, y: 4 (y_hi: 2, y_lo: 2; y = y_hi * 2 + y_lo), z: 8, core: 2. Of those that a mesh axis runs over, the one named last changes fastest.
Arguments:
- query_map: bfloat16 [128, 512, 1024], P('row', 'col'), may hold values from -12 to 12
- key_map: bfloat16 [128, 512, 1024], P('row', 'col'), may hold values from -12 to 12
- value_map: bfloat16 [128, 512, 1024], P('row', 'col'), may hold values from -6 to 6
- out_grad: bfloat16 [128, 512, 2048], P('row', 'col'), may hold values from -6 to 6
- keep_mask: int32 [128, 512, 2048], P('row', 'col'), may hold values 0 or 1
- log_scale: float32 [32], replicated, may hold values from 1 to 4.6
- bias_table: float32 [32, 31, 31], replicated, may hold values from 0 to 16
- proj_weight: bfloat16 [1024, 2048], replicated, may hold values from -0.1875 to 0.1875
Outputs:
- query_grad: bfloat16 [128, 512, 1024], P('row', 'col')
- key_grad: bfloat16 [128, 512, 1024], P('row', 'col')
- value_grad: bfloat16 [128, 512, 1024], P('row', 'col')
- weight_grad: float32 [1024, 2048], P(('row', 'col'))
- table_grad: float32 [32, 31, 31], replicated
- scale_grad: float32 [32], replicated
All inputs are finite; a program needn't handle non-finite values. No bound on the sum of `keep_mask` on one device may be relied on, other than what follows from the above.
Results may differ from a plain program's by a relative error of at most 0.013.
The roundings to bfloat16 on the way count: a program that leaves them out, or rounds other values in their place, can miss the bound.
Values may be sent and summed in bfloat16 or wider, within the bound.
No kernel may reach another device: no remote copies, remote signals or barrier semaphores. Data moves between devices by JAX's collectives and lax.ppermute only.
A program may use at most 192 MiB of HBM per device.

v0:
```python
import functools

import jax
import jax.numpy as jnp
import numpy as np
from jax import lax
from jax.experimental import pallas as pl
from jax.experimental.pallas import tpu as pltpu
from jax.sharding import PartitionSpec as P

D = 2048
HEADS = 32
HEAD_DIM = 32
INNER = 1024
WINDOWS = 256
KEEP_RATE = 0.9
SIDE = 31
LOG2E = 1.4426950408889634

NX, NYL, NZ, NYH, NCORE = 4, 2, 8, 2, 2

F32 = jnp.float32
BF16 = jnp.bfloat16
TILE = 128
PER_TILE = TILE // HEAD_DIM
GROUP = 2
QUAD = 64
TOKENS = 256

VMEM_BYTES = 48 * 1024 * 1024


def params():
    return pltpu.CompilerParams(vmem_limit_bytes=VMEM_BYTES)


def cost(flops, nbytes):
    return pl.CostEstimate(flops=int(flops), bytes_accessed=int(nbytes), transcendentals=0)


def move(value, target):
    sizes = (NX, NYL, NZ, NYH, NCORE)
    pairs = []
    for src in range(NX * NYL * NZ * NYH * NCORE):
        place = np.unravel_index(src, sizes)
        goal = [int(g) % s for g, s in zip(target(*[int(p) for p in place]), sizes)]
        pairs.append((src, int(np.ravel_multi_index(goal, sizes))))
    return lax.ppermute(value, ("row", "col"), pairs)


def move_map(value, d_row, d_col):
    rows, cols = NX * NYL, NZ * NYH * NCORE
    pairs = [
        (r * cols + c, ((r + d_row) % rows) * cols + (c + d_col) % cols)
        for r in range(rows)
        for c in range(cols)
    ]
    return lax.ppermute(value, ("row", "col"), pairs)


def along_x(step):
    return lambda x, yl, z, yh, c: (x + step, yl, z, yh, c)


def along_y(step):
    def goal(x, yl, z, yh, c):
        y = (2 * yh + yl + step) % 4
        return (x, y % 2, z, y // 2, c)

    return goal


def along_z(step):
    return lambda x, yl, z, yh, c: (x, yl, z + step, yh, c)


def other_core(x, yl, z, yh, c):
    return (x, yl, z, yh, 1 - c)


def coordinates():
    row = lax.axis_index("row")
    col = lax.axis_index("col")
    x, y_lo = row // 2, row % 2
    z, y_hi, core = col // 4, (col // 2) % 2, col % 2
    return x, 2 * y_hi + y_lo, z, core


def quarters_of(block):
    n = block.shape[-1]
    cut = lambda a, b: block[a : a + 8, b : b + 8, :].reshape(QUAD, n).astype(BF16)
    return cut(0, 0), cut(0, 8), cut(8, 0), cut(8, 8)


def split_kernel(q_ref, k_ref, v_ref, tl_ref, tr_ref, bl_ref, br_ref):
    for which, ref in enumerate((q_ref, k_ref, v_ref)):
        for out, part in zip((tl_ref, tr_ref, bl_ref, br_ref), quarters_of(ref[...].astype(F32))):
            out[which] = part


def split_maps(query_map, key_map, value_map):
    spec = pl.BlockSpec((16, 16, 256), lambda t: (0, 0, t))
    out = pl.BlockSpec((3, QUAD, 256), lambda t: (0, 0, t))
    return pl.pallas_call(
        split_kernel,
        grid=(INNER // 256,),
        in_specs=[spec] * 3,
        out_specs=[out] * 4,
        out_shape=[jax.ShapeDtypeStruct((3, QUAD, INNER), BF16)] * 4,
        compiler_params=params(),
        name="split_maps",
    )(query_map, key_map, value_map)


def drop_kernel(grad_ref, keep_ref, tl_ref, tr_ref, bl_ref, br_ref):
    dropped = grad_ref[...].astype(F32) * keep_ref[...].astype(F32) * (1.0 / KEEP_RATE)
    for out, part in zip((tl_ref, tr_ref, bl_ref, br_ref), quarters_of(dropped)):
        out[...] = part


def split_dropped(out_grad, keep_mask):
    spec = pl.BlockSpec((16, 16, 512), lambda t: (0, 0, t))
    out = pl.BlockSpec((QUAD, 512), lambda t: (0, t))
    return pl.pallas_call(
        drop_kernel,
        grid=(D // 512,),
        in_specs=[spec] * 2,
        out_specs=[out] * 4,
        out_shape=[jax.ShapeDtypeStruct((QUAD, D), BF16)] * 4,
        compiler_params=params(),
        name="split_dropped",
    )(out_grad, keep_mask)


def join_kernel(tl_ref, tr_ref, bl_ref, br_ref, *outs):
    for which, out in enumerate(outs):
        part = lambda ref: ref[which].astype(F32).reshape(8, 8, ref.shape[-1])
        out[:8] = jnp.concatenate([part(tl_ref), part(tr_ref)], axis=1).astype(BF16)
        out[8:] = jnp.concatenate([part(bl_ref), part(br_ref)], axis=1).astype(BF16)


def join_maps(tl, tr, bl, br):
    spec = pl.BlockSpec((3, QUAD, 256), lambda t: (0, 0, t))
    out = pl.BlockSpec((16, 16, 256), lambda t: (0, 0, t))
    return pl.pallas_call(
        join_kernel,
        grid=(INNER // 256,),
        in_specs=[spec] * 4,
        out_specs=[out] * 3,
        out_shape=[jax.ShapeDtypeStruct((16, 16, INNER), BF16)] * 3,
        compiler_params=params(),
        name="join_maps",
    )(tl, tr, bl, br)


def bias_kernel(table_ref, out_ref):
    lane = iota((PER_TILE, 8, 256), 2)
    spread = jnp.where(iota((32, 256), 1) // 8 == iota((32, 256), 0), 1.0, 0.0)
    wide = jnp.dot(
        table_ref[...].reshape(PER_TILE * 32, 32),
        spread,
        precision=lax.Precision.HIGHEST,
        preferred_element_type=F32,
    ).reshape(PER_TILE, 32, 256)
    for d in range(3):
        strip = jnp.zeros((PER_TILE, 8, 256), F32)
        for xi in range(8):
            first = 23 - 8 * d - xi
            strip = jnp.where(lane % 8 == xi, wide[:, first : first + 8, :], strip)
        strip = strip.reshape(PER_TILE * 8, 256)
        for yj in range(16):
            start = 8 * (15 - yj)
            moved = strip if start == 0 else pltpu.roll(strip, 256 - start, 1)
            out_ref[:, d, 8 * yj : 8 * yj + 8, :] = moved[:, :128].reshape(PER_TILE, 8, 128)


def bias_blocks(bias_table):
    table = jnp.pad(bias_table * LOG2E, ((0, 0), (0, 1), (0, 0)))
    table = jnp.pad(jnp.flip(table.transpose(0, 2, 1), 1), ((0, 0), (0, 1), (0, 0)))
    return pl.pallas_call(
        bias_kernel,
        grid=(HEADS // PER_TILE,),
        in_specs=[pl.BlockSpec((PER_TILE, 32, 32), lambda t: (t, 0, 0))],
        out_specs=pl.BlockSpec((PER_TILE, 3, 128, 128), lambda t: (t, 0, 0, 0)),
        out_shape=jax.ShapeDtypeStruct((HEADS, 3, 128, 128), F32),
        compiler_params=params(),
        cost_estimate=cost(1e7, 8e6),
        name="bias_blocks",
    )(table)


def iota(shape, dim):
    return lax.broadcasted_iota(jnp.int32, shape, dim)


def per_head_sum(value):
    high = value.astype(BF16)
    low = (value - high.astype(F32)).astype(BF16)
    shape = (2 * TILE, TILE)
    same = (iota(shape, 0) % TILE) // HEAD_DIM == iota(shape, 1) // HEAD_DIM
    ones = jnp.where(same, 1.0, 0.0).astype(BF16)
    both = jnp.concatenate([high, low], axis=1)
    return jnp.dot(both, ones, preferred_element_type=F32)


def normalize(rows):
    value = rows.astype(F32)
    length = jnp.sqrt(per_head_sum(value * value))
    inverse = 1.0 / jnp.maximum(length, 1.0)
    return value * inverse, length, inverse


def normalize_back(unit, length, inverse, grad):
    projection = per_head_sum(unit * grad)
    return jnp.where(length > 1.0, (grad - unit * projection) * inverse, grad)


def of_head(rows, head):
    keep = iota(rows.shape, 1) // HEAD_DIM == head
    return jnp.where(keep, rows, jnp.zeros_like(rows))


def rows_of(refs, which, tile):
    lanes = slice(TILE * tile, TILE * tile + TILE)
    return jnp.concatenate([ref[which, :, lanes] for ref in refs], axis=0)


def mul(left, right):
    return jnp.dot(left, right, preferred_element_type=F32)


def head_rows(head):
    return slice(HEAD_DIM * head, HEAD_DIM * head + HEAD_DIM)


def cosines_of(k_round, q_round):
    q_t = q_round.T
    return [mul(of_head(k_round, head), q_t) for head in range(PER_TILE)]


def forward_kernel(scale_ref, tl_ref, bl_ref, tr_ref, br_ref, bias_ref, attn_ref, probs_ref):
    step = pl.program_id(0)
    quads = (tl_ref, bl_ref, tr_ref, br_ref)
    cosines, values_t = [], []
    for tile in range(GROUP):
        q_round = normalize(rows_of(quads, 0, tile))[0].astype(BF16)
        k_round = normalize(rows_of(quads, 1, tile))[0].astype(BF16)
        values_t.append(rows_of(quads, 2, tile).T)
        cosines += cosines_of(k_round, q_round)
    rounded = []
    for head in range(GROUP * PER_TILE):
        scale = scale_ref[step * GROUP * PER_TILE + head]
        halves = []
        for half in range(2):
            lanes = slice(128 * half, 128 * half + 128)
            bias = jnp.concatenate([bias_ref[head, 1 + half], bias_ref[head, half]], axis=0)
            scores = cosines[head][:, lanes] * scale + bias
            weights = jnp.exp2(scores - jnp.max(scores, axis=0, keepdims=True))
            probs = weights * (1.0 / jnp.sum(weights, axis=0, keepdims=True))
            probs_ref[head, :, lanes] = probs
            halves.append(probs.astype(BF16))
        rounded.append(jnp.concatenate(halves, axis=1))
    for head in range(GROUP * PER_TILE):
        value_t = values_t[head // PER_TILE][head_rows(head % PER_TILE)]
        attn_ref[head_rows(head), :] = mul(value_t, rounded[head]).astype(BF16)


def quad_spec():
    return pl.BlockSpec((3, QUAD, GROUP * TILE), lambda t: (0, 0, t))


def probs_spec():
    return pl.BlockSpec((GROUP * PER_TILE, TOKENS, TOKENS), lambda t: (t, 0, 0))


def forward(scales, quads, bias):
    return pl.pallas_call(
        forward_kernel,
        grid=(INNER // TILE // GROUP,),
        in_specs=[pl.BlockSpec(memory_space=pltpu.SMEM)]
        + [quad_spec()] * 4
        + [pl.BlockSpec((GROUP * PER_TILE, 3, 128, 128), lambda t: (t, 0, 0, 0))],
        out_specs=[pl.BlockSpec((GROUP * TILE, TOKENS), lambda t: (t, 0)), probs_spec()],
        out_shape=[
            jax.ShapeDtypeStruct((INNER, TOKENS), BF16),
            jax.ShapeDtypeStruct((HEADS, TOKENS, TOKENS), F32),
        ],
        compiler_params=params(),
        cost_estimate=cost(8e9, 16e6),
        name="forward",
    )(scales, *quads, bias)


def diagonal_sums(blocks):
    lane = iota((8, 128), 1)
    strips = []
    for block in blocks:
        total = jnp.zeros((8, 128), F32)
        first = jnp.zeros((8, 128), F32)
        for yj in range(16):
            start = 8 * (15 - yj)
            piece = block[8 * yj : 8 * yj + 8]
            if start:
                piece = pltpu.roll(piece, start, 1)
                first = first + jnp.where(lane >= start, piece, 0.0)
            else:
                first = first + piece
            total = total + piece
        strips.append(jnp.concatenate([first, total - first], axis=1))
    return strips


def offset_sums(strips):
    shape = strips[0].shape
    xj, lane = iota(shape, 0) % 8, iota(shape, 1)
    even = ((lane + xj) // 8) % 2 == 0
    sums = []
    for strip in strips:
        for bit in range(3):
            moved = pltpu.roll(strip, 256 - (1 << bit), 1)
            strip = jnp.where((xj // (1 << bit)) % 2 == 1, moved, strip)
        part = jnp.where(even, strip, 0.0)
        total = lambda v: jnp.sum(v.reshape(PER_TILE, 8, 256), axis=1)
        sums.append((pltpu.roll(total(part), 7, 1), pltpu.roll(total(strip - part), 255, 1)))
    inner = iota((PER_TILE, 256), 1) % 16
    result = []
    for parity in range(2):
        left, middle, right = (pair[parity] for pair in sums)
        result.append(left + jnp.where(inner >= 8, pltpu.roll(middle, 8, 1), 0.0))
        result.append(right + jnp.where(inner < 8, pltpu.roll(middle, 248, 1), 0.0))
    return result


def table_of(strips, log_sums):
    rows = offset_sums(strips)
    spot = iota((PER_TILE, 256), 1) == 240
    rows[2] = jnp.where(spot, jnp.concatenate(log_sums, axis=0), rows[2])
    shape = (32, 256)
    k, lane = iota(shape, 0), iota(shape, 1)
    mine, odd = lane // 16 == k // 2, k % 2 == 1
    total = jnp.zeros((PER_TILE * 32, TILE), F32)
    for half in range(2):
        picked = []
        for head in range(PER_TILE):
            both = jnp.where(odd, rows[2 + half][head : head + 1], rows[half][head : head + 1])
            picked.append(jnp.where(mine, both, 0.0).astype(BF16))
        source, goal = iota((256, TILE), 0), iota((256, TILE), 1)
        place = jnp.where(goal == 16 * half + source % 16, 1.0, 0.0).astype(BF16)
        total = total + mul(jnp.concatenate(picked, axis=0), place)
    table = total[:32]
    for head in range(1, PER_TILE):
        table = table + pltpu.roll(total[32 * head : 32 * head + 32], 32 * head, 1)
    return table


def backward_kernel(
    first_step,
    scale_ref,
    tl_ref,
    bl_ref,
    tr_ref,
    br_ref,
    grad_ref,
    probs_ref,
    *refs,
):
    gtl_ref, gbl_ref, gtr_ref, gbr_ref, table_ref = refs[-5:]
    step = pl.program_id(0) + first_step
    quads = (tl_ref, bl_ref, tr_ref, br_ref)
    heads = range(GROUP * PER_TILE)
    queries, keys, grads, grad_probs, cosines = [], [], [], [], []
    for tile in range(GROUP):
        queries.append(normalize(rows_of(quads, 0, tile)))
        keys.append(normalize(rows_of(quads, 1, tile)))
        grads.append(grad_ref[:, TILE * tile : TILE * tile + TILE])
        value, grad_t = rows_of(quads, 2, tile), grads[-1].T
        grad_probs += [mul(of_head(value, head), grad_t) for head in range(PER_TILE)]
        cosines += cosines_of(keys[-1][0].astype(BF16), queries[-1][0].astype(BF16))
    prob_rounds, grad_coss, blocks, log_sums = [], [], [], []
    for head in heads:
        scale = scale_ref[step * GROUP * PER_TILE + head]
        log_sum = jnp.zeros((1, 128), F32)
        halves, rounded, cos_grads = [], [], []
        for half in range(2):
            lanes = slice(128 * half, 128 * half + 128)
            probs = probs_ref[head, :, lanes]
            part = grad_probs[head][:, lanes]
            inner = jnp.sum(probs * part, axis=0, keepdims=True)
            score_grad = probs * (part - inner)
            halves.append(score_grad)
            log_sum = log_sum + jnp.sum(
                score_grad * cosines[head][:, lanes], axis=0, keepdims=True
            )
            rounded.append(probs.astype(BF16))
            cos_grads.append((score_grad * scale).astype(BF16))
        blocks.append((halves[0][128:], halves[0][:128] + halves[1][128:], halves[1][:128]))
        prob_rounds.append(jnp.concatenate(rounded, axis=1))
        grad_coss.append(jnp.concatenate(cos_grads, axis=1))
        log_sums.append(scale * jnp.sum(log_sum, axis=1, keepdims=True))
    for tile in range(GROUP):
        grad_v = jnp.zeros((TOKENS, TILE), F32)
        grad_k = jnp.zeros((TOKENS, TILE), F32)
        grad_q = []
        q_round, key_t = queries[tile][0].astype(BF16), keys[tile][0].astype(BF16).T
        for head in range(PER_TILE):
            grad_cos = grad_coss[PER_TILE * tile + head]
            grad_q.append(mul(key_t[head_rows(head)], grad_cos))
            grad_v = grad_v + mul(prob_rounds[PER_TILE * tile + head], of_head(grads[tile], head))
            grad_k = grad_k + mul(grad_cos, of_head(q_round, head))
        results = (
            normalize_back(*queries[tile], jnp.concatenate(grad_q, axis=0).T).astype(BF16),
            normalize_back(*keys[tile], grad_k).astype(BF16),
            grad_v.astype(BF16),
        )
        lanes = slice(TILE * tile, TILE * tile + TILE)
        for part, ref in enumerate((gtl_ref, gbl_ref, gtr_ref, gbr_ref)):
            for which, result in enumerate(results):
                ref[which, :, lanes] = result[QUAD * part : QUAD * part + QUAD]
    for tile in range(GROUP):
        mine = range(PER_TILE * tile, PER_TILE * tile + PER_TILE)
        found = [diagonal_sums(blocks[head]) for head in mine]
        strips = [jnp.concatenate([strip[d] for strip in found], axis=0) for d in range(3)]
        table_ref[tile] = table_of(strips, [log_sums[head] for head in mine]).astype(BF16)


def backward(scales, quads, grad_attn, probs, half, earlier=()):
    steps = INNER // TILE // GROUP // 2
    first = half * steps
    quad = pl.BlockSpec((3, QUAD, GROUP * TILE), lambda t: (0, 0, t + first))
    return pl.pallas_call(
        functools.partial(backward_kernel, first),
        grid=(steps,),
        in_specs=[pl.BlockSpec(memory_space=pltpu.SMEM)]
        + [quad] * 4
        + [
            pl.BlockSpec((TOKENS, GROUP * TILE), lambda t: (0, t + first)),
            pl.BlockSpec((GROUP * PER_TILE, TOKENS, TOKENS), lambda t: (t + first, 0, 0)),
        ]
        + [pl.BlockSpec(memory_space=pl.ANY)] * len(earlier),
        out_specs=[quad] * 4 + [pl.BlockSpec((GROUP, 32, TILE), lambda t: (t + first, 0, 0))],
        out_shape=[jax.ShapeDtypeStruct((3, QUAD, INNER), BF16)] * 4
        + [jax.ShapeDtypeStruct((INNER // TILE, 32, TILE), BF16)],
        input_output_aliases={7 + i: i for i in range(len(earlier))},
        compiler_params=params(),
        cost_estimate=cost(8e9, 10e6),
        name="backward",
    )(scales, *quads, grad_attn, probs, *earlier)


def outer_kernel(place_ref, own_ref, other_ref, drop_ref, drop_other_ref, *refs):
    outs, left_ref = refs[:NX], refs[NX]
    goal, source = iota((64, TILE), 0), iota((64, TILE), 1)
    wanted = ((goal // 4) % NZ) * 16 + (goal // 32) * 8 + place_ref[3] * 4 + goal % 4
    pick = jnp.where(source == wanted, 1.0, 0.0).astype(BF16)
    for tile in range(INNER // TILE):
        rows, goals = slice(TILE * tile, TILE * tile + TILE), slice(64 * tile, 64 * tile + 64)
        left_ref[goals, :TOKENS] = mul(pick, own_ref[rows, :]).astype(BF16)
        left_ref[goals, TOKENS:] = mul(pick, other_ref[rows, :]).astype(BF16)
    for step, out in enumerate(outs):
        start = pl.multiple_of(((place_ref[0] + step) % NX) * 128, 128)
        left = left_ref[pl.ds(start, 128), :]
        for col in range(0, D, 512):
            part = mul(left[:, :TOKENS], drop_ref[:, col : col + 512])
            part = part + mul(left[:, TOKENS:], drop_other_ref[:, col : col + 512])
            out[:, col : col + 512] = part.astype(out.dtype)


def outer_terms(place, own, other, dropped, dropped_other):
    whole = pl.BlockSpec(memory_space=pltpu.VMEM)
    return pl.pallas_call(
        outer_kernel,
        in_specs=[pl.BlockSpec(memory_space=pltpu.SMEM)] + [whole] * 4,
        out_specs=[whole] * NX,
        out_shape=[jax.ShapeDtypeStruct((128, D), F32 if s == 0 else BF16) for s in range(NX)],
        scratch_shapes=[pltpu.VMEM((512, 2 * TOKENS), BF16)],
        compiler_params=params(),
        cost_estimate=cost(1.1e9, 6e6),
        name="outer_terms",
    )(place, own, other, dropped, dropped_other)


def sum_y_kernel(place_ref, *refs):
    terms, outs = refs[:4], refs[4:8]
    for step, out in enumerate(outs):
        y = (place_ref[1] + step) % 4
        start = pl.multiple_of(((y % 2) * 2 + y // 2) * 32, 32)
        rows = pl.ds(start, 32)
        total = terms[0][rows, :]
        for term in terms[1:]:
            total = total + term[rows, :].astype(F32)
        out[...] = total.astype(out.dtype)


def sum_for_y(place, terms):
    whole = pl.BlockSpec(memory_space=pltpu.VMEM)
    return pl.pallas_call(
        sum_y_kernel,
        in_specs=[pl.BlockSpec(memory_space=pltpu.SMEM)] + [whole] * 4,
        out_specs=[whole] * 4,
        out_shape=[jax.ShapeDtypeStruct((32, D), F32 if s == 0 else BF16) for s in range(4)],
        compiler_params=params(),
        name="sum_for_y",
    )(place, *terms)


def sum_z_kernel(*refs):
    terms, out = refs[:4], refs[4]
    total = terms[0][...]
    for term in terms[1:]:
        total = total + term[...].astype(F32)
    for z in range(NZ):
        out[z] = total[4 * z : 4 * z + 4].astype(BF16)


def sum_for_z(terms):
    whole = pl.BlockSpec(memory_space=pltpu.VMEM)
    return pl.pallas_call(
        sum_z_kernel,
        in_specs=[whole] * 4,
        out_specs=whole,
        out_shape=jax.ShapeDtypeStruct((NZ, 4, D), BF16),
        compiler_params=params(),
        name="sum_for_z",
    )(*terms)


def place_scalars():
    x, y, z, core = coordinates()
    return jnp.stack([x, y, z, core]).astype(jnp.int32)


def weight_total(place, terms):
    terms = sum_for_y(place, terms)
    terms = [terms[0]] + [move(terms[s], along_y(s)) for s in range(1, 4)]
    rest = NYH * NCORE
    groups = [[rest * z + one for z in range(NZ)] for one in range(rest)]
    found = lax.all_to_all(
        sum_for_z(terms), "col", 0, 0, axis_index_groups=groups, tiled=True
    )
    return jnp.sum(found.astype(F32), axis=0)


def table_pieces(part):
    found = lax.all_to_all(part.reshape(WINDOWS, 1, TILE), ("row", "col"), 0, 0, tiled=True)
    return jnp.sum(found.astype(F32), axis=0, keepdims=True) / WINDOWS


def table_whole(piece):
    same = jnp.broadcast_to(piece, (WINDOWS, 1, TILE))
    return lax.all_to_all(same, ("row", "col"), 0, 0, tiled=True)


def unpack_kernel(total_ref, table_ref):
    for tile in range(INNER // TILE):
        for head in range(PER_TILE):
            rows = total_ref[32 * tile : 32 * tile + 32, 32 * head : 32 * head + 32]
            table_ref[PER_TILE * tile + head] = rows[:SIDE, :SIDE]


def unpack_table(total):
    whole = pl.BlockSpec(memory_space=pltpu.VMEM)
    total = total.reshape(WINDOWS, TILE)
    table = pl.pallas_call(
        unpack_kernel,
        in_specs=[whole],
        out_specs=whole,
        out_shape=jax.ShapeDtypeStruct((HEADS, SIDE, SIDE), F32),
        compiler_params=params(),
        name="unpack_table",
    )(total)
    return table, total[31::32, ::32].reshape(HEADS)


def per_device(
    query_map, key_map, value_map, out_grad, keep_mask, log_scale, bias_table, proj_weight
):
    logit_scale = jnp.exp(log_scale)
    tl, tr, bl, br = split_maps(query_map, key_map, value_map)
    quads = (br, move_map(tr, -1, 0), move_map(bl, 0, -1), move_map(tl, -1, -1))
    bias = bias_blocks(bias_table)
    tl, tr, bl, br = split_dropped(out_grad, keep_mask)
    bias, tr, bl = lax.optimization_barrier((bias, tr, bl))
    up, left = move_map(tr, -1, 0), move_map(bl, 0, -1)
    quads, tl = lax.optimization_barrier((quads, tl))
    attn_t, probs = forward(logit_scale * LOG2E, quads, bias)
    pieces = (br, up, left, move_map(tl, -1, -1))
    attn_t, pieces = lax.optimization_barrier((attn_t, pieces))
    dropped = jnp.concatenate(pieces, axis=0)
    other, dropped_other = move(attn_t, other_core), move(dropped, other_core)
    grad_attn = lax.dot_general(
        dropped, proj_weight, (((1,), (1,)), ((), ())), preferred_element_type=F32
    ).astype(BF16)
    found = backward(logit_scale, quads, grad_attn, probs, 0)
    found, other, dropped_other = lax.optimization_barrier((found, other, dropped_other))
    place = place_scalars()
    terms = outer_terms(place, attn_t, other, dropped, dropped_other)
    terms, found = lax.optimization_barrier((terms, found))
    g_tl, g_bl, g_tr, g_br, table_part = backward(
        logit_scale, quads, grad_attn, probs, 1, found
    )
    arrived = (move_map(g_br, 1, 1), move_map(g_bl, 1, 0), move_map(g_tr, 0, 1))
    near = [move(terms[s], along_x(s)) for s in (1, 3)]
    near, table_part, across = lax.optimization_barrier((near, table_part, terms[2]))
    terms = (terms[0], near[0], move(across, along_x(2)), near[1])
    piece = table_pieces(table_part)
    piece, arrived = lax.optimization_barrier((piece, arrived))
    grads = join_maps(*arrived, g_tl)
    piece, grads = lax.optimization_barrier((piece, grads))
    table_grad, log_grad = unpack_table(table_whole(piece))
    weight_grad = weight_total(place, terms)
    return (*grads, weight_grad / WINDOWS, table_grad, log_grad)


def solution(mesh):
    return jax.shard_map(
        per_device,
        mesh=mesh,
        in_specs=(
            P("row", "col", None),
            P("row", "col", None),
            P("row", "col", None),
            P("row", "col", None),
            P("row", "col", None),
            P(),
            P(),
            P(),
        ),
        out_specs=(
            P("row", "col", None),
            P("row", "col", None),
            P("row", "col", None),
            P(("row", "col"), None),
            P(),
            P(),
        ),
        check_vma=False,
    )
```

profile of v0, /device:TPU:24, one launch (start us, length us, event | category | flops | bytes accessed | tf_op | source)
XLA Modules:
  0.0 166.7 jit_solution(6115481263546844812)
XLA Ops:
  0.7 1.2 copy-done.2
  1.8 1.0 copy-done.3
  2.9 1.0 copy-done.4
  3.9 1.8 %split_maps.1 = (bf16[3,64,1024]{2,1,0:T(8,128)(2,1)}, bf16[3,64,1024]{2,1,0:T(8,128)(2,1)}, bf16[3,64,1024]{2,1,0:T(8,128)(2,1)}, bf16[3,64,1024]{2,1,0:T(8,128)(2,1)S(1)}) custom-call(bf16[16,16,1024]{2,1,0:T(8,128)(2,1)S(1)} %copy-done.2, bf16[16,16,1024]{2,1,0:T(8,128)(2,1)S(1)} %copy-done.3, bf16[16,16,1024]{2,1,0:T(8,128)(2,1)S(1)} %copy-done.4), custom_call_target="tpu_custom_call" | custom-call | tf_op jit(solution)/shard_map/split_maps/pallas_call | solution.py:104
  5.7 0.7 copy-done.6
  6.4 0.7 collective-permute-start
  7.2 3.4 %collective-permute-start.2 = (bf16[3,64,1024]{2,1,0:T(8,128)(2,1)}, bf16[3,64,1024]{2,1,0:T(8,128)(2,1)}, u32[]{:S(2)}, u32[]{:S(2)}) collective-permute-start(bf16[3,64,1024]{2,1,0:T(8,128)(2,1)} %get-tuple-element.81), channel_id=1, source_target_pairs={{0,255},{1,224},{2,225},{3,226},{4,227},{5,228},{6,229},{7,230},{8... | collective-permute-start | bytes 1179656 | tf_op jit(solution)/shard_map/ppermute | solution.py:58
  10.5 2.2 %copy.26 = f32[32,31,31]{1,2,0:T(8,128)} copy(f32[32,31,31]{2,0,1:T(8,128)} %param.14) | data formatting | bytes 246016 | tf_op args[6]
  12.7 1.1 broadcast_multiply_fusion
  13.8 0.8 pad_bitcast_fusion
  14.7 1.9 %rev.4 = f32[32,31,32]{2,1,0:T(8,128)} reverse(f32[32,31,32]{2,1,0:T(8,128)} %pad_bitcast_fusion), dimensions={1} | reverse | bytes 253952 | tf_op jit(solution)/shard_map/jit(_flip)/rev | solution.py:179
  16.6 1.1 pad.9.table_ref
  17.7 1.8 %split_dropped.1 = (bf16[64,2048]{1,0:T(8,128)(2,1)S(1)}, bf16[64,2048]{1,0:T(8,128)(2,1)}, bf16[64,2048]{1,0:T(8,128)(2,1)}, bf16[64,2048]{1,0:T(8,128)(2,1)S(1)}) custom-call(bf16[16,16,2048]{2,1,0:T(8,128)(2,1)S(1)} %copy-done.1, s32[16,16,2048]{2,1,0:T(8,128)S(1)} %copy-done), custom_call_target="tpu_custom_call" | custom-call | tf_op jit(solution)/shard_map/split_dropped/pallas_call | solution.py:124
  19.5 7.4 %bias_blocks.1.bias_ref = f32[32,3,128,128]{3,2,1,0:T(8,128)} custom-call(f32[32,32,32]{2,1,0:T(8,128)S(1)} %pad.9.table_ref), custom_call_target="tpu_custom_call" | custom-call | flops 10000000 | bytes 8000000 | tf_op jit(solution)/shard_map/bias_blocks/pallas_call | solution.py:180
  27.0 8.3 %collective-permute-start.4 = (bf16[64,2048]{1,0:T(8,128)(2,1)}, bf16[64,2048]{1,0:T(8,128)(2,1)S(1)}, u32[]{:S(2)}, u32[]{:S(2)}) collective-permute-start(bf16[64,2048]{1,0:T(8,128)(2,1)} %get-tuple-element.93), channel_id=1, source_target_pairs={{0,31},{1,0},{2,1},{3,2},{4,3},{5,4},{6,5},{7,6},{8,7},{9,8},{10,9... | collective-permute-start | bytes 786440 | tf_op jit(solution)/shard_map/ppermute | solution.py:58
  35.5 0.6 collective-permute-start.5
  36.1 9.8 %forward.1 = (bf16[1024,256]{1,0:T(8,128)(2,1)S(1)}, f32[32,256,256]{2,1,0:T(8,128)}) custom-call(f32[32]{0:T(128)S(1)} %get-tuple-element.175.scale_ref, bf16[3,64,1024]{2,1,0:T(8,128)(2,1)S(1)} %copy-done.7, bf16[3,64,1024]{2,1,0:T(8,128)(2,1)} %collective-permute-done.bl_ref, bf16[3,64,1024]{2,1,0:T(8,128)(2,1)} %collective-permute-done.1.tr_ref, ...), custom_call_target="tpu_custom_call" | custom-call | flops 8000000000 | bytes 16000000 | tf_op jit(solution)/shard_map/forward/pallas_call | solution.py:277
  45.9 1.0 collective-permute-start.6
  47.3 1.3 convolution_convert_fusion.grad_ref
  48.6 7.2 %backward.2 = (bf16[3,64,1024]{2,1,0:T(8,128)(2,1)S(1)}, bf16[3,64,1024]{2,1,0:T(8,128)(2,1)S(1)}, bf16[3,64,1024]{2,1,0:T(8,128)(2,1)S(1)}, bf16[3,64,1024]{2,1,0:T(8,128)(2,1)S(1)}, bf16[8,32,128]{2,1,0:T(8,128)(2,1)S(1)}) custom-call(f32[32]{0:T(128)S(1)} %get-tuple-element.174.scale_ref, bf16[3,64,1024]{2,1,0:T(8,128)(2,1)S(1)} %copy-done.7, ...), custom_call_target="tpu_custom_call" | custom-call | flops 8000000000 | bytes 10000000 | tf_op jit(solution)/shard_map/backward/pallas_call | solution.py:430
  55.9 2.2 %outer_terms.1 = (f32[128,2048]{1,0:T(8,128)S(1)}, bf16[128,2048]{1,0:T(8,128)(2,1)S(1)}, bf16[128,2048]{1,0:T(8,128)(2,1)S(1)}, bf16[128,2048]{1,0:T(8,128)(2,1)S(1)}) custom-call(s32[4]{0:T(128)S(1)} %pad_add_fusion.place_ref, bf16[1024,256]{1,0:T(8,128)(2,1)S(1)} %get-tuple-element.95.own_ref, bf16[1024,256]{1,0:T(8,128)(2,1)S(1)} %collective-permute-done.6.other_ref, ...), custom_call_target="tpu_custom_call" | custom-call | flops 1100000000 | bytes 6000000 | tf_op jit(solution)/shard_map/outer_terms/pallas_call | solution.py:470
  58.0 1.3 collective-permute-start.8
  59.3 2.0 %collective-permute-start.9 = (bf16[128,2048]{1,0:T(8,128)(2,1)S(1)}, bf16[128,2048]{1,0:T(8,128)(2,1)S(1)}, u32[]{:S(2)}, u32[]{:S(2)}) collective-permute-start(bf16[128,2048]{1,0:T(8,128)(2,1)S(1)} %get-tuple-element.118), channel_id=1, source_target_pairs={{0,192},{1,193},{2,194},{3,195},{4,196},{5,197},{6,198},{7,199},{8... | collective-permute-start | bytes 1572872 | tf_op jit(solution)/shard_map/ppermute | solution.py:48
  61.4 7.1 %backward.3 = (bf16[3,64,1024]{2,1,0:T(8,128)(2,1)S(1)}, bf16[3,64,1024]{2,1,0:T(8,128)(2,1)S(1)}, bf16[3,64,1024]{2,1,0:T(8,128)(2,1)S(1)}, bf16[3,64,1024]{2,1,0:T(8,128)(2,1)S(1)}, bf16[8,32,128]{2,1,0:T(8,128)(2,1)S(1)}) custom-call(f32[32]{0:T(128)S(1)} %get-tuple-element.174.scale_ref, ...), custom_call_target="tpu_custom_call", output_to_operand_aliasing={{0}: (7, {}), {1}: (8, {}), {2}: (9, {}), {3}: (10, {}), {4... | custom-call | flops 8000000000 | bytes 10000000 | tf_op jit(solution)/shard_map/backward/pallas_call | solution.py:430
  68.5 5.1 %collective-permute-done.8.refs_1_ = bf16[128,2048]{1,0:T(8,128)(2,1)S(1)} collective-permute-done((bf16[128,2048]{1,0:T(8,128)(2,1)S(1)}, bf16[128,2048]{1,0:T(8,128)(2,1)S(1)}, u32[]{:S(2)}, u32[]{:S(2)}) %collective-permute-start.8) | collective-permute-done | bytes 524320 | tf_op jit(solution)/shard_map/ppermute | solution.py:48
  73.7 0.8 copy.28
  74.4 11.8 %all-to-all-start = ((bf16[256,1,128]{2,1,0:T(2,128)(2,1)}), bf16[256,1,128]{2,1,0:T(2,128)(2,1)S(1)}, u32[]{:S(2)}, u32[]{:S(2)}) async-start(bf16[256,1,128]{2,1,0:T(2,128)(2,1)} %copy.28), calls=%async_computation | async-start | bytes 262144 | tf_op jit(solution)/shard_map/all_to_all | solution.py:544
  86.3 3.1 %collective-permute-start.13 = (bf16[128,2048]{1,0:T(8,128)(2,1)}, bf16[128,2048]{1,0:T(8,128)(2,1)S(1)}, u32[]{:S(2)}, u32[]{:S(2)}) collective-permute-start(bf16[128,2048]{1,0:T(8,128)(2,1)} %copy-done.5), channel_id=1, source_target_pairs={{0,128},{1,129},{2,130},{3,131},{4,132},{5,133},{6,134},{7,135},{8... | collective-permute-start | bytes 1572872 | tf_op jit(solution)/shard_map/ppermute | solution.py:48
  89.6 1.2 collective-permute-start.11
  90.9 0.8 collective-permute-start.12
  91.7 5.5 %all-to-all-done = bf16[256,1,128]{2,1,0:T(2,128)(2,1)S(1)} async-done(((bf16[256,1,128]{2,1,0:T(2,128)(2,1)}), bf16[256,1,128]{2,1,0:T(2,128)(2,1)S(1)}, u32[]{:S(2)}, u32[]{:S(2)}) %all-to-all-start) | async-done | bytes 65568 | tf_op jit(solution)/shard_map/all_to_all | solution.py:544
  97.4 17.2 %collective-permute-done.10.tl_ref = bf16[3,64,1024]{2,1,0:T(8,128)(2,1)S(1)} collective-permute-done((bf16[3,64,1024]{2,1,0:T(8,128)(2,1)}, bf16[3,64,1024]{2,1,0:T(8,128)(2,1)S(1)}, u32[]{:S(2)}, u32[]{:S(2)}) %collective-permute-start.10) | collective-permute-done | bytes 393248 | tf_op jit(solution)/shard_map/ppermute | solution.py:58
  114.6 4.2 %collective-permute-done.11.tr_ref = bf16[3,64,1024]{2,1,0:T(8,128)(2,1)} collective-permute-done((bf16[3,64,1024]{2,1,0:T(8,128)(2,1)}, bf16[3,64,1024]{2,1,0:T(8,128)(2,1)}, u32[]{:S(2)}, u32[]{:S(2)}) %collective-permute-start.11) | collective-permute-done | bytes 393248 | tf_op jit(solution)/shard_map/ppermute | solution.py:58
  118.9 3.5 %join_maps.1 = (bf16[16,16,1024]{2,1,0:T(8,128)(2,1)}, bf16[16,16,1024]{2,1,0:T(8,128)(2,1)}, bf16[16,16,1024]{2,1,0:T(8,128)(2,1)}) custom-call(bf16[3,64,1024]{2,1,0:T(8,128)(2,1)S(1)} %collective-permute-done.10.tl_ref, bf16[3,64,1024]{2,1,0:T(8,128)(2,1)} %collective-permute-done.11.tr_ref, bf16[3,64,1024]{2,1,0:T(8,128)(2,1)} %collective-permute-done.12.bl_ref, ...), custom_call_target="tpu_custom_call" | custom-call | tf_op jit(solution)/shard_map/join_maps/pallas_call | solution.py:145
  122.3 0.7 broadcast_in_dim.9
  123.1 14.5 %all-to-all-start.2 = ((f32[256,1,128]{2,1,0:T(1,128)}), f32[256,1,128]{2,1,0:T(1,128)S(1)}, u32[]{:S(2)}, u32[]{:S(2)}) async-start(f32[256,1,128]{2,1,0:T(1,128)} %broadcast_in_dim.9), calls=%async_computation.2 | async-start | bytes 262144 | tf_op jit(solution)/shard_map/all_to_all | solution.py:550
  137.6 0.8 sum_for_y.1
  138.3 2.2 %collective-permute-start.14 = (bf16[32,2048]{1,0:T(8,128)(2,1)S(1)}, bf16[32,2048]{1,0:T(8,128)(2,1)S(1)}, u32[]{:S(2)}, u32[]{:S(2)}) collective-permute-start(bf16[32,2048]{1,0:T(8,128)(2,1)S(1)} %get-tuple-element.146), channel_id=1, source_target_pairs={{0,32},{1,33},{2,34},{3,35},{4,36},{5,37},{6,38},{7,39},{8,40},{9,... | collective-permute-start | bytes 393224 | tf_op jit(solution)/shard_map/ppermute | solution.py:48
  140.5 0.8 collective-permute-start.15
  141.5 4.0 %collective-permute-done.14.refs_1_ = bf16[32,2048]{1,0:T(8,128)(2,1)S(1)} collective-permute-done((bf16[32,2048]{1,0:T(8,128)(2,1)S(1)}, bf16[32,2048]{1,0:T(8,128)(2,1)S(1)}, u32[]{:S(2)}, u32[]{:S(2)}) %collective-permute-start.14) | collective-permute-done | bytes 131104 | tf_op jit(solution)/shard_map/ppermute | solution.py:48
  145.4 2.7 %collective-permute-done.15.refs_2_ = bf16[32,2048]{1,0:T(8,128)(2,1)S(1)} collective-permute-done((bf16[32,2048]{1,0:T(8,128)(2,1)S(1)}, bf16[32,2048]{1,0:T(8,128)(2,1)S(1)}, u32[]{:S(2)}, u32[]{:S(2)}) %collective-permute-start.15) | collective-permute-done | bytes 131104 | tf_op jit(solution)/shard_map/ppermute | solution.py:48
  148.2 1.2 collective-permute-done.16.refs_3_
  149.4 0.7 sum_for_z.1
  150.1 6.8 %all-to-all-start.1 = ((bf16[8,4,2048]{2,1,0:T(4,128)(2,1)}), bf16[8,4,2048]{2,1,0:T(4,128)(2,1)S(1)}, u32[]{:S(2)}, u32[]{:S(2)}) async-start(bf16[8,4,2048]{2,1,0:T(4,128)(2,1)} %sum_for_z.1), calls=%async_computation.1 | async-start | bytes 262144 | tf_op jit(solution)/shard_map/all_to_all | solution.py:537
  157.2 0.6 reshape.38
  157.8 1.1 copy.29
  158.9 7.1 %all-to-all-done.1 = bf16[8,4,2048]{2,1,0:T(4,128)(2,1)S(1)} async-done(((bf16[8,4,2048]{2,1,0:T(4,128)(2,1)}), bf16[8,4,2048]{2,1,0:T(4,128)(2,1)S(1)}, u32[]{:S(2)}, u32[]{:S(2)}) %all-to-all-start.1) | async-done | bytes 131104 | tf_op jit(solution)/shard_map/all_to_all | solution.py:537
  166.1 0.6 broadcast_multiply_fusion.1
  (54 shorter events, 1.7 us)
Async XLA Ops:
  0.6 17.1 %copy-start = (s32[16,16,2048]{2,1,0:T(8,128)S(1)}, s32[16,16,2048]{2,1,0:T(8,128)}, u32[]{:S(2)}) copy-start(s32[16,16,2048]{2,1,0:T(8,128)} %keep_ref.1) | copy-start | bytes 6291460
  0.6 17.1 %copy-start.1 = (bf16[16,16,2048]{2,1,0:T(8,128)(2,1)S(1)}, bf16[16,16,2048]{2,1,0:T(8,128)(2,1)}, u32[]{:S(2)}) copy-start(bf16[16,16,2048]{2,1,0:T(8,128)(2,1)} %grad_ref.1) | copy-start | bytes 3145732
  0.7 1.2 copy-start.2
  1.8 1.0 copy-start.3
  2.9 1.0 copy-start.4
  5.7 0.7 copy-start.6
  6.4 29.0 %collective-permute-start = (bf16[3,64,1024]{2,1,0:T(8,128)(2,1)}, bf16[3,64,1024]{2,1,0:T(8,128)(2,1)}, u32[]{:S(2)}, u32[]{:S(2)}) collective-permute-start(bf16[3,64,1024]{2,1,0:T(8,128)(2,1)} %get-tuple-element.79), channel_id=1, source_target_pairs={{0,224},{1,225},{2,226},{3,227},{4,228},{5,229},{6,230},{7,231},{8... | collective-permute-start | bytes 1179656 | tf_op jit(solution)/shard_map/ppermute | solution.py:58
  7.2 28.3 %collective-permute-start.1 = (bf16[3,64,1024]{2,1,0:T(8,128)(2,1)}, bf16[3,64,1024]{2,1,0:T(8,128)(2,1)}, u32[]{:S(2)}, u32[]{:S(2)}) collective-permute-start(bf16[3,64,1024]{2,1,0:T(8,128)(2,1)} %get-tuple-element.80), channel_id=1, source_target_pairs={{0,31},{1,0},{2,1},{3,2},{4,3},{5,4},{6,5},{7,6},{8,7},{9,8},{10,9... | collective-permute-start | bytes 1179656 | tf_op jit(solution)/shard_map/ppermute | solution.py:58
  7.2 28.3 %collective-permute-start.2 = (bf16[3,64,1024]{2,1,0:T(8,128)(2,1)}, bf16[3,64,1024]{2,1,0:T(8,128)(2,1)}, u32[]{:S(2)}, u32[]{:S(2)}) collective-permute-start(bf16[3,64,1024]{2,1,0:T(8,128)(2,1)} %get-tuple-element.81), channel_id=1, source_target_pairs={{0,255},{1,224},{2,225},{3,226},{4,227},{5,228},{6,229},{7,230},{8... | collective-permute-start | bytes 1179656 | tf_op jit(solution)/shard_map/ppermute | solution.py:58
  19.5 7.4 %copy-start.12 = (bf16[64,2048]{1,0:T(8,128)(2,1)}, bf16[64,2048]{1,0:T(8,128)(2,1)S(1)}, u32[]{:S(2)}) copy-start(bf16[64,2048]{1,0:T(8,128)(2,1)S(1)} %get-tuple-element.94) | copy-start | bytes 786436
  19.5 15.9 %copy-start.14 = (f32[32]{0:T(128)S(1)}, f32[32]{0:T(128)}, u32[]{:S(2)}) copy-start(f32[32]{0:T(128)} %param.13) | copy-start | bytes 388
  19.5 16.6 %copy-start.7 = (bf16[3,64,1024]{2,1,0:T(8,128)(2,1)S(1)}, bf16[3,64,1024]{2,1,0:T(8,128)(2,1)}, u32[]{:S(2)}) copy-start(bf16[3,64,1024]{2,1,0:T(8,128)(2,1)} %copy-done.6) | copy-start | bytes 1179652
  26.9 18.9 %collective-permute-start.3 = (bf16[64,2048]{1,0:T(8,128)(2,1)}, bf16[64,2048]{1,0:T(8,128)(2,1)S(1)}, u32[]{:S(2)}, u32[]{:S(2)}) collective-permute-start(bf16[64,2048]{1,0:T(8,128)(2,1)} %get-tuple-element.92), channel_id=1, source_target_pairs={{0,224},{1,225},{2,226},{3,227},{4,228},{5,229},{6,230},{7,231},{8... | collective-permute-start | bytes 786440 | tf_op jit(solution)/shard_map/ppermute | solution.py:58
  27.0 18.8 %collective-permute-start.4 = (bf16[64,2048]{1,0:T(8,128)(2,1)}, bf16[64,2048]{1,0:T(8,128)(2,1)S(1)}, u32[]{:S(2)}, u32[]{:S(2)}) collective-permute-start(bf16[64,2048]{1,0:T(8,128)(2,1)} %get-tuple-element.93), channel_id=1, source_target_pairs={{0,31},{1,0},{2,1},{3,2},{4,3},{5,4},{6,5},{7,6},{8,7},{9,8},{10,9... | collective-permute-start | bytes 786440 | tf_op jit(solution)/shard_map/ppermute | solution.py:58
  35.5 10.4 %collective-permute-start.5 = (bf16[64,2048]{1,0:T(8,128)(2,1)}, bf16[64,2048]{1,0:T(8,128)(2,1)S(1)}, u32[]{:S(2)}, u32[]{:S(2)}) collective-permute-start(bf16[64,2048]{1,0:T(8,128)(2,1)} %copy-done.12), channel_id=1, source_target_pairs={{0,255},{1,224},{2,225},{3,226},{4,227},{5,228},{6,229},{7,230},{8... | collective-permute-start | bytes 786440 | tf_op jit(solution)/shard_map/ppermute | solution.py:58
  36.1 11.2 %copy-start.13 = (bf16[1024,2048]{1,0:T(8,128)(2,1)S(1)}, bf16[1024,2048]{1,0:T(8,128)(2,1)}, u32[]{:S(2)}) copy-start(bf16[1024,2048]{1,0:T(8,128)(2,1)} %param.15) | copy-start | bytes 12582916
  45.9 9.9 %collective-permute-start.6 = (bf16[1024,256]{1,0:T(8,128)(2,1)S(1)}, bf16[1024,256]{1,0:T(8,128)(2,1)S(1)}, u32[]{:S(2)}, u32[]{:S(2)}) collective-permute-start(bf16[1024,256]{1,0:T(8,128)(2,1)S(1)} %get-tuple-element.95.own_ref), channel_id=1, source_target_pairs={{0,1},{1,0},{2,3},{3,2},{4,5},{5,4},{6,7},{7,6},{8,9},{9,8},{10,11... | collective-permute-start | bytes 1572872 | tf_op jit(solution)/shard_map/ppermute | solution.py:48
  47.0 8.8 %collective-permute-start.7 = (bf16[256,2048]{1,0:T(8,128)(2,1)S(1)}, bf16[256,2048]{1,0:T(8,128)(2,1)S(1)}, u32[]{:S(2)}, u32[]{:S(2)}) collective-permute-start(bf16[256,2048]{1,0:T(8,128)(2,1)S(1)} %constant_dynamic-update-slice_fusion.drop_ref), channel_id=1, source_target_pairs={{0,1},{1,0},{2,3},{3,2},{4,5},{5,4},{6,7},{7,6},{8,9},{9,8},{10,11... | collective-permute-start | bytes 3145736 | tf_op jit(solution)/shard_map/ppermute | solution.py:48
  48.6 12.7 %copy-start.8 = (bf16[3,64,1024]{2,1,0:T(8,128)(2,1)S(1)}, bf16[3,64,1024]{2,1,0:T(8,128)(2,1)}, u32[]{:S(2)}) copy-start(bf16[3,64,1024]{2,1,0:T(8,128)(2,1)} %copy-done.6) | copy-start | bytes 1179652
  58.0 10.5 %copy-start.5 = (bf16[128,2048]{1,0:T(8,128)(2,1)}, bf16[128,2048]{1,0:T(8,128)(2,1)S(1)}, u32[]{:S(2)}) copy-start(bf16[128,2048]{1,0:T(8,128)(2,1)S(1)} %get-tuple-element.143) | copy-start | bytes 1572868
  58.0 15.6 %collective-permute-start.8 = (bf16[128,2048]{1,0:T(8,128)(2,1)S(1)}, bf16[128,2048]{1,0:T(8,128)(2,1)S(1)}, u32[]{:S(2)}, u32[]{:S(2)}) collective-permute-start(bf16[128,2048]{1,0:T(8,128)(2,1)S(1)} %get-tuple-element.117), channel_id=1, source_target_pairs={{0,64},{1,65},{2,66},{3,67},{4,68},{5,69},{6,70},{7,71},{8,72},{9,... | collective-permute-start | bytes 1572872 | tf_op jit(solution)/shard_map/ppermute | solution.py:48
  59.3 14.3 %collective-permute-start.9 = (bf16[128,2048]{1,0:T(8,128)(2,1)S(1)}, bf16[128,2048]{1,0:T(8,128)(2,1)S(1)}, u32[]{:S(2)}, u32[]{:S(2)}) collective-permute-start(bf16[128,2048]{1,0:T(8,128)(2,1)S(1)} %get-tuple-element.118), channel_id=1, source_target_pairs={{0,192},{1,193},{2,194},{3,195},{4,196},{5,197},{6,198},{7,199},{8... | collective-permute-start | bytes 1572872 | tf_op jit(solution)/shard_map/ppermute | solution.py:48
  68.5 5.1 %copy-start.10 = (bf16[3,64,1024]{2,1,0:T(8,128)(2,1)}, bf16[3,64,1024]{2,1,0:T(8,128)(2,1)S(1)}, u32[]{:S(2)}) copy-start(bf16[3,64,1024]{2,1,0:T(8,128)(2,1)S(1)} %get-tuple-element.129) | copy-start | bytes 1179652
  68.5 5.1 %copy-start.11 = (bf16[3,64,1024]{2,1,0:T(8,128)(2,1)}, bf16[3,64,1024]{2,1,0:T(8,128)(2,1)S(1)}, u32[]{:S(2)}) copy-start(bf16[3,64,1024]{2,1,0:T(8,128)(2,1)S(1)} %get-tuple-element.127) | copy-start | bytes 1179652
  68.5 20.8 %copy-start.9 = (bf16[3,64,1024]{2,1,0:T(8,128)(2,1)}, bf16[3,64,1024]{2,1,0:T(8,128)(2,1)S(1)}, u32[]{:S(2)}) copy-start(bf16[3,64,1024]{2,1,0:T(8,128)(2,1)S(1)} %get-tuple-element.128) | copy-start | bytes 1179652
  74.4 22.7 %all-to-all-start = ((bf16[256,1,128]{2,1,0:T(2,128)(2,1)}), bf16[256,1,128]{2,1,0:T(2,128)(2,1)S(1)}, u32[]{:S(2)}, u32[]{:S(2)}) async-start(bf16[256,1,128]{2,1,0:T(2,128)(2,1)} %copy.28), calls=%async_computation | async-start | bytes 262144 | tf_op jit(solution)/shard_map/all_to_all | solution.py:544
  86.3 51.3 %collective-permute-start.13 = (bf16[128,2048]{1,0:T(8,128)(2,1)}, bf16[128,2048]{1,0:T(8,128)(2,1)S(1)}, u32[]{:S(2)}, u32[]{:S(2)}) collective-permute-start(bf16[128,2048]{1,0:T(8,128)(2,1)} %copy-done.5), channel_id=1, source_target_pairs={{0,128},{1,129},{2,130},{3,131},{4,132},{5,133},{6,134},{7,135},{8... | collective-permute-start | bytes 1572872 | tf_op jit(solution)/shard_map/ppermute | solution.py:48
  89.4 25.3 %collective-permute-start.10 = (bf16[3,64,1024]{2,1,0:T(8,128)(2,1)}, bf16[3,64,1024]{2,1,0:T(8,128)(2,1)S(1)}, u32[]{:S(2)}, u32[]{:S(2)}) collective-permute-start(bf16[3,64,1024]{2,1,0:T(8,128)(2,1)} %copy-done.11), channel_id=1, source_target_pairs={{0,33},{1,34},{2,35},{3,36},{4,37},{5,38},{6,39},{7,40},{8,41},{9,... | collective-permute-start | bytes 1179656 | tf_op jit(solution)/shard_map/ppermute | solution.py:58
  89.6 29.2 %collective-permute-start.11 = (bf16[3,64,1024]{2,1,0:T(8,128)(2,1)}, bf16[3,64,1024]{2,1,0:T(8,128)(2,1)}, u32[]{:S(2)}, u32[]{:S(2)}) collective-permute-start(bf16[3,64,1024]{2,1,0:T(8,128)(2,1)} %copy-done.9), channel_id=1, source_target_pairs={{0,32},{1,33},{2,34},{3,35},{4,36},{5,37},{6,38},{7,39},{8,40},{9,... | collective-permute-start | bytes 1179656 | tf_op jit(solution)/shard_map/ppermute | solution.py:58
  90.9 28.0 %collective-permute-start.12 = (bf16[3,64,1024]{2,1,0:T(8,128)(2,1)}, bf16[3,64,1024]{2,1,0:T(8,128)(2,1)}, u32[]{:S(2)}, u32[]{:S(2)}) collective-permute-start(bf16[3,64,1024]{2,1,0:T(8,128)(2,1)} %copy-done.10), channel_id=1, source_target_pairs={{0,1},{1,2},{2,3},{3,4},{4,5},{5,6},{6,7},{7,8},{8,9},{9,10},{10,1... | collective-permute-start | bytes 1179656 | tf_op jit(solution)/shard_map/ppermute | solution.py:58
  123.1 27.1 %all-to-all-start.2 = ((f32[256,1,128]{2,1,0:T(1,128)}), f32[256,1,128]{2,1,0:T(1,128)S(1)}, u32[]{:S(2)}, u32[]{:S(2)}) async-start(f32[256,1,128]{2,1,0:T(1,128)} %broadcast_in_dim.9), calls=%async_computation.2 | async-start | bytes 262144 | tf_op jit(solution)/shard_map/all_to_all | solution.py:550
  138.3 7.1 %collective-permute-start.14 = (bf16[32,2048]{1,0:T(8,128)(2,1)S(1)}, bf16[32,2048]{1,0:T(8,128)(2,1)S(1)}, u32[]{:S(2)}, u32[]{:S(2)}) collective-permute-start(bf16[32,2048]{1,0:T(8,128)(2,1)S(1)} %get-tuple-element.146), channel_id=1, source_target_pairs={{0,32},{1,33},{2,34},{3,35},{4,36},{5,37},{6,38},{7,39},{8,40},{9,... | collective-permute-start | bytes 393224 | tf_op jit(solution)/shard_map/ppermute | solution.py:48
  140.5 7.7 %collective-permute-start.15 = (bf16[32,2048]{1,0:T(8,128)(2,1)S(1)}, bf16[32,2048]{1,0:T(8,128)(2,1)S(1)}, u32[]{:S(2)}, u32[]{:S(2)}) collective-permute-start(bf16[32,2048]{1,0:T(8,128)(2,1)S(1)} %get-tuple-element.147), channel_id=1, source_target_pairs={{0,2},{1,3},{2,0},{3,1},{4,6},{5,7},{6,4},{7,5},{8,10},{9,11},{10,... | collective-permute-start | bytes 393224 | tf_op jit(solution)/shard_map/ppermute | solution.py:48
  141.3 8.1 %collective-permute-start.16 = (bf16[32,2048]{1,0:T(8,128)(2,1)S(1)}, bf16[32,2048]{1,0:T(8,128)(2,1)S(1)}, u32[]{:S(2)}, u32[]{:S(2)}) collective-permute-start(bf16[32,2048]{1,0:T(8,128)(2,1)S(1)} %get-tuple-element.148), channel_id=1, source_target_pairs={{0,34},{1,35},{2,32},{3,33},{4,38},{5,39},{6,36},{7,37},{8,42},{9,... | collective-permute-start | bytes 393224 | tf_op jit(solution)/shard_map/ppermute | solution.py:48
  150.1 15.9 %all-to-all-start.1 = ((bf16[8,4,2048]{2,1,0:T(4,128)(2,1)}), bf16[8,4,2048]{2,1,0:T(4,128)(2,1)S(1)}, u32[]{:S(2)}, u32[]{:S(2)}) async-start(bf16[8,4,2048]{2,1,0:T(4,128)(2,1)} %sum_for_z.1), calls=%async_computation.1 | async-start | bytes 262144 | tf_op jit(solution)/shard_map/all_to_all | solution.py:537
where the time goes:
time: 168 us; the launch traced here: 167 us
  starting transfers between devices  59.4 us (35%)
  waiting for transfers between devices  47.1 us (28%)
  Pallas kernels  42.4 us (25%)
  local copies, waits for them, and re-layouts  13.4 us (8%)
  other arithmetic  2.15 us (1%)
    ppermute x9, waiting for transfers between devices, move_map(): return lax.ppermute(value, ('row', 'col'), pairs)  21.5 us
    ppermute x9, starting transfers between devices, move_map(): return lax.ppermute(value, ('row', 'col'), pairs)  15.5 us
    all_to_all x1, starting transfers between devices, table_whole(): return lax.all_to_all(same, ('row', 'col'), 0, 0, tiled=True)  14.5 us
    pallas_call x2, Pallas kernels, backward(): pl.pallas_call(functools.partial(backward_kernel, first), grid=(steps,),...  14.3 us
    ppermute x8, waiting for transfers between devices, move(): return lax.ppermute(value, ('row', 'col'), pairs)  13 us
    all_to_all x1, starting transfers between devices, table_pieces(): lax.all_to_all(part.reshape(WINDOWS, 1, TILE), ('row', 'col'), 0, 0, tile...  11.8 us
    ppermute x8, starting transfers between devices, move(): return lax.ppermute(value, ('row', 'col'), pairs)  10.9 us
    pallas_call x1, Pallas kernels, forward(): pl.pallas_call(forward_kernel, grid=(INNER // TILE // GROUP,), in_specs=[...  9.78 us
  transfers between devices with their start and end apart: 20, of which 8 were waited for; matrix products, arithmetic and copies ran while one was open for 7% of the time, Pallas kernels for 23%

commit v1 on v0

--- a/solution.py
+++ b/solution.py
@@ -24,14 +24,16 @@
 TILE = 128
 PER_TILE = TILE // HEAD_DIM
 GROUP = 2
+BIAS_HEADS = 8
+EARLY = 1
 QUAD = 64
 TOKENS = 256
 
 VMEM_BYTES = 48 * 1024 * 1024
 
 
-def params():
-    return pltpu.CompilerParams(vmem_limit_bytes=VMEM_BYTES)
+def params(vmem=VMEM_BYTES):
+    return pltpu.CompilerParams(vmem_limit_bytes=vmem)
 
 
 def cost(flops, nbytes):
@@ -107,7 +109,7 @@
         in_specs=[spec] * 3,
         out_specs=[out] * 4,
         out_shape=[jax.ShapeDtypeStruct((3, QUAD, INNER), BF16)] * 4,
-        compiler_params=params(),
+        compiler_params=params(60 * 1024 * 1024),
         name="split_maps",
     )(query_map, key_map, value_map)
 
@@ -127,7 +129,7 @@
         in_specs=[spec] * 2,
         out_specs=[out] * 4,
         out_shape=[jax.ShapeDtypeStruct((QUAD, D), BF16)] * 4,
-        compiler_params=params(),
+        compiler_params=params(60 * 1024 * 1024),
         name="split_dropped",
     )(out_grad, keep_mask)
 
@@ -154,39 +156,37 @@
 
 
 def bias_kernel(table_ref, out_ref):
-    lane = iota((PER_TILE, 8, 256), 2)
-    spread = jnp.where(iota((32, 256), 1) // 8 == iota((32, 256), 0), 1.0, 0.0)
-    wide = jnp.dot(
-        table_ref[...].reshape(PER_TILE * 32, 32),
-        spread,
-        precision=lax.Precision.HIGHEST,
-        preferred_element_type=F32,
-    ).reshape(PER_TILE, 32, 256)
+    lane = iota((BIAS_HEADS, 8, 256), 2)
+    turn = jnp.where(iota((SIDE, 32), 0) + iota((SIDE, 32), 1) == 30, LOG2E, 0.0)
+    spread = jnp.where(iota((SIDE, 256), 1) // 8 == iota((SIDE, 256), 0), 1.0, 0.0)
+    exact = dict(precision=lax.Precision.HIGHEST, preferred_element_type=F32)
+    turned = [jnp.dot(table_ref[head], turn, **exact) for head in range(BIAS_HEADS)]
+    wide = jnp.stack(
+        [lax.dot_general(rows, spread, (((0,), (0,)), ((), ())), **exact) for rows in turned]
+    )
     for d in range(3):
-        strip = jnp.zeros((PER_TILE, 8, 256), F32)
+        strip = jnp.zeros((BIAS_HEADS, 8, 256), F32)
         for xi in range(8):
             first = 23 - 8 * d - xi
             strip = jnp.where(lane % 8 == xi, wide[:, first : first + 8, :], strip)
-        strip = strip.reshape(PER_TILE * 8, 256)
+        strip = strip.reshape(BIAS_HEADS * 8, 256)
         for yj in range(16):
             start = 8 * (15 - yj)
             moved = strip if start == 0 else pltpu.roll(strip, 256 - start, 1)
-            out_ref[:, d, 8 * yj : 8 * yj + 8, :] = moved[:, :128].reshape(PER_TILE, 8, 128)
+            out_ref[:, d, 8 * yj : 8 * yj + 8, :] = moved[:, :128].reshape(BIAS_HEADS, 8, 128)
 
 
 def bias_blocks(bias_table):
-    table = jnp.pad(bias_table * LOG2E, ((0, 0), (0, 1), (0, 0)))
-    table = jnp.pad(jnp.flip(table.transpose(0, 2, 1), 1), ((0, 0), (0, 1), (0, 0)))
     return pl.pallas_call(
         bias_kernel,
-        grid=(HEADS // PER_TILE,),
-        in_specs=[pl.BlockSpec((PER_TILE, 32, 32), lambda t: (t, 0, 0))],
-        out_specs=pl.BlockSpec((PER_TILE, 3, 128, 128), lambda t: (t, 0, 0, 0)),
+        grid=(HEADS // BIAS_HEADS,),
+        in_specs=[pl.BlockSpec((BIAS_HEADS, SIDE, SIDE), lambda t: (t, 0, 0))],
+        out_specs=pl.BlockSpec((BIAS_HEADS, 3, 128, 128), lambda t: (t, 0, 0, 0)),
         out_shape=jax.ShapeDtypeStruct((HEADS, 3, 128, 128), F32),
         compiler_params=params(),
         cost_estimate=cost(1e7, 8e6),
         name="bias_blocks",
-    )(table)
+    )(bias_table)
 
 
 def iota(shape, dim):
@@ -423,9 +423,7 @@
         table_ref[tile] = table_of(strips, [log_sums[head] for head in mine]).astype(BF16)
 
 
-def backward(scales, quads, grad_attn, probs, half, earlier=()):
-    steps = INNER // TILE // GROUP // 2
-    first = half * steps
+def backward(scales, quads, grad_attn, probs, first, steps, earlier=()):
     quad = pl.BlockSpec((3, QUAD, GROUP * TILE), lambda t: (0, 0, t + first))
     return pl.pallas_call(
         functools.partial(backward_kernel, first),
@@ -529,8 +527,7 @@
     return jnp.stack([x, y, z, core]).astype(jnp.int32)
 
 
-def weight_total(place, terms):
-    terms = sum_for_y(place, terms)
+def weight_total(terms):
     terms = [terms[0]] + [move(terms[s], along_y(s)) for s in range(1, 4)]
     rest = NYH * NCORE
     groups = [[rest * z + one for z in range(NZ)] for one in range(rest)]
@@ -540,14 +537,23 @@
     return jnp.sum(found.astype(F32), axis=0)
 
 
+def row_exchange(value):
+    return lax.all_to_all(value, "row", 0, 0, tiled=True)
+
+
 def table_pieces(part):
-    found = lax.all_to_all(part.reshape(WINDOWS, 1, TILE), ("row", "col"), 0, 0, tiled=True)
-    return jnp.sum(found.astype(F32), axis=0, keepdims=True) / WINDOWS
+    return jnp.sum(row_exchange(part).astype(F32), axis=0)
+
+
+def table_column(piece):
+    cols = NZ * NYH * NCORE
+    same = jnp.broadcast_to(piece.astype(BF16), (cols, 32, TILE))
+    found = lax.all_to_all(same, "col", 0, 0, tiled=True)
+    return jnp.sum(found.astype(F32), axis=0) / WINDOWS
 
 
 def table_whole(piece):
-    same = jnp.broadcast_to(piece, (WINDOWS, 1, TILE))
-    return lax.all_to_all(same, ("row", "col"), 0, 0, tiled=True)
+    return row_exchange(jnp.broadcast_to(piece, (NX * NYL, 32, TILE)))
 
 
 def unpack_kernel(total_ref, table_ref):
@@ -590,24 +596,26 @@
     grad_attn = lax.dot_general(
         dropped, proj_weight, (((1,), (1,)), ((), ())), preferred_element_type=F32
     ).astype(BF16)
-    found = backward(logit_scale, quads, grad_attn, probs, 0)
+    found = backward(logit_scale, quads, grad_attn, probs, 0, EARLY)
     found, other, dropped_other = lax.optimization_barrier((found, other, dropped_other))
     place = place_scalars()
     terms = outer_terms(place, attn_t, other, dropped, dropped_other)
     terms, found = lax.optimization_barrier((terms, found))
     g_tl, g_bl, g_tr, g_br, table_part = backward(
-        logit_scale, quads, grad_attn, probs, 1, found
+        logit_scale, quads, grad_attn, probs, EARLY, INNER // TILE // GROUP - EARLY, found
     )
     arrived = (move_map(g_br, 1, 1), move_map(g_bl, 1, 0), move_map(g_tr, 0, 1))
     near = [move(terms[s], along_x(s)) for s in (1, 3)]
-    near, table_part, across = lax.optimization_barrier((near, table_part, terms[2]))
-    terms = (terms[0], near[0], move(across, along_x(2)), near[1])
+    across = move(terms[2], along_x(2))
+    near, table_part = lax.optimization_barrier((near, table_part))
     piece = table_pieces(table_part)
-    piece, arrived = lax.optimization_barrier((piece, arrived))
+    terms = sum_for_y(place, (terms[0], near[0], across, near[1]))
+    terms, piece = lax.optimization_barrier((terms, piece))
+    piece = table_column(piece)
+    arrived, piece = lax.optimization_barrier((arrived, piece))
     grads = join_maps(*arrived, g_tl)
-    piece, grads = lax.optimization_barrier((piece, grads))
     table_grad, log_grad = unpack_table(table_whole(piece))
-    weight_grad = weight_total(place, terms)
+    weight_grad = weight_total(terms)
     return (*grads, weight_grad / WINDOWS, table_grad, log_grad)
 
 

time: 168 us -> 169 us (level)
  blocking collectives: 0 us -> 20.3 us
  starting transfers between devices: 59.4 us -> 48 us
  local copies, waits for them, and re-layouts: 13.4 us -> 7.31 us
  waiting for transfers between devices: 47.1 us -> 44.1 us
  Pallas kernels: 42.4 us -> 44.4 us
    all_to_all x0 -> x1, blocking collectives: none -> 20.3 us  [weight_total(): lax.all_to_all(sum_for_z(terms), 'col', 0, 0, axis_index_groups=groups, t...]
    all_to_all x3, starting transfers between devices: 33.1 us -> 17.9 us  [the longest x2 13 us: row_exchange(): return lax.all_to_all(value, 'row', 0, 0, tiled=True)]
    ppermute x9, waiting for transfers between devices: 21.5 us -> 11 us  [move_map(): return lax.ppermute(value, ('row', 'col'), pairs)]
    all_to_all x3, waiting for transfers between devices: 12.6 us -> 17.1 us  [the longest x1 10.4 us: table_column(): found = lax.all_to_all(same, 'col', 0, 0, tiled=True)]
    ppermute x8, starting transfers between devices: 10.9 us -> 15.1 us  [move(): return lax.ppermute(value, ('row', 'col'), pairs)]
    ppermute x8, waiting for transfers between devices: 13 us -> 16 us  [move(): return lax.ppermute(value, ('row', 'col'), pairs)]
    unnamed x35 -> x41, local copies, waits for them, and re-layouts: 7.4 us -> 5.21 us
    pallas_call x1, Pallas kernels: 1.79 us -> 3.84 us  [split_dropped(): pl.pallas_call(drop_kernel, grid=(D // 512,), in_specs=[spec] * 2, out_sp...]
  transfers between devices with their start and end apart: 20 -> 20, of which waited for: 8 -> 10; matrix products, arithmetic and copies ran while one was open for 7% -> 3% of each run, Pallas kernels for 23% -> 23%
where the time goes in v1:
time: 169 us; the launch traced here: 168 us
  starting transfers between devices  48 us (28%)
  Pallas kernels  44.4 us (26%)
  waiting for transfers between devices  44.1 us (26%)
  blocking collectives  20.3 us (12%)
  local copies, waits for them, and re-layouts  7.31 us (4%)
    all_to_all x1, blocking collectives, weight_total(): lax.all_to_all(sum_for_z(terms), 'col', 0, 0, axis_index_groups=groups, t...  20.3 us
    ppermute x8, waiting for transfers between devices, move(): return lax.ppermute(value, ('row', 'col'), pairs)  16 us
    pallas_call x2, Pallas kernels, backward(): pl.pallas_call(functools.partial(backward_kernel, first), grid=(steps,),...  15.3 us
    ppermute x8, starting transfers between devices, move(): return lax.ppermute(value, ('row', 'col'), pairs)  15.1 us
    ppermute x9, starting transfers between devices, move_map(): return lax.ppermute(value, ('row', 'col'), pairs)  15 us
    all_to_all x2, starting transfers between devices, row_exchange(): return lax.all_to_all(value, 'row', 0, 0, tiled=True)  13 us
    ppermute x9, waiting for transfers between devices, move_map(): return lax.ppermute(value, ('row', 'col'), pairs)  11 us
    all_to_all x1, waiting for transfers between devices, table_column(): found = lax.all_to_all(same, 'col', 0, 0, tiled=True)  10.4 us
  transfers between devices with their start and end apart: 20, of which 10 were waited for; matrix products, arithmetic and copies ran while one was open for 3% of the time, Pallas kernels for 23%

profile of v1, /device:TPU:24, one launch (start us, length us, event | category | flops | bytes accessed | tf_op | source)
XLA Modules:
  0.0 168.1 jit_solution(5306804227706037284)
XLA Ops:
  0.6 3.6 %split_maps.1 = (bf16[3,64,1024]{2,1,0:T(8,128)(2,1)}, bf16[3,64,1024]{2,1,0:T(8,128)(2,1)}, bf16[3,64,1024]{2,1,0:T(8,128)(2,1)}, bf16[3,64,1024]{2,1,0:T(8,128)(2,1)}) custom-call(bf16[16,16,1024]{2,1,0:T(8,128)(2,1)} %q_ref.1, bf16[16,16,1024]{2,1,0:T(8,128)(2,1)} %k_ref.1, bf16[16,16,1024]{2,1,0:T(8,128)(2,1)} %v_ref.1), custom_call_target="tpu_custom_call" | custom-call | tf_op jit(solution)/shard_map/split_maps/pallas_call | solution.py:106
  4.3 0.8 collective-permute-start
  5.0 3.3 %collective-permute-start.2 = (bf16[3,64,1024]{2,1,0:T(8,128)(2,1)}, bf16[3,64,1024]{2,1,0:T(8,128)(2,1)S(1)}, u32[]{:S(2)}, u32[]{:S(2)}) collective-permute-start(bf16[3,64,1024]{2,1,0:T(8,128)(2,1)} %get-tuple-element.81), channel_id=1, source_target_pairs={{0,255},{1,224},{2,225},{3,226},{4,227},{5,228},{6,229},{7,230},{8... | collective-permute-start | bytes 1179656 | tf_op jit(solution)/shard_map/ppermute | solution.py:60
  8.4 1.3 copy.23.table_ref
  9.7 3.8 %split_dropped.1 = (bf16[64,2048]{1,0:T(8,128)(2,1)}, bf16[64,2048]{1,0:T(8,128)(2,1)}, bf16[64,2048]{1,0:T(8,128)(2,1)}, bf16[64,2048]{1,0:T(8,128)(2,1)}) custom-call(bf16[16,16,2048]{2,1,0:T(8,128)(2,1)} %grad_ref.1, s32[16,16,2048]{2,1,0:T(8,128)} %keep_ref.1), custom_call_target="tpu_custom_call" | custom-call | tf_op jit(solution)/shard_map/split_dropped/pallas_call | solution.py:126
  13.6 6.5 %bias_blocks.1.bias_ref = f32[32,3,128,128]{3,2,1,0:T(8,128)} custom-call(f32[32,31,31]{2,1,0:T(8,128)S(1)} %copy.23.table_ref), custom_call_target="tpu_custom_call" | custom-call | flops 10000000 | bytes 8000000 | tf_op jit(solution)/shard_map/bias_blocks/pallas_call | solution.py:180
  20.2 8.4 %collective-permute-start.4 = (bf16[64,2048]{1,0:T(8,128)(2,1)S(1)}, bf16[64,2048]{1,0:T(8,128)(2,1)}, u32[]{:S(2)}, u32[]{:S(2)}) collective-permute-start(bf16[64,2048]{1,0:T(8,128)(2,1)S(1)} %copy-done.15), channel_id=1, source_target_pairs={{0,31},{1,0},{2,1},{3,2},{4,3},{5,4},{6,5},{7,6},{8,7},{9,8},{10,9... | collective-permute-start | bytes 786440 | tf_op jit(solution)/shard_map/ppermute | solution.py:60
  28.7 0.5 collective-permute-start.5
  29.3 9.6 %forward.1 = (bf16[1024,256]{1,0:T(8,128)(2,1)S(1)}, f32[32,256,256]{2,1,0:T(8,128)}) custom-call(f32[32]{0:T(128)S(1)} %get-tuple-element.168.scale_ref, bf16[3,64,1024]{2,1,0:T(8,128)(2,1)S(1)} %copy-done, bf16[3,64,1024]{2,1,0:T(8,128)(2,1)S(1)} %collective-permute-done.bl_ref, bf16[3,64,1024]{2,1,0:T(8,128)(2,1)S(1)} %collective-permute-done.1.tr_ref, ...), custom_call_target="tpu_custom_call" | custom-call | flops 8000000000 | bytes 16000000 | tf_op jit(solution)/shard_map/forward/pallas_call | solution.py:277
  38.9 1.0 collective-permute-start.6
  40.0 1.0 constant_dynamic-update-slice_fusion.1
  41.1 0.3 collective-permute-start.7
  41.4 1.3 convolution_convert_fusion.grad_ref
  42.7 5.0 %backward.2 = (bf16[3,64,1024]{2,1,0:T(8,128)(2,1)S(1)}, bf16[3,64,1024]{2,1,0:T(8,128)(2,1)S(1)}, bf16[3,64,1024]{2,1,0:T(8,128)(2,1)S(1)}, bf16[3,64,1024]{2,1,0:T(8,128)(2,1)S(1)}, bf16[8,32,128]{2,1,0:T(8,128)(2,1)}) custom-call(f32[32]{0:T(128)S(1)} %get-tuple-element.169.scale_ref, bf16[3,64,1024]{2,1,0:T(8,128)(2,1)S(1)} %copy-done, ...), custom_call_target="tpu_custom_call" | custom-call | flops 8000000000 | bytes 10000000 | tf_op jit(solution)/shard_map/backward/pallas_call | solution.py:428
  47.7 2.7 %outer_terms.1 = (f32[128,2048]{1,0:T(8,128)S(1)}, bf16[128,2048]{1,0:T(8,128)(2,1)S(1)}, bf16[128,2048]{1,0:T(8,128)(2,1)}, bf16[128,2048]{1,0:T(8,128)(2,1)S(1)}) custom-call(s32[4]{0:T(128)S(1)} %pad_add_fusion.place_ref, bf16[1024,256]{1,0:T(8,128)(2,1)S(1)} %get-tuple-element.100.own_ref, bf16[1024,256]{1,0:T(8,128)(2,1)S(1)} %collective-permute-done.6.other_ref, ...), custom_call_target="tpu_custom_call" | custom-call | flops 1100000000 | bytes 6000000 | tf_op jit(solution)/shard_map/outer_terms/pallas_call | solution.py:468
  50.4 1.2 collective-permute-start.11
  51.6 5.9 %collective-permute-start.12 = (bf16[128,2048]{1,0:T(8,128)(2,1)S(1)}, bf16[128,2048]{1,0:T(8,128)(2,1)S(1)}, u32[]{:S(2)}, u32[]{:S(2)}) collective-permute-start(bf16[128,2048]{1,0:T(8,128)(2,1)S(1)} %get-tuple-element.127), channel_id=1, source_target_pairs={{0,192},{1,193},{2,194},{3,195},{4,196},{5,197},{6,198},{7,199},{8... | collective-permute-start | bytes 1572872 | tf_op jit(solution)/shard_map/ppermute | solution.py:50
  57.5 1.5 collective-permute-start.13
  59.0 1.0 copy-done.3
  60.0 10.4 %backward.3 = (bf16[3,64,1024]{2,1,0:T(8,128)(2,1)S(1)}, bf16[3,64,1024]{2,1,0:T(8,128)(2,1)S(1)}, bf16[3,64,1024]{2,1,0:T(8,128)(2,1)S(1)}, bf16[3,64,1024]{2,1,0:T(8,128)(2,1)S(1)}, bf16[8,32,128]{2,1,0:T(8,128)(2,1)}) custom-call(f32[32]{0:T(128)S(1)} %get-tuple-element.169.scale_ref, ...), custom_call_target="tpu_custom_call", output_to_operand_aliasing={{0}: (7, {}), {1}: (8, {}), {2}: (9, {}), {3}: (10, {}), {4... | custom-call | flops 8000000000 | bytes 10000000 | tf_op jit(solution)/shard_map/backward/pallas_call | solution.py:428
  70.4 9.8 %collective-permute-done.12.refs_3_ = bf16[128,2048]{1,0:T(8,128)(2,1)S(1)} collective-permute-done((bf16[128,2048]{1,0:T(8,128)(2,1)S(1)}, bf16[128,2048]{1,0:T(8,128)(2,1)S(1)}, u32[]{:S(2)}, u32[]{:S(2)}) %collective-permute-start.12) | collective-permute-done | bytes 524320 | tf_op jit(solution)/shard_map/ppermute | solution.py:50
  80.2 6.4 %all-to-all-start = ((bf16[8,32,128]{2,1,0:T(8,128)(2,1)}), bf16[8,32,128]{2,1,0:T(8,128)(2,1)}, u32[]{:S(2)}, u32[]{:S(2)}) async-start(bf16[8,32,128]{2,1,0:T(8,128)(2,1)} %get-tuple-element.136), calls=%async_computation | async-start | bytes 131072 | tf_op jit(solution)/shard_map/all_to_all | solution.py:541
  86.6 0.8 sum_for_y.1
  87.4 0.6 copy-done.11
  88.0 3.7 %all-to-all-done = bf16[8,32,128]{2,1,0:T(8,128)(2,1)} async-done(((bf16[8,32,128]{2,1,0:T(8,128)(2,1)}), bf16[8,32,128]{2,1,0:T(8,128)(2,1)}, u32[]{:S(2)}, u32[]{:S(2)}) %all-to-all-start) | async-done | bytes 65568 | tf_op jit(solution)/shard_map/all_to_all | solution.py:541
  91.8 0.9 convert_reduce_fusion.2
  92.6 3.5 %collective-permute-start.14 = (bf16[32,2048]{1,0:T(8,128)(2,1)}, bf16[32,2048]{1,0:T(8,128)(2,1)S(1)}, u32[]{:S(2)}, u32[]{:S(2)}) collective-permute-start(bf16[32,2048]{1,0:T(8,128)(2,1)} %copy-done.11), channel_id=1, source_target_pairs={{0,32},{1,33},{2,34},{3,35},{4,36},{5,37},{6,38},{7,39},{8,40},{9,... | collective-permute-start | bytes 393224 | tf_op jit(solution)/shard_map/ppermute | solution.py:50
  96.1 0.4 collective-permute-start.15
  96.4 1.3 collective-permute-start.16
  97.8 2.9 %collective-permute-done.14.refs_1_ = bf16[32,2048]{1,0:T(8,128)(2,1)S(1)} collective-permute-done((bf16[32,2048]{1,0:T(8,128)(2,1)}, bf16[32,2048]{1,0:T(8,128)(2,1)S(1)}, u32[]{:S(2)}, u32[]{:S(2)}) %collective-permute-start.14) | collective-permute-done | bytes 131104 | tf_op jit(solution)/shard_map/ppermute | solution.py:50
  100.6 2.0 %collective-permute-done.15.refs_2_ = bf16[32,2048]{1,0:T(8,128)(2,1)S(1)} collective-permute-done((bf16[32,2048]{1,0:T(8,128)(2,1)S(1)}, bf16[32,2048]{1,0:T(8,128)(2,1)S(1)}, u32[]{:S(2)}, u32[]{:S(2)}) %collective-permute-start.15) | collective-permute-done | bytes 131104 | tf_op jit(solution)/shard_map/ppermute | solution.py:50
  102.7 1.3 collective-permute-done.16.refs_3_
  104.0 20.3 %all_to_all.20 = bf16[8,4,2048]{2,1,0:T(4,128)(2,1)S(1)} all-to-all(bf16[8,4,2048]{2,1,0:T(4,128)(2,1)S(1)} %sum_for_z.1), channel_id=1, replica_groups={{0,4,8,12,16,20,24,28},{1,5,9,13,17,21,25,29},{2,6,10,14,18,22,26,30},{..., dimensions={0} | all-to-all | bytes 262144 | tf_op jit(solution)/shard_map/all_to_all | solution.py:534
  124.3 0.7 broadcast_in_dim.6
  125.1 5.0 %all-to-all-start.1 = ((bf16[32,32,128]{2,1,0:T(8,128)(2,1)}), bf16[32,32,128]{2,1,0:T(8,128)(2,1)S(1)}, u32[]{:S(2)}, u32[]{:S(2)}) async-start(bf16[32,32,128]{2,1,0:T(8,128)(2,1)} %broadcast_in_dim.6), calls=%async_computation.1 | async-start | bytes 524288 | tf_op jit(solution)/shard_map/all_to_all | solution.py:551
  130.1 1.8 %collective-permute-start.9 = (bf16[3,64,1024]{2,1,0:T(8,128)(2,1)}, bf16[3,64,1024]{2,1,0:T(8,128)(2,1)S(1)}, u32[]{:S(2)}, u32[]{:S(2)}) collective-permute-start(bf16[3,64,1024]{2,1,0:T(8,128)(2,1)} %copy-done.8), channel_id=1, source_target_pairs={{0,32},{1,33},{2,34},{3,35},{4,36},{5,37},{6,38},{7,39},{8,40},{9,... | collective-permute-start | bytes 1179656 | tf_op jit(solution)/shard_map/ppermute | solution.py:60
  132.0 10.4 %all-to-all-done.1 = bf16[32,32,128]{2,1,0:T(8,128)(2,1)S(1)} async-done(((bf16[32,32,128]{2,1,0:T(8,128)(2,1)}), bf16[32,32,128]{2,1,0:T(8,128)(2,1)S(1)}, u32[]{:S(2)}, u32[]{:S(2)}) %all-to-all-start.1) | async-done | bytes 262176 | tf_op jit(solution)/shard_map/all_to_all | solution.py:551
  142.5 4.6 %collective-permute-done.8.tl_ref = bf16[3,64,1024]{2,1,0:T(8,128)(2,1)S(1)} collective-permute-done((bf16[3,64,1024]{2,1,0:T(8,128)(2,1)}, bf16[3,64,1024]{2,1,0:T(8,128)(2,1)S(1)}, u32[]{:S(2)}, u32[]{:S(2)}) %collective-permute-start.8) | collective-permute-done | bytes 393248 | tf_op jit(solution)/shard_map/ppermute | solution.py:60
  147.1 6.1 %collective-permute-done.9.tr_ref = bf16[3,64,1024]{2,1,0:T(8,128)(2,1)S(1)} collective-permute-done((bf16[3,64,1024]{2,1,0:T(8,128)(2,1)}, bf16[3,64,1024]{2,1,0:T(8,128)(2,1)S(1)}, u32[]{:S(2)}, u32[]{:S(2)}) %collective-permute-start.9) | collective-permute-done | bytes 393248 | tf_op jit(solution)/shard_map/ppermute | solution.py:60
  153.2 0.3 collective-permute-done.10.bl_ref
  153.5 0.7 broadcast_in_dim.7
  154.2 6.5 %all-to-all-start.3 = ((f32[8,32,128]{2,1,0:T(8,128)}), f32[8,32,128]{2,1,0:T(8,128)S(1)}, u32[]{:S(2)}, u32[]{:S(2)}) async-start(f32[8,32,128]{2,1,0:T(8,128)} %broadcast_in_dim.7), calls=%async_computation.3 | async-start | bytes 262144 | tf_op jit(solution)/shard_map/all_to_all | solution.py:541
  160.7 0.6 broadcast_multiply_fusion
  161.3 1.9 %join_maps.1 = (bf16[16,16,1024]{2,1,0:T(8,128)(2,1)}, bf16[16,16,1024]{2,1,0:T(8,128)(2,1)}, bf16[16,16,1024]{2,1,0:T(8,128)(2,1)}) custom-call(bf16[3,64,1024]{2,1,0:T(8,128)(2,1)S(1)} %collective-permute-done.8.tl_ref, bf16[3,64,1024]{2,1,0:T(8,128)(2,1)S(1)} %collective-permute-done.9.tr_ref, bf16[3,64,1024]{2,1,0:T(8,128)(2,1)S(1)} %collective-permute-done.10.bl_ref, ...), custom_call_target="tpu_custom_call" | custom-call | tf_op jit(solution)/shard_map/join_maps/pallas_call | solution.py:147
  163.2 2.9 %all-to-all-done.3 = f32[8,32,128]{2,1,0:T(8,128)S(1)} async-done(((f32[8,32,128]{2,1,0:T(8,128)}), f32[8,32,128]{2,1,0:T(8,128)S(1)}, u32[]{:S(2)}, u32[]{:S(2)}) %all-to-all-start.3) | async-done | bytes 131104 | tf_op jit(solution)/shard_map/all_to_all | solution.py:541
  166.2 0.2 unpack_table.1
  166.4 0.6 reshape.19
  167.0 1.1 copy.24
  (58 shorter events, 0.8 us)
Async XLA Ops:
  4.3 24.4 %collective-permute-start = (bf16[3,64,1024]{2,1,0:T(8,128)(2,1)}, bf16[3,64,1024]{2,1,0:T(8,128)(2,1)S(1)}, u32[]{:S(2)}, u32[]{:S(2)}) collective-permute-start(bf16[3,64,1024]{2,1,0:T(8,128)(2,1)} %get-tuple-element.79), channel_id=1, source_target_pairs={{0,224},{1,225},{2,226},{3,227},{4,228},{5,229},{6,230},{7,231},{8... | collective-permute-start | bytes 1179656 | tf_op jit(solution)/shard_map/ppermute | solution.py:60
  5.0 23.7 %collective-permute-start.1 = (bf16[3,64,1024]{2,1,0:T(8,128)(2,1)}, bf16[3,64,1024]{2,1,0:T(8,128)(2,1)S(1)}, u32[]{:S(2)}, u32[]{:S(2)}) collective-permute-start(bf16[3,64,1024]{2,1,0:T(8,128)(2,1)} %get-tuple-element.80), channel_id=1, source_target_pairs={{0,31},{1,0},{2,1},{3,2},{4,3},{5,4},{6,5},{7,6},{8,7},{9,8},{10,9... | collective-permute-start | bytes 1179656 | tf_op jit(solution)/shard_map/ppermute | solution.py:60
  5.0 23.7 %collective-permute-start.2 = (bf16[3,64,1024]{2,1,0:T(8,128)(2,1)}, bf16[3,64,1024]{2,1,0:T(8,128)(2,1)S(1)}, u32[]{:S(2)}, u32[]{:S(2)}) collective-permute-start(bf16[3,64,1024]{2,1,0:T(8,128)(2,1)} %get-tuple-element.81), channel_id=1, source_target_pairs={{0,255},{1,224},{2,225},{3,226},{4,227},{5,228},{6,229},{7,230},{8... | collective-permute-start | bytes 1179656 | tf_op jit(solution)/shard_map/ppermute | solution.py:60
  13.6 6.5 %copy-start.16 = (bf16[64,2048]{1,0:T(8,128)(2,1)S(1)}, bf16[64,2048]{1,0:T(8,128)(2,1)}, u32[]{:S(2)}) copy-start(bf16[64,2048]{1,0:T(8,128)(2,1)} %get-tuple-element.92) | copy-start | bytes 786436
  13.6 6.7 %copy-start.15 = (bf16[64,2048]{1,0:T(8,128)(2,1)S(1)}, bf16[64,2048]{1,0:T(8,128)(2,1)}, u32[]{:S(2)}) copy-start(bf16[64,2048]{1,0:T(8,128)(2,1)} %get-tuple-element.93) | copy-start | bytes 786436
  13.6 15.1 %copy-start.17 = (f32[32]{0:T(128)S(1)}, f32[32]{0:T(128)}, u32[]{:S(2)}) copy-start(f32[32]{0:T(128)} %param.13) | copy-start | bytes 388
  13.6 15.2 %copy-start.14 = (bf16[64,2048]{1,0:T(8,128)(2,1)S(1)}, bf16[64,2048]{1,0:T(8,128)(2,1)}, u32[]{:S(2)}) copy-start(bf16[64,2048]{1,0:T(8,128)(2,1)} %get-tuple-element.94) | copy-start | bytes 786436
  13.6 15.7 %copy-start = (bf16[3,64,1024]{2,1,0:T(8,128)(2,1)S(1)}, bf16[3,64,1024]{2,1,0:T(8,128)(2,1)}, u32[]{:S(2)}) copy-start(bf16[3,64,1024]{2,1,0:T(8,128)(2,1)} %get-tuple-element.83.tl_ref) | copy-start | bytes 1179652
  20.1 18.8 %collective-permute-start.3 = (bf16[64,2048]{1,0:T(8,128)(2,1)S(1)}, bf16[64,2048]{1,0:T(8,128)(2,1)S(1)}, u32[]{:S(2)}, u32[]{:S(2)}) collective-permute-start(bf16[64,2048]{1,0:T(8,128)(2,1)S(1)} %copy-done.16), channel_id=1, source_target_pairs={{0,224},{1,225},{2,226},{3,227},{4,228},{5,229},{6,230},{7,231},{8... | collective-permute-start | bytes 786440 | tf_op jit(solution)/shard_map/ppermute | solution.py:60
  20.2 18.7 %collective-permute-start.4 = (bf16[64,2048]{1,0:T(8,128)(2,1)S(1)}, bf16[64,2048]{1,0:T(8,128)(2,1)}, u32[]{:S(2)}, u32[]{:S(2)}) collective-permute-start(bf16[64,2048]{1,0:T(8,128)(2,1)S(1)} %copy-done.15), channel_id=1, source_target_pairs={{0,31},{1,0},{2,1},{3,2},{4,3},{5,4},{6,5},{7,6},{8,7},{9,8},{10,9... | collective-permute-start | bytes 786440 | tf_op jit(solution)/shard_map/ppermute | solution.py:60
  28.7 14.0 %copy-start.2 = (bf16[3,64,1024]{2,1,0:T(8,128)(2,1)}, bf16[3,64,1024]{2,1,0:T(8,128)(2,1)S(1)}, u32[]{:S(2)}) copy-start(bf16[3,64,1024]{2,1,0:T(8,128)(2,1)S(1)} %collective-permute-done.bl_ref) | copy-start | bytes 1179652
  28.7 10.2 %copy-start.4 = (bf16[3,64,1024]{2,1,0:T(8,128)(2,1)}, bf16[3,64,1024]{2,1,0:T(8,128)(2,1)S(1)}, u32[]{:S(2)}) copy-start(bf16[3,64,1024]{2,1,0:T(8,128)(2,1)S(1)} %collective-permute-done.1.tr_ref) | copy-start | bytes 1179652
  28.7 10.2 %copy-start.6 = (bf16[3,64,1024]{2,1,0:T(8,128)(2,1)}, bf16[3,64,1024]{2,1,0:T(8,128)(2,1)S(1)}, u32[]{:S(2)}) copy-start(bf16[3,64,1024]{2,1,0:T(8,128)(2,1)S(1)} %collective-permute-done.2.br_ref) | copy-start | bytes 1179652
  28.7 10.2 %collective-permute-start.5 = (bf16[64,2048]{1,0:T(8,128)(2,1)S(1)}, bf16[64,2048]{1,0:T(8,128)(2,1)S(1)}, u32[]{:S(2)}, u32[]{:S(2)}) collective-permute-start(bf16[64,2048]{1,0:T(8,128)(2,1)S(1)} %copy-done.14), channel_id=1, source_target_pairs={{0,255},{1,224},{2,225},{3,226},{4,227},{5,228},{6,229},{7,230},{8... | collective-permute-start | bytes 786440 | tf_op jit(solution)/shard_map/ppermute | solution.py:60
  29.3 10.7 %copy-start.12 = (bf16[64,2048]{1,0:T(8,128)(2,1)S(1)}, bf16[64,2048]{1,0:T(8,128)(2,1)}, u32[]{:S(2)}) copy-start(bf16[64,2048]{1,0:T(8,128)(2,1)} %get-tuple-element.95) | copy-start | bytes 786436
  29.3 12.1 %copy-start.13 = (bf16[1024,2048]{1,0:T(8,128)(2,1)S(1)}, bf16[1024,2048]{1,0:T(8,128)(2,1)}, u32[]{:S(2)}) copy-start(bf16[1024,2048]{1,0:T(8,128)(2,1)} %param.15) | copy-start | bytes 12582916
  38.9 8.8 %collective-permute-start.6 = (bf16[1024,256]{1,0:T(8,128)(2,1)S(1)}, bf16[1024,256]{1,0:T(8,128)(2,1)S(1)}, u32[]{:S(2)}, u32[]{:S(2)}) collective-permute-start(bf16[1024,256]{1,0:T(8,128)(2,1)S(1)} %get-tuple-element.100.own_ref), channel_id=1, source_target_pairs={{0,1},{1,0},{2,3},{3,2},{4,5},{5,4},{6,7},{7,6},{8,9},{9,8},{10,11... | collective-permute-start | bytes 1572872 | tf_op jit(solution)/shard_map/ppermute | solution.py:50
  40.0 2.7 %copy-start.5 = (bf16[3,64,1024]{2,1,0:T(8,128)(2,1)S(1)}, bf16[3,64,1024]{2,1,0:T(8,128)(2,1)}, u32[]{:S(2)}) copy-start(bf16[3,64,1024]{2,1,0:T(8,128)(2,1)} %copy-done.4) | copy-start | bytes 1179652
  40.0 2.7 %copy-start.7 = (bf16[3,64,1024]{2,1,0:T(8,128)(2,1)S(1)}, bf16[3,64,1024]{2,1,0:T(8,128)(2,1)}, u32[]{:S(2)}) copy-start(bf16[3,64,1024]{2,1,0:T(8,128)(2,1)} %copy-done.6) | copy-start | bytes 1179652
  41.1 6.6 %collective-permute-start.7 = (bf16[256,2048]{1,0:T(8,128)(2,1)S(1)}, bf16[256,2048]{1,0:T(8,128)(2,1)S(1)}, u32[]{:S(2)}, u32[]{:S(2)}) collective-permute-start(bf16[256,2048]{1,0:T(8,128)(2,1)S(1)} %constant_dynamic-update-slice_fusion.drop_ref), channel_id=1, source_target_pairs={{0,1},{1,0},{2,3},{3,2},{4,5},{5,4},{6,7},{7,6},{8,9},{9,8},{10,11... | collective-permute-start | bytes 3145736 | tf_op jit(solution)/shard_map/ppermute | solution.py:50
  42.7 16.3 %copy-start.1 = (bf16[3,64,1024]{2,1,0:T(8,128)(2,1)S(1)}, bf16[3,64,1024]{2,1,0:T(8,128)(2,1)}, u32[]{:S(2)}) copy-start(bf16[3,64,1024]{2,1,0:T(8,128)(2,1)} %get-tuple-element.83.tl_ref) | copy-start | bytes 1179652
  50.4 20.0 %collective-permute-start.11 = (bf16[128,2048]{1,0:T(8,128)(2,1)S(1)}, bf16[128,2048]{1,0:T(8,128)(2,1)S(1)}, u32[]{:S(2)}, u32[]{:S(2)}) collective-permute-start(bf16[128,2048]{1,0:T(8,128)(2,1)S(1)} %get-tuple-element.126), channel_id=1, source_target_pairs={{0,64},{1,65},{2,66},{3,67},{4,68},{5,69},{6,70},{7,71},{8,72},{9,... | collective-permute-start | bytes 1572872 | tf_op jit(solution)/shard_map/ppermute | solution.py:50
  51.6 28.5 %collective-permute-start.12 = (bf16[128,2048]{1,0:T(8,128)(2,1)S(1)}, bf16[128,2048]{1,0:T(8,128)(2,1)S(1)}, u32[]{:S(2)}, u32[]{:S(2)}) collective-permute-start(bf16[128,2048]{1,0:T(8,128)(2,1)S(1)} %get-tuple-element.127), channel_id=1, source_target_pairs={{0,192},{1,193},{2,194},{3,195},{4,196},{5,197},{6,198},{7,199},{8... | collective-permute-start | bytes 1572872 | tf_op jit(solution)/shard_map/ppermute | solution.py:50
  57.5 29.1 %collective-permute-start.13 = (bf16[128,2048]{1,0:T(8,128)(2,1)}, bf16[128,2048]{1,0:T(8,128)(2,1)S(1)}, u32[]{:S(2)}, u32[]{:S(2)}) collective-permute-start(bf16[128,2048]{1,0:T(8,128)(2,1)} %get-tuple-element.130), channel_id=1, source_target_pairs={{0,128},{1,129},{2,130},{3,131},{4,132},{5,133},{6,134},{7,135},{8... | collective-permute-start | bytes 1572872 | tf_op jit(solution)/shard_map/ppermute | solution.py:50
  59.0 1.0 copy-start.3
  70.3 9.8 %copy-start.8 = (bf16[3,64,1024]{2,1,0:T(8,128)(2,1)}, bf16[3,64,1024]{2,1,0:T(8,128)(2,1)S(1)}, u32[]{:S(2)}) copy-start(bf16[3,64,1024]{2,1,0:T(8,128)(2,1)S(1)} %get-tuple-element.123) | copy-start | bytes 1179652
  70.3 9.8 %copy-start.9 = (bf16[3,64,1024]{2,1,0:T(8,128)(2,1)}, bf16[3,64,1024]{2,1,0:T(8,128)(2,1)S(1)}, u32[]{:S(2)}) copy-start(bf16[3,64,1024]{2,1,0:T(8,128)(2,1)S(1)} %get-tuple-element.124) | copy-start | bytes 1179652
  70.4 9.8 %copy-start.10 = (bf16[3,64,1024]{2,1,0:T(8,128)(2,1)}, bf16[3,64,1024]{2,1,0:T(8,128)(2,1)S(1)}, u32[]{:S(2)}) copy-start(bf16[3,64,1024]{2,1,0:T(8,128)(2,1)S(1)} %get-tuple-element.122) | copy-start | bytes 1179652
  80.2 11.6 %all-to-all-start = ((bf16[8,32,128]{2,1,0:T(8,128)(2,1)}), bf16[8,32,128]{2,1,0:T(8,128)(2,1)}, u32[]{:S(2)}, u32[]{:S(2)}) async-start(bf16[8,32,128]{2,1,0:T(8,128)(2,1)} %get-tuple-element.136), calls=%async_computation | async-start | bytes 131072 | tf_op jit(solution)/shard_map/all_to_all | solution.py:541
  87.4 0.7 copy-start.11
  92.6 8.0 %collective-permute-start.14 = (bf16[32,2048]{1,0:T(8,128)(2,1)}, bf16[32,2048]{1,0:T(8,128)(2,1)S(1)}, u32[]{:S(2)}, u32[]{:S(2)}) collective-permute-start(bf16[32,2048]{1,0:T(8,128)(2,1)} %copy-done.11), channel_id=1, source_target_pairs={{0,32},{1,33},{2,34},{3,35},{4,36},{5,37},{6,38},{7,39},{8,40},{9,... | collective-permute-start | bytes 393224 | tf_op jit(solution)/shard_map/ppermute | solution.py:50
  96.1 6.6 %collective-permute-start.15 = (bf16[32,2048]{1,0:T(8,128)(2,1)S(1)}, bf16[32,2048]{1,0:T(8,128)(2,1)S(1)}, u32[]{:S(2)}, u32[]{:S(2)}) collective-permute-start(bf16[32,2048]{1,0:T(8,128)(2,1)S(1)} %get-tuple-element.147), channel_id=1, source_target_pairs={{0,2},{1,3},{2,0},{3,1},{4,6},{5,7},{6,4},{7,5},{8,10},{9,11},{10,... | collective-permute-start | bytes 393224 | tf_op jit(solution)/shard_map/ppermute | solution.py:50
  96.4 7.5 %collective-permute-start.16 = (bf16[32,2048]{1,0:T(8,128)(2,1)S(1)}, bf16[32,2048]{1,0:T(8,128)(2,1)S(1)}, u32[]{:S(2)}, u32[]{:S(2)}) collective-permute-start(bf16[32,2048]{1,0:T(8,128)(2,1)S(1)} %get-tuple-element.148), channel_id=1, source_target_pairs={{0,34},{1,35},{2,32},{3,33},{4,38},{5,39},{6,36},{7,37},{8,42},{9,... | collective-permute-start | bytes 393224 | tf_op jit(solution)/shard_map/ppermute | solution.py:50
  125.1 17.3 %all-to-all-start.1 = ((bf16[32,32,128]{2,1,0:T(8,128)(2,1)}), bf16[32,32,128]{2,1,0:T(8,128)(2,1)S(1)}, u32[]{:S(2)}, u32[]{:S(2)}) async-start(bf16[32,32,128]{2,1,0:T(8,128)(2,1)} %broadcast_in_dim.6), calls=%async_computation.1 | async-start | bytes 524288 | tf_op jit(solution)/shard_map/all_to_all | solution.py:551
  130.1 17.0 %collective-permute-start.8 = (bf16[3,64,1024]{2,1,0:T(8,128)(2,1)}, bf16[3,64,1024]{2,1,0:T(8,128)(2,1)S(1)}, u32[]{:S(2)}, u32[]{:S(2)}) collective-permute-start(bf16[3,64,1024]{2,1,0:T(8,128)(2,1)} %copy-done.10), channel_id=1, source_target_pairs={{0,33},{1,34},{2,35},{3,36},{4,37},{5,38},{6,39},{7,40},{8,41},{9,... | collective-permute-start | bytes 1179656 | tf_op jit(solution)/shard_map/ppermute | solution.py:60
  130.1 23.1 %collective-permute-start.9 = (bf16[3,64,1024]{2,1,0:T(8,128)(2,1)}, bf16[3,64,1024]{2,1,0:T(8,128)(2,1)S(1)}, u32[]{:S(2)}, u32[]{:S(2)}) collective-permute-start(bf16[3,64,1024]{2,1,0:T(8,128)(2,1)} %copy-done.8), channel_id=1, source_target_pairs={{0,32},{1,33},{2,34},{3,35},{4,36},{5,37},{6,38},{7,39},{8,40},{9,... | collective-permute-start | bytes 1179656 | tf_op jit(solution)/shard_map/ppermute | solution.py:60
  131.9 21.6 %collective-permute-start.10 = (bf16[3,64,1024]{2,1,0:T(8,128)(2,1)}, bf16[3,64,1024]{2,1,0:T(8,128)(2,1)S(1)}, u32[]{:S(2)}, u32[]{:S(2)}) collective-permute-start(bf16[3,64,1024]{2,1,0:T(8,128)(2,1)} %copy-done.9), channel_id=1, source_target_pairs={{0,1},{1,2},{2,3},{3,4},{4,5},{5,6},{6,7},{7,8},{8,9},{9,10},{10,1... | collective-permute-start | bytes 1179656 | tf_op jit(solution)/shard_map/ppermute | solution.py:60
  154.2 12.0 %all-to-all-start.3 = ((f32[8,32,128]{2,1,0:T(8,128)}), f32[8,32,128]{2,1,0:T(8,128)S(1)}, u32[]{:S(2)}, u32[]{:S(2)}) async-start(f32[8,32,128]{2,1,0:T(8,128)} %broadcast_in_dim.7), calls=%async_computation.3 | async-start | bytes 262144 | tf_op jit(solution)/shard_map/all_to_all | solution.py:541

commit v2 on v1

--- a/solution.py
+++ b/solution.py
@@ -502,24 +502,27 @@
 
 
 def sum_z_kernel(*refs):
-    terms, out = refs[:4], refs[4]
+    terms, piece, out = refs[:4], refs[4], refs[5]
     total = terms[0][...]
     for term in terms[1:]:
         total = total + term[...].astype(F32)
     for z in range(NZ):
-        out[z] = total[4 * z : 4 * z + 4].astype(BF16)
-
-
-def sum_for_z(terms):
+        out[z, :, :D] = total[4 * z : 4 * z + 4].astype(BF16)
+        for part in range(8):
+            lanes = slice(D + TILE * part, D + TILE * part + TILE)
+            out[z, :, lanes] = piece[4 * part : 4 * part + 4].astype(BF16)
+
+
+def sum_for_z(terms, piece):
     whole = pl.BlockSpec(memory_space=pltpu.VMEM)
     return pl.pallas_call(
         sum_z_kernel,
-        in_specs=[whole] * 4,
+        in_specs=[whole] * 5,
         out_specs=whole,
-        out_shape=jax.ShapeDtypeStruct((NZ, 4, D), BF16),
+        out_shape=jax.ShapeDtypeStruct((NZ, 4, D + 8 * TILE), BF16),
         compiler_params=params(),
         name="sum_for_z",
-    )(*terms)
+    )(*terms, piece)
 
 
 def place_scalars():
@@ -527,54 +530,59 @@
     return jnp.stack([x, y, z, core]).astype(jnp.int32)
 
 
-def weight_total(terms):
-    terms = [terms[0]] + [move(terms[s], along_y(s)) for s in range(1, 4)]
+def along_z_exchange(value):
     rest = NYH * NCORE
     groups = [[rest * z + one for z in range(NZ)] for one in range(rest)]
+    return lax.all_to_all(value, "col", 0, 0, axis_index_groups=groups, tiled=True)
+
+
+def table_pieces(part):
+    return jnp.sum(along_z_exchange(part).astype(F32), axis=0)
+
+
+def table_plane(piece):
+    cols, rest = NZ * NYH * NCORE, NYH * NCORE
+    groups = [
+        [cols * row + rest * z + one for row in range(NX * NYL) for one in range(rest)]
+        for z in range(NZ)
+    ]
+    same = jnp.broadcast_to(piece.astype(BF16), (len(groups[0]), 32, TILE))
     found = lax.all_to_all(
-        sum_for_z(terms), "col", 0, 0, axis_index_groups=groups, tiled=True
+        same, ("row", "col"), 0, 0, axis_index_groups=groups, tiled=True
     )
-    return jnp.sum(found.astype(F32), axis=0)
-
-
-def row_exchange(value):
-    return lax.all_to_all(value, "row", 0, 0, tiled=True)
-
-
-def table_pieces(part):
-    return jnp.sum(row_exchange(part).astype(F32), axis=0)
-
-
-def table_column(piece):
-    cols = NZ * NYH * NCORE
-    same = jnp.broadcast_to(piece.astype(BF16), (cols, 32, TILE))
-    found = lax.all_to_all(same, "col", 0, 0, tiled=True)
     return jnp.sum(found.astype(F32), axis=0) / WINDOWS
 
 
-def table_whole(piece):
-    return row_exchange(jnp.broadcast_to(piece, (NX * NYL, 32, TILE)))
-
-
-def unpack_kernel(total_ref, table_ref):
+def totals_kernel(found_ref, weight_ref, table_ref):
+    total = found_ref[0, :, :D].astype(F32)
+    for z in range(1, NZ):
+        total = total + found_ref[z, :, :D].astype(F32)
+    weight_ref[...] = total * (1.0 / WINDOWS)
     for tile in range(INNER // TILE):
+        parts = [found_ref[tile, :, D + TILE * p : D + TILE * p + TILE] for p in range(8)]
+        rows = jnp.concatenate([part.astype(F32) for part in parts], axis=0)
         for head in range(PER_TILE):
-            rows = total_ref[32 * tile : 32 * tile + 32, 32 * head : 32 * head + 32]
-            table_ref[PER_TILE * tile + head] = rows[:SIDE, :SIDE]
-
-
-def unpack_table(total):
+            place = rows[:, 32 * head : 32 * head + 32]
+            table_ref[PER_TILE * tile + head] = place[:SIDE, :SIDE]
+
+
+def totals(terms, piece):
+    terms = [terms[0]] + [move(terms[s], along_y(s)) for s in range(1, 4)]
+    found = along_z_exchange(sum_for_z(terms, piece))
     whole = pl.BlockSpec(memory_space=pltpu.VMEM)
-    total = total.reshape(WINDOWS, TILE)
-    table = pl.pallas_call(
-        unpack_kernel,
+    weight, table = pl.pallas_call(
+        totals_kernel,
         in_specs=[whole],
-        out_specs=whole,
-        out_shape=jax.ShapeDtypeStruct((HEADS, SIDE, SIDE), F32),
-        compiler_params=params(),
-        name="unpack_table",
-    )(total)
-    return table, total[31::32, ::32].reshape(HEADS)
+        out_specs=[whole] * 2,
+        out_shape=[
+            jax.ShapeDtypeStruct((4, D), F32),
+            jax.ShapeDtypeStruct((HEADS, SIDE, SIDE), F32),
+        ],
+        compiler_params=params(),
+        name="totals",
+    )(found)
+    log_sum = found[:, 3, D + 7 * TILE :: 32].astype(F32)
+    return weight, table, log_sum.reshape(HEADS)
 
 
 def per_device(
@@ -604,19 +612,18 @@
     g_tl, g_bl, g_tr, g_br, table_part = backward(
         logit_scale, quads, grad_attn, probs, EARLY, INNER // TILE // GROUP - EARLY, found
     )
-    arrived = (move_map(g_br, 1, 1), move_map(g_bl, 1, 0), move_map(g_tr, 0, 1))
     near = [move(terms[s], along_x(s)) for s in (1, 3)]
     across = move(terms[2], along_x(2))
-    near, table_part = lax.optimization_barrier((near, table_part))
-    piece = table_pieces(table_part)
+    near, g_tl, g_bl, g_tr, g_br, table_part = lax.optimization_barrier(
+        (near, g_tl, g_bl, g_tr, g_br, table_part)
+    )
+    arrived = (move_map(g_br, 1, 1), move_map(g_bl, 1, 0), move_map(g_tr, 0, 1))
+    piece = table_plane(table_pieces(table_part))
+    across, arrived = lax.optimization_barrier((across, arrived))
     terms = sum_for_y(place, (terms[0], near[0], across, near[1]))
-    terms, piece = lax.optimization_barrier((terms, piece))
-    piece = table_column(piece)
-    arrived, piece = lax.optimization_barrier((arrived, piece))
     grads = join_maps(*arrived, g_tl)
-    table_grad, log_grad = unpack_table(table_whole(piece))
-    weight_grad = weight_total(terms)
-    return (*grads, weight_grad / WINDOWS, table_grad, log_grad)
+    weight_grad, table_grad, log_grad = totals(terms, piece)
+    return (*grads, weight_grad, table_grad, log_grad)
 
 
 def solution(mesh):

time: 169 us -> 153 us (0.905); the launches traced: 168 us -> 150 us
  waiting for transfers between devices: 44.1 us -> 28.4 us
  Pallas kernels: 44.4 us -> 47.1 us
  blocking collectives: 20.3 us -> 17.7 us
    ppermute x9, waiting for transfers between devices: 11 us -> 0.02 us  [move_map(): return lax.ppermute(value, ('row', 'col'), pairs)]
    all_to_all x3 -> x2, waiting for transfers between devices: 17.1 us -> 9.74 us  [along_z_exchange(): lax.all_to_all(value, 'col', 0, 0, axis_index_groups=groups, tiled=True)]
    ppermute x9, starting transfers between devices: 15 us -> 18.1 us  [move_map(): return lax.ppermute(value, ('row', 'col'), pairs)]
    all_to_all x1, blocking collectives: 20.3 us -> 17.7 us  [table_plane(): lax.all_to_all(same, ('row', 'col'), 0, 0, axis_index_groups=groups, tile...]
    ppermute x8, waiting for transfers between devices: 16 us -> 18.6 us  [move(): return lax.ppermute(value, ('row', 'col'), pairs)]
    ppermute x8, starting transfers between devices: 15.1 us -> 13.1 us  [move(): return lax.ppermute(value, ('row', 'col'), pairs)]
    all_to_all x3 -> x2, starting transfers between devices: 17.9 us -> 17.5 us  [along_z_exchange(): lax.all_to_all(value, 'col', 0, 0, axis_index_groups=groups, tiled=True)]
    unnamed x41 -> x39, local copies, waits for them, and re-layouts: 5.21 us -> 5.27 us
  transfers between devices with their start and end apart: 20 -> 19, of which waited for: 10 -> 7; matrix products, arithmetic and copies ran while one was open for 3% -> 2% of each run, Pallas kernels for 23% -> 26%
where the time goes in v2:
time: 153 us; the launch traced here: 150 us
  starting transfers between devices  48.7 us (32%)
  Pallas kernels  47.1 us (31%)
  waiting for transfers between devices  28.4 us (19%)
  blocking collectives  17.7 us (12%)
  local copies, waits for them, and re-layouts  6.02 us (4%)
    ppermute x8, waiting for transfers between devices, move(): return lax.ppermute(value, ('row', 'col'), pairs)  18.6 us
    ppermute x9, starting transfers between devices, move_map(): return lax.ppermute(value, ('row', 'col'), pairs)  18.1 us
    all_to_all x1, blocking collectives, table_plane(): lax.all_to_all(same, ('row', 'col'), 0, 0, axis_index_groups=groups, tile...  17.7 us
    all_to_all x2, starting transfers between devices, along_z_exchange(): lax.all_to_all(value, 'col', 0, 0, axis_index_groups=groups, tiled=True)  17.5 us
    pallas_call x2, Pallas kernels, backward(): pl.pallas_call(functools.partial(backward_kernel, first), grid=(steps,),...  15.3 us
    ppermute x8, starting transfers between devices, move(): return lax.ppermute(value, ('row', 'col'), pairs)  13.1 us
    all_to_all x2, waiting for transfers between devices, along_z_exchange(): lax.all_to_all(value, 'col', 0, 0, axis_index_groups=groups, tiled=True)  9.74 us
    pallas_call x1, Pallas kernels, forward(): pl.pallas_call(forward_kernel, grid=(INNER // TILE // GROUP,), in_specs=[...  9.57 us
  transfers between devices with their start and end apart: 19, of which 7 were waited for; matrix products, arithmetic and copies ran while one was open for 2% of the time, Pallas kernels for 26%

profile of v2, /device:TPU:24, one launch (start us, length us, event | category | flops | bytes accessed | tf_op | source)
XLA Modules:
  0.0 150.2 jit_solution(7734470173217158652)
XLA Ops:
  0.6 3.6 %split_maps.1 = (bf16[3,64,1024]{2,1,0:T(8,128)(2,1)}, bf16[3,64,1024]{2,1,0:T(8,128)(2,1)}, bf16[3,64,1024]{2,1,0:T(8,128)(2,1)}, bf16[3,64,1024]{2,1,0:T(8,128)(2,1)}) custom-call(bf16[16,16,1024]{2,1,0:T(8,128)(2,1)} %q_ref.1, bf16[16,16,1024]{2,1,0:T(8,128)(2,1)} %k_ref.1, bf16[16,16,1024]{2,1,0:T(8,128)(2,1)} %v_ref.1), custom_call_target="tpu_custom_call" | custom-call | tf_op jit(solution)/shard_map/split_maps/pallas_call | solution.py:106
  4.3 0.8 collective-permute-start
  5.0 0.0 collective-permute-start.1
  5.0 3.3 %collective-permute-start.2 = (bf16[3,64,1024]{2,1,0:T(8,128)(2,1)}, bf16[3,64,1024]{2,1,0:T(8,128)(2,1)S(1)}, u32[]{:S(2)}, u32[]{:S(2)}) collective-permute-start(bf16[3,64,1024]{2,1,0:T(8,128)(2,1)} %get-tuple-element.82), channel_id=1, source_target_pairs={{0,255},{1,224},{2,225},{3,226},{4,227},{5,228},{6,229},{7,230},{8... | collective-permute-start | bytes 1179656 | tf_op jit(solution)/shard_map/ppermute | solution.py:60
  8.4 1.3 copy.23.table_ref
  9.7 3.8 %split_dropped.1 = (bf16[64,2048]{1,0:T(8,128)(2,1)}, bf16[64,2048]{1,0:T(8,128)(2,1)}, bf16[64,2048]{1,0:T(8,128)(2,1)}, bf16[64,2048]{1,0:T(8,128)(2,1)}) custom-call(bf16[16,16,2048]{2,1,0:T(8,128)(2,1)} %grad_ref.1, s32[16,16,2048]{2,1,0:T(8,128)} %keep_ref.1), custom_call_target="tpu_custom_call" | custom-call | tf_op jit(solution)/shard_map/split_dropped/pallas_call | solution.py:126
  13.6 0.0 copy-start.2
  13.6 6.5 %bias_blocks.1.bias_ref = f32[32,3,128,128]{3,2,1,0:T(8,128)} custom-call(f32[32,31,31]{2,1,0:T(8,128)S(1)} %copy.23.table_ref), custom_call_target="tpu_custom_call" | custom-call | flops 10000000 | bytes 8000000 | tf_op jit(solution)/shard_map/bias_blocks/pallas_call | solution.py:180
  20.0 0.1 collective-permute-start.3
  20.2 8.3 %collective-permute-start.4 = (bf16[64,2048]{1,0:T(8,128)(2,1)}, bf16[64,2048]{1,0:T(8,128)(2,1)S(1)}, u32[]{:S(2)}, u32[]{:S(2)}) collective-permute-start(bf16[64,2048]{1,0:T(8,128)(2,1)} %get-tuple-element.94), channel_id=1, source_target_pairs={{0,31},{1,0},{2,1},{3,2},{4,3},{5,4},{6,5},{7,6},{8,7},{9,8},{10,9... | collective-permute-start | bytes 786440 | tf_op jit(solution)/shard_map/ppermute | solution.py:60
  28.4 0.1 pad_add_fusion.place_ref
  28.6 0.0 copy-start.6
  28.6 0.6 collective-permute-start.5
  29.3 9.6 %forward.1 = (bf16[1024,256]{1,0:T(8,128)(2,1)S(1)}, f32[32,256,256]{2,1,0:T(8,128)}) custom-call(f32[32]{0:T(128)S(1)} %get-tuple-element.171.scale_ref, bf16[3,64,1024]{2,1,0:T(8,128)(2,1)S(1)} %copy-done.2, bf16[3,64,1024]{2,1,0:T(8,128)(2,1)S(1)} %collective-permute-done.bl_ref, bf16[3,64,1024]{2,1,0:T(8,128)(2,1)S(1)} %collective-permute-done.1.tr_ref, ...), custom_call_target="tpu_custom_call" | custom-call | flops 8000000000 | bytes 16000000 | tf_op jit(solution)/shard_map/forward/pallas_call | solution.py:277
  38.9 1.1 collective-permute-start.6
  40.0 0.0 copy-start.9
  40.0 0.3 collective-permute-start.7
  40.3 1.3 convolution_convert_fusion.grad_ref
  41.7 5.0 %backward.2 = (bf16[3,64,1024]{2,1,0:T(8,128)(2,1)S(1)}, bf16[3,64,1024]{2,1,0:T(8,128)(2,1)S(1)}, bf16[3,64,1024]{2,1,0:T(8,128)(2,1)S(1)}, bf16[3,64,1024]{2,1,0:T(8,128)(2,1)S(1)}, bf16[8,32,128]{2,1,0:T(8,128)(2,1)}) custom-call(f32[32]{0:T(128)S(1)} %get-tuple-element.170.scale_ref, bf16[3,64,1024]{2,1,0:T(8,128)(2,1)S(1)} %copy-done.2, ...), custom_call_target="tpu_custom_call" | custom-call | flops 8000000000 | bytes 10000000 | tf_op jit(solution)/shard_map/backward/pallas_call | solution.py:428
  46.6 2.7 %outer_terms.1 = (f32[128,2048]{1,0:T(8,128)S(1)}, bf16[128,2048]{1,0:T(8,128)(2,1)S(1)}, bf16[128,2048]{1,0:T(8,128)(2,1)}, bf16[128,2048]{1,0:T(8,128)(2,1)S(1)}) custom-call(s32[4]{0:T(128)S(1)} %pad_add_fusion.place_ref, bf16[1024,256]{1,0:T(8,128)(2,1)S(1)} %get-tuple-element.96.own_ref, bf16[1024,256]{1,0:T(8,128)(2,1)S(1)} %collective-permute-done.6.other_ref, ...), custom_call_target="tpu_custom_call" | custom-call | flops 1100000000 | bytes 6000000 | tf_op jit(solution)/shard_map/outer_terms/pallas_call | solution.py:468
  49.4 1.3 collective-permute-start.8
  50.6 6.8 %collective-permute-start.9 = (bf16[128,2048]{1,0:T(8,128)(2,1)S(1)}, bf16[128,2048]{1,0:T(8,128)(2,1)S(1)}, u32[]{:S(2)}, u32[]{:S(2)}) collective-permute-start(bf16[128,2048]{1,0:T(8,128)(2,1)S(1)} %get-tuple-element.119), channel_id=1, source_target_pairs={{0,64},{1,65},{2,66},{3,67},{4,68},{5,69},{6,70},{7,71},{8,72},{9,... | collective-permute-start | bytes 1572872 | tf_op jit(solution)/shard_map/ppermute | solution.py:50
  57.4 1.0 copy-done.5
  58.4 10.4 %backward.3 = (bf16[3,64,1024]{2,1,0:T(8,128)(2,1)S(1)}, bf16[3,64,1024]{2,1,0:T(8,128)(2,1)S(1)}, bf16[3,64,1024]{2,1,0:T(8,128)(2,1)S(1)}, bf16[3,64,1024]{2,1,0:T(8,128)(2,1)S(1)}, bf16[8,32,128]{2,1,0:T(8,128)(2,1)}) custom-call(f32[32]{0:T(128)S(1)} %get-tuple-element.170.scale_ref, ...), custom_call_target="tpu_custom_call", output_to_operand_aliasing={{0}: (7, {}), {1}: (8, {}), {2}: (9, {}), {3}: (10, {}), {4... | custom-call | flops 8000000000 | bytes 10000000 | tf_op jit(solution)/shard_map/backward/pallas_call | solution.py:428
  68.7 0.7 copy-done
  69.5 7.1 %collective-permute-done.9.refs_1_ = bf16[128,2048]{1,0:T(8,128)(2,1)S(1)} collective-permute-done((bf16[128,2048]{1,0:T(8,128)(2,1)S(1)}, bf16[128,2048]{1,0:T(8,128)(2,1)S(1)}, u32[]{:S(2)}, u32[]{:S(2)}) %collective-permute-start.9) | collective-permute-done | bytes 524320 | tf_op jit(solution)/shard_map/ppermute | solution.py:50
  76.6 4.1 %collective-permute-done.10.refs_3_ = bf16[128,2048]{1,0:T(8,128)(2,1)S(1)} collective-permute-done((bf16[128,2048]{1,0:T(8,128)(2,1)S(1)}, bf16[128,2048]{1,0:T(8,128)(2,1)S(1)}, u32[]{:S(2)}, u32[]{:S(2)}) %collective-permute-start.10) | collective-permute-done | bytes 524320 | tf_op jit(solution)/shard_map/ppermute | solution.py:50
  80.7 9.9 %all-to-all-start = ((bf16[8,32,128]{2,1,0:T(8,128)(2,1)}), bf16[8,32,128]{2,1,0:T(8,128)(2,1)S(1)}, u32[]{:S(2)}, u32[]{:S(2)}) async-start(bf16[8,32,128]{2,1,0:T(8,128)(2,1)} %get-tuple-element.149), calls=%async_computation | async-start | bytes 131072 | tf_op jit(solution)/shard_map/all_to_all | solution.py:536
  90.6 1.0 collective-permute-start.12
  91.6 3.9 %collective-permute-start.13 = (bf16[3,64,1024]{2,1,0:T(8,128)(2,1)}, bf16[3,64,1024]{2,1,0:T(8,128)(2,1)}, u32[]{:S(2)}, u32[]{:S(2)}) collective-permute-start(bf16[3,64,1024]{2,1,0:T(8,128)(2,1)} %copy-done.11), channel_id=1, source_target_pairs={{0,1},{1,2},{2,3},{3,4},{4,5},{5,6},{6,7},{7,8},{8,9},{9,10},{10,1... | collective-permute-start | bytes 1179656 | tf_op jit(solution)/shard_map/ppermute | solution.py:60
  95.5 3.5 %all-to-all-done = bf16[8,32,128]{2,1,0:T(8,128)(2,1)S(1)} async-done(((bf16[8,32,128]{2,1,0:T(8,128)(2,1)}), bf16[8,32,128]{2,1,0:T(8,128)(2,1)S(1)}, u32[]{:S(2)}, u32[]{:S(2)}) %all-to-all-start) | async-done | bytes 65568 | tf_op jit(solution)/shard_map/all_to_all | solution.py:536
  99.1 17.7 %all_to_all.15 = bf16[32,32,128]{2,1,0:T(8,128)(2,1)S(1)} all-to-all(bf16[32,32,128]{2,1,0:T(8,128)(2,1)S(1)} %broadcast_in_dim.3), channel_id=1, replica_groups={{0,1,2,3,32,33,34,35,64,65,66,67,96,97,98,99,128,129,130,131,160,161,16..., dimensions={0} | all-to-all | bytes 524288 | tf_op jit(solution)/shard_map/all_to_all | solution.py:550
  116.9 0.8 sum_for_y.1
  117.7 1.2 collective-permute-start.14
  118.9 1.1 collective-permute-start.15
  120.1 1.3 collective-permute-start.16
  121.4 2.7 %collective-permute-done.14.refs_1_ = bf16[32,2048]{1,0:T(8,128)(2,1)S(1)} collective-permute-done((bf16[32,2048]{1,0:T(8,128)(2,1)S(1)}, bf16[32,2048]{1,0:T(8,128)(2,1)S(1)}, u32[]{:S(2)}, u32[]{:S(2)}) %collective-permute-start.14) | collective-permute-done | bytes 131104 | tf_op jit(solution)/shard_map/ppermute | solution.py:50
  124.1 2.7 %collective-permute-done.15.refs_2_ = bf16[32,2048]{1,0:T(8,128)(2,1)S(1)} collective-permute-done((bf16[32,2048]{1,0:T(8,128)(2,1)S(1)}, bf16[32,2048]{1,0:T(8,128)(2,1)S(1)}, u32[]{:S(2)}, u32[]{:S(2)}) %collective-permute-start.15) | collective-permute-done | bytes 131104 | tf_op jit(solution)/shard_map/ppermute | solution.py:50
  126.8 2.0 %collective-permute-done.16.refs_3_ = bf16[32,2048]{1,0:T(8,128)(2,1)S(1)} collective-permute-done((bf16[32,2048]{1,0:T(8,128)(2,1)S(1)}, bf16[32,2048]{1,0:T(8,128)(2,1)S(1)}, u32[]{:S(2)}, u32[]{:S(2)}) %collective-permute-start.16) | collective-permute-done | bytes 131104 | tf_op jit(solution)/shard_map/ppermute | solution.py:50
  128.8 0.8 sum_for_z.1
  129.5 7.6 %all-to-all-start.2 = ((bf16[8,4,3072]{2,1,0:T(4,128)(2,1)}), bf16[8,4,3072]{2,1,0:T(4,128)(2,1)S(1)}, u32[]{:S(2)}, u32[]{:S(2)}) async-start(bf16[8,4,3072]{2,1,0:T(4,128)(2,1)} %sum_for_z.1), calls=%async_computation.2 | async-start | bytes 393216 | tf_op jit(solution)/shard_map/all_to_all | solution.py:536
  137.2 1.0 copy-done.1
  138.1 3.4 %join_maps.1 = (bf16[16,16,1024]{2,1,0:T(8,128)(2,1)}, bf16[16,16,1024]{2,1,0:T(8,128)(2,1)}, bf16[16,16,1024]{2,1,0:T(8,128)(2,1)}) custom-call(bf16[3,64,1024]{2,1,0:T(8,128)(2,1)S(1)} %collective-permute-done.11.tl_ref, bf16[3,64,1024]{2,1,0:T(8,128)(2,1)S(1)} %collective-permute-done.12.tr_ref, bf16[3,64,1024]{2,1,0:T(8,128)(2,1)} %collective-permute-done.13.bl_ref, ...), custom_call_target="tpu_custom_call" | custom-call | tf_op jit(solution)/shard_map/join_maps/pallas_call | solution.py:147
  141.5 6.2 %all-to-all-done.2.found_ref = bf16[8,4,3072]{2,1,0:T(4,128)(2,1)S(1)} async-done(((bf16[8,4,3072]{2,1,0:T(4,128)(2,1)}), bf16[8,4,3072]{2,1,0:T(4,128)(2,1)S(1)}, u32[]{:S(2)}, u32[]{:S(2)}) %all-to-all-start.2) | async-done | bytes 196640 | tf_op jit(solution)/shard_map/all_to_all | solution.py:536
  147.7 0.1 slice.3
  147.9 0.6 reshape.16
  148.5 0.7 totals.1
  149.1 1.1 copy.24
  (52 shorter events, 0.3 us)
Async XLA Ops:
  4.3 24.3 %collective-permute-start = (bf16[3,64,1024]{2,1,0:T(8,128)(2,1)}, bf16[3,64,1024]{2,1,0:T(8,128)(2,1)S(1)}, u32[]{:S(2)}, u32[]{:S(2)}) collective-permute-start(bf16[3,64,1024]{2,1,0:T(8,128)(2,1)} %get-tuple-element.80), channel_id=1, source_target_pairs={{0,224},{1,225},{2,226},{3,227},{4,228},{5,229},{6,230},{7,231},{8... | collective-permute-start | bytes 1179656 | tf_op jit(solution)/shard_map/ppermute | solution.py:60
  5.0 23.5 %collective-permute-start.1 = (bf16[3,64,1024]{2,1,0:T(8,128)(2,1)}, bf16[3,64,1024]{2,1,0:T(8,128)(2,1)S(1)}, u32[]{:S(2)}, u32[]{:S(2)}) collective-permute-start(bf16[3,64,1024]{2,1,0:T(8,128)(2,1)} %get-tuple-element.81), channel_id=1, source_target_pairs={{0,31},{1,0},{2,1},{3,2},{4,3},{5,4},{6,5},{7,6},{8,7},{9,8},{10,9... | collective-permute-start | bytes 1179656 | tf_op jit(solution)/shard_map/ppermute | solution.py:60
  5.0 23.5 %collective-permute-start.2 = (bf16[3,64,1024]{2,1,0:T(8,128)(2,1)}, bf16[3,64,1024]{2,1,0:T(8,128)(2,1)S(1)}, u32[]{:S(2)}, u32[]{:S(2)}) collective-permute-start(bf16[3,64,1024]{2,1,0:T(8,128)(2,1)} %get-tuple-element.82), channel_id=1, source_target_pairs={{0,255},{1,224},{2,225},{3,226},{4,227},{5,228},{6,229},{7,230},{8... | collective-permute-start | bytes 1179656 | tf_op jit(solution)/shard_map/ppermute | solution.py:60
  13.5 15.0 %copy-start.16 = (f32[32]{0:T(128)S(1)}, f32[32]{0:T(128)}, u32[]{:S(2)}) copy-start(f32[32]{0:T(128)} %param.13) | copy-start | bytes 388
  13.5 15.1 %copy-start.15 = (bf16[64,2048]{1,0:T(8,128)(2,1)S(1)}, bf16[64,2048]{1,0:T(8,128)(2,1)}, u32[]{:S(2)}) copy-start(bf16[64,2048]{1,0:T(8,128)(2,1)} %get-tuple-element.95) | copy-start | bytes 786436
  13.6 15.7 %copy-start.2 = (bf16[3,64,1024]{2,1,0:T(8,128)(2,1)S(1)}, bf16[3,64,1024]{2,1,0:T(8,128)(2,1)}, u32[]{:S(2)}) copy-start(bf16[3,64,1024]{2,1,0:T(8,128)(2,1)} %get-tuple-element.84.tl_ref) | copy-start | bytes 1179652
  20.0 18.8 %collective-permute-start.3 = (bf16[64,2048]{1,0:T(8,128)(2,1)}, bf16[64,2048]{1,0:T(8,128)(2,1)S(1)}, u32[]{:S(2)}, u32[]{:S(2)}) collective-permute-start(bf16[64,2048]{1,0:T(8,128)(2,1)} %get-tuple-element.93), channel_id=1, source_target_pairs={{0,224},{1,225},{2,226},{3,227},{4,228},{5,229},{6,230},{7,231},{8... | collective-permute-start | bytes 786440 | tf_op jit(solution)/shard_map/ppermute | solution.py:60
  20.2 18.7 %collective-permute-start.4 = (bf16[64,2048]{1,0:T(8,128)(2,1)}, bf16[64,2048]{1,0:T(8,128)(2,1)S(1)}, u32[]{:S(2)}, u32[]{:S(2)}) collective-permute-start(bf16[64,2048]{1,0:T(8,128)(2,1)} %get-tuple-element.94), channel_id=1, source_target_pairs={{0,31},{1,0},{2,1},{3,2},{4,3},{5,4},{6,5},{7,6},{8,7},{9,8},{10,9... | collective-permute-start | bytes 786440 | tf_op jit(solution)/shard_map/ppermute | solution.py:60
  28.5 13.1 %copy-start.4 = (bf16[3,64,1024]{2,1,0:T(8,128)(2,1)}, bf16[3,64,1024]{2,1,0:T(8,128)(2,1)S(1)}, u32[]{:S(2)}) copy-start(bf16[3,64,1024]{2,1,0:T(8,128)(2,1)S(1)} %collective-permute-done.bl_ref) | copy-start | bytes 1179652
  28.6 10.3 %copy-start.6 = (bf16[3,64,1024]{2,1,0:T(8,128)(2,1)}, bf16[3,64,1024]{2,1,0:T(8,128)(2,1)S(1)}, u32[]{:S(2)}) copy-start(bf16[3,64,1024]{2,1,0:T(8,128)(2,1)S(1)} %collective-permute-done.1.tr_ref) | copy-start | bytes 1179652
  28.6 10.2 %copy-start.8 = (bf16[3,64,1024]{2,1,0:T(8,128)(2,1)}, bf16[3,64,1024]{2,1,0:T(8,128)(2,1)S(1)}, u32[]{:S(2)}) copy-start(bf16[3,64,1024]{2,1,0:T(8,128)(2,1)S(1)} %collective-permute-done.2.br_ref) | copy-start | bytes 1179652
  28.6 10.2 %collective-permute-start.5 = (bf16[64,2048]{1,0:T(8,128)(2,1)S(1)}, bf16[64,2048]{1,0:T(8,128)(2,1)S(1)}, u32[]{:S(2)}, u32[]{:S(2)}) collective-permute-start(bf16[64,2048]{1,0:T(8,128)(2,1)S(1)} %copy-done.15), channel_id=1, source_target_pairs={{0,255},{1,224},{2,225},{3,226},{4,227},{5,228},{6,229},{7,230},{8... | collective-permute-start | bytes 786440 | tf_op jit(solution)/shard_map/ppermute | solution.py:60
  29.3 10.7 %copy-start.13 = (bf16[64,2048]{1,0:T(8,128)(2,1)S(1)}, bf16[64,2048]{1,0:T(8,128)(2,1)}, u32[]{:S(2)}) copy-start(bf16[64,2048]{1,0:T(8,128)(2,1)} %get-tuple-element.97) | copy-start | bytes 786436
  29.3 11.1 %copy-start.14 = (bf16[1024,2048]{1,0:T(8,128)(2,1)S(1)}, bf16[1024,2048]{1,0:T(8,128)(2,1)}, u32[]{:S(2)}) copy-start(bf16[1024,2048]{1,0:T(8,128)(2,1)} %param.15) | copy-start | bytes 12582916
  38.9 7.8 %collective-permute-start.6 = (bf16[1024,256]{1,0:T(8,128)(2,1)S(1)}, bf16[1024,256]{1,0:T(8,128)(2,1)S(1)}, u32[]{:S(2)}, u32[]{:S(2)}) collective-permute-start(bf16[1024,256]{1,0:T(8,128)(2,1)S(1)} %get-tuple-element.96.own_ref), channel_id=1, source_target_pairs={{0,1},{1,0},{2,3},{3,2},{4,5},{5,4},{6,7},{7,6},{8,9},{9,8},{10,11... | collective-permute-start | bytes 1572872 | tf_op jit(solution)/shard_map/ppermute | solution.py:50
  40.0 1.7 %copy-start.7 = (bf16[3,64,1024]{2,1,0:T(8,128)(2,1)S(1)}, bf16[3,64,1024]{2,1,0:T(8,128)(2,1)}, u32[]{:S(2)}) copy-start(bf16[3,64,1024]{2,1,0:T(8,128)(2,1)} %copy-done.6) | copy-start | bytes 1179652
  40.0 1.7 %copy-start.9 = (bf16[3,64,1024]{2,1,0:T(8,128)(2,1)S(1)}, bf16[3,64,1024]{2,1,0:T(8,128)(2,1)}, u32[]{:S(2)}) copy-start(bf16[3,64,1024]{2,1,0:T(8,128)(2,1)} %copy-done.8) | copy-start | bytes 1179652
  40.0 6.6 %collective-permute-start.7 = (bf16[256,2048]{1,0:T(8,128)(2,1)S(1)}, bf16[256,2048]{1,0:T(8,128)(2,1)S(1)}, u32[]{:S(2)}, u32[]{:S(2)}) collective-permute-start(bf16[256,2048]{1,0:T(8,128)(2,1)S(1)} %constant_dynamic-update-slice_fusion.drop_ref), channel_id=1, source_target_pairs={{0,1},{1,0},{2,3},{3,2},{4,5},{5,4},{6,7},{7,6},{8,9},{9,8},{10,11... | collective-permute-start | bytes 3145736 | tf_op jit(solution)/shard_map/ppermute | solution.py:50
  41.7 15.7 %copy-start.3 = (bf16[3,64,1024]{2,1,0:T(8,128)(2,1)S(1)}, bf16[3,64,1024]{2,1,0:T(8,128)(2,1)}, u32[]{:S(2)}) copy-start(bf16[3,64,1024]{2,1,0:T(8,128)(2,1)} %get-tuple-element.84.tl_ref) | copy-start | bytes 1179652
  49.4 67.5 %collective-permute-start.8 = (bf16[128,2048]{1,0:T(8,128)(2,1)}, bf16[128,2048]{1,0:T(8,128)(2,1)S(1)}, u32[]{:S(2)}, u32[]{:S(2)}) collective-permute-start(bf16[128,2048]{1,0:T(8,128)(2,1)} %get-tuple-element.118), channel_id=1, source_target_pairs={{0,128},{1,129},{2,130},{3,131},{4,132},{5,133},{6,134},{7,135},{8... | collective-permute-start | bytes 1572872 | tf_op jit(solution)/shard_map/ppermute | solution.py:50
  50.6 26.0 %collective-permute-start.9 = (bf16[128,2048]{1,0:T(8,128)(2,1)S(1)}, bf16[128,2048]{1,0:T(8,128)(2,1)S(1)}, u32[]{:S(2)}, u32[]{:S(2)}) collective-permute-start(bf16[128,2048]{1,0:T(8,128)(2,1)S(1)} %get-tuple-element.119), channel_id=1, source_target_pairs={{0,64},{1,65},{2,66},{3,67},{4,68},{5,69},{6,70},{7,71},{8,72},{9,... | collective-permute-start | bytes 1572872 | tf_op jit(solution)/shard_map/ppermute | solution.py:50
  57.4 23.3 %collective-permute-start.10 = (bf16[128,2048]{1,0:T(8,128)(2,1)S(1)}, bf16[128,2048]{1,0:T(8,128)(2,1)S(1)}, u32[]{:S(2)}, u32[]{:S(2)}) collective-permute-start(bf16[128,2048]{1,0:T(8,128)(2,1)S(1)} %get-tuple-element.120), channel_id=1, source_target_pairs={{0,192},{1,193},{2,194},{3,195},{4,196},{5,197},{6,198},{7,199},{8... | collective-permute-start | bytes 1572872 | tf_op jit(solution)/shard_map/ppermute | solution.py:50
  57.4 1.0 copy-start.5
  68.7 0.7 copy-start
  69.5 11.2 %copy-start.10 = (bf16[3,64,1024]{2,1,0:T(8,128)(2,1)}, bf16[3,64,1024]{2,1,0:T(8,128)(2,1)S(1)}, u32[]{:S(2)}) copy-start(bf16[3,64,1024]{2,1,0:T(8,128)(2,1)S(1)} %get-tuple-element.132) | copy-start | bytes 1179652
  69.5 11.2 %copy-start.11 = (bf16[3,64,1024]{2,1,0:T(8,128)(2,1)}, bf16[3,64,1024]{2,1,0:T(8,128)(2,1)S(1)}, u32[]{:S(2)}) copy-start(bf16[3,64,1024]{2,1,0:T(8,128)(2,1)S(1)} %get-tuple-element.133) | copy-start | bytes 1179652
  69.5 11.2 %copy-start.12 = (bf16[3,64,1024]{2,1,0:T(8,128)(2,1)}, bf16[3,64,1024]{2,1,0:T(8,128)(2,1)S(1)}, u32[]{:S(2)}) copy-start(bf16[3,64,1024]{2,1,0:T(8,128)(2,1)S(1)} %get-tuple-element.131) | copy-start | bytes 1179652
  80.7 18.4 %all-to-all-start = ((bf16[8,32,128]{2,1,0:T(8,128)(2,1)}), bf16[8,32,128]{2,1,0:T(8,128)(2,1)S(1)}, u32[]{:S(2)}, u32[]{:S(2)}) async-start(bf16[8,32,128]{2,1,0:T(8,128)(2,1)} %get-tuple-element.149), calls=%async_computation | async-start | bytes 131072 | tf_op jit(solution)/shard_map/all_to_all | solution.py:536
  90.6 26.3 %collective-permute-start.11 = (bf16[3,64,1024]{2,1,0:T(8,128)(2,1)}, bf16[3,64,1024]{2,1,0:T(8,128)(2,1)S(1)}, u32[]{:S(2)}, u32[]{:S(2)}) collective-permute-start(bf16[3,64,1024]{2,1,0:T(8,128)(2,1)} %copy-done.12), channel_id=1, source_target_pairs={{0,33},{1,34},{2,35},{3,36},{4,37},{5,38},{6,39},{7,40},{8,41},{9,... | collective-permute-start | bytes 1179656 | tf_op jit(solution)/shard_map/ppermute | solution.py:60
  90.6 26.3 %collective-permute-start.12 = (bf16[3,64,1024]{2,1,0:T(8,128)(2,1)}, bf16[3,64,1024]{2,1,0:T(8,128)(2,1)S(1)}, u32[]{:S(2)}, u32[]{:S(2)}) collective-permute-start(bf16[3,64,1024]{2,1,0:T(8,128)(2,1)} %copy-done.10), channel_id=1, source_target_pairs={{0,32},{1,33},{2,34},{3,35},{4,36},{5,37},{6,38},{7,39},{8,40},{9,... | collective-permute-start | bytes 1179656 | tf_op jit(solution)/shard_map/ppermute | solution.py:60
  91.6 25.3 %collective-permute-start.13 = (bf16[3,64,1024]{2,1,0:T(8,128)(2,1)}, bf16[3,64,1024]{2,1,0:T(8,128)(2,1)}, u32[]{:S(2)}, u32[]{:S(2)}) collective-permute-start(bf16[3,64,1024]{2,1,0:T(8,128)(2,1)} %copy-done.11), channel_id=1, source_target_pairs={{0,1},{1,2},{2,3},{3,4},{4,5},{5,6},{6,7},{7,8},{8,9},{9,10},{10,1... | collective-permute-start | bytes 1179656 | tf_op jit(solution)/shard_map/ppermute | solution.py:60
  117.7 6.4 %collective-permute-start.14 = (bf16[32,2048]{1,0:T(8,128)(2,1)S(1)}, bf16[32,2048]{1,0:T(8,128)(2,1)S(1)}, u32[]{:S(2)}, u32[]{:S(2)}) collective-permute-start(bf16[32,2048]{1,0:T(8,128)(2,1)S(1)} %get-tuple-element.146), channel_id=1, source_target_pairs={{0,32},{1,33},{2,34},{3,35},{4,36},{5,37},{6,38},{7,39},{8,40},{9,... | collective-permute-start | bytes 393224 | tf_op jit(solution)/shard_map/ppermute | solution.py:50
  118.9 7.9 %collective-permute-start.15 = (bf16[32,2048]{1,0:T(8,128)(2,1)S(1)}, bf16[32,2048]{1,0:T(8,128)(2,1)S(1)}, u32[]{:S(2)}, u32[]{:S(2)}) collective-permute-start(bf16[32,2048]{1,0:T(8,128)(2,1)S(1)} %get-tuple-element.147), channel_id=1, source_target_pairs={{0,2},{1,3},{2,0},{3,1},{4,6},{5,7},{6,4},{7,5},{8,10},{9,11},{10,... | collective-permute-start | bytes 393224 | tf_op jit(solution)/shard_map/ppermute | solution.py:50
  120.1 8.7 %collective-permute-start.16 = (bf16[32,2048]{1,0:T(8,128)(2,1)S(1)}, bf16[32,2048]{1,0:T(8,128)(2,1)S(1)}, u32[]{:S(2)}, u32[]{:S(2)}) collective-permute-start(bf16[32,2048]{1,0:T(8,128)(2,1)S(1)} %get-tuple-element.148), channel_id=1, source_target_pairs={{0,34},{1,35},{2,32},{3,33},{4,38},{5,39},{6,36},{7,37},{8,42},{9,... | collective-permute-start | bytes 393224 | tf_op jit(solution)/shard_map/ppermute | solution.py:50
  129.5 18.2 %all-to-all-start.2 = ((bf16[8,4,3072]{2,1,0:T(4,128)(2,1)}), bf16[8,4,3072]{2,1,0:T(4,128)(2,1)S(1)}, u32[]{:S(2)}, u32[]{:S(2)}) async-start(bf16[8,4,3072]{2,1,0:T(4,128)(2,1)} %sum_for_z.1), calls=%async_computation.2 | async-start | bytes 393216 | tf_op jit(solution)/shard_map/all_to_all | solution.py:536
  137.2 1.0 copy-start.1

commit v3 on v2

--- a/solution.py
+++ b/solution.py
@@ -25,7 +25,7 @@
 PER_TILE = TILE // HEAD_DIM
 GROUP = 2
 BIAS_HEADS = 8
-EARLY = 1
+EARLY = 2
 QUAD = 64
 TOKENS = 256
 
@@ -612,15 +612,17 @@
     g_tl, g_bl, g_tr, g_br, table_part = backward(
         logit_scale, quads, grad_attn, probs, EARLY, INNER // TILE // GROUP - EARLY, found
     )
-    near = [move(terms[s], along_x(s)) for s in (1, 3)]
-    across = move(terms[2], along_x(2))
-    near, g_tl, g_bl, g_tr, g_br, table_part = lax.optimization_barrier(
-        (near, g_tl, g_bl, g_tr, g_br, table_part)
+    down, right = move_map(g_bl, 1, 0), move_map(g_tr, 0, 1)
+    sent = [move(terms[s], along_x(s)) for s in range(1, NX)]
+    sent[0], sent[2], g_br, table_part = lax.optimization_barrier(
+        (sent[0], sent[2], g_br, table_part)
     )
-    arrived = (move_map(g_br, 1, 1), move_map(g_bl, 1, 0), move_map(g_tr, 0, 1))
-    piece = table_plane(table_pieces(table_part))
-    across, arrived = lax.optimization_barrier((across, arrived))
-    terms = sum_for_y(place, (terms[0], near[0], across, near[1]))
+    arrived = (move_map(g_br, 1, 1), down, right)
+    piece = table_pieces(table_part)
+    sent, arrived = lax.optimization_barrier((sent, arrived))
+    terms = sum_for_y(place, (terms[0], *sent))
+    terms, piece = lax.optimization_barrier((terms, piece))
+    piece = table_plane(piece)
     grads = join_maps(*arrived, g_tl)
     weight_grad, table_grad, log_grad = totals(terms, piece)
     return (*grads, weight_grad, table_grad, log_grad)

time: 153 us -> 144 us (0.941)
  starting transfers between devices: 48.7 us -> 41.3 us
  Pallas kernels: 47.1 us -> 43.8 us
  waiting for transfers between devices: 28.4 us -> 31.3 us
  local copies, waits for them, and re-layouts: 6.02 us -> 3.95 us
    all_to_all x2 -> x1, starting transfers between devices: 17.5 us -> 3.5 us  [along_z_exchange(): lax.all_to_all(value, 'col', 0, 0, axis_index_groups=groups, tiled=True)]
    all_to_all x0 -> x1, starting transfers between devices: none -> 11.4 us  [table_plane(): lax.all_to_all(same, ('row', 'col'), 0, 0, axis_index_groups=groups, tile...]
    ppermute x9, starting transfers between devices: 18.1 us -> 13.4 us  [move_map(): return lax.ppermute(value, ('row', 'col'), pairs)]
    all_to_all x0 -> x1, waiting for transfers between devices: none -> 4.58 us  [table_plane(): lax.all_to_all(same, ('row', 'col'), 0, 0, axis_index_groups=groups, tile...]
    unnamed x39 -> x19, local copies, waits for them, and re-layouts: 5.27 us -> 2.5 us
    all_to_all x1, blocking collectives: 17.7 us -> 19.2 us  [along_z_exchange(): lax.all_to_all(value, 'col', 0, 0, axis_index_groups=groups, tiled=True)]
    all_to_all x2 -> x1, waiting for transfers between devices: 9.74 us -> 8.67 us  [along_z_exchange(): lax.all_to_all(value, 'col', 0, 0, axis_index_groups=groups, tiled=True)]
  transfers between devices with their start and end apart: 19 -> 19, of which waited for: 7 -> 7; matrix products, arithmetic and copies ran while one was open for 2% -> 2% of each run, Pallas kernels for 26% -> 25%
where the time goes in v3:
time: 144 us; the launch traced here: 142 us
  Pallas kernels  43.8 us (30%)
  starting transfers between devices  41.3 us (29%)
  waiting for transfers between devices  31.3 us (22%)
  blocking collectives  19.2 us (13%)
  local copies, waits for them, and re-layouts  3.95 us (3%)
    all_to_all x1, blocking collectives, along_z_exchange(): lax.all_to_all(value, 'col', 0, 0, axis_index_groups=groups, tiled=True)  19.2 us
    ppermute x8, waiting for transfers between devices, move(): return lax.ppermute(value, ('row', 'col'), pairs)  18.1 us
    pallas_call x2, Pallas kernels, backward(): pl.pallas_call(functools.partial(backward_kernel, first), grid=(steps,),...  14.1 us
    ppermute x9, starting transfers between devices, move_map(): return lax.ppermute(value, ('row', 'col'), pairs)  13.4 us
    ppermute x8, starting transfers between devices, move(): return lax.ppermute(value, ('row', 'col'), pairs)  13 us
    all_to_all x1, starting transfers between devices, table_plane(): lax.all_to_all(same, ('row', 'col'), 0, 0, axis_index_groups=groups, tile...  11.4 us
    pallas_call x1, Pallas kernels, forward(): pl.pallas_call(forward_kernel, grid=(INNER // TILE // GROUP,), in_specs=[...  9.58 us
    all_to_all x1, waiting for transfers between devices, along_z_exchange(): lax.all_to_all(value, 'col', 0, 0, axis_index_groups=groups, tiled=True)  8.67 us
  transfers between devices with their start and end apart: 19, of which 7 were waited for; matrix products, arithmetic and copies ran while one was open for 2% of the time, Pallas kernels for 25%

profile of v3, /device:TPU:24, one launch (start us, length us, event | category | flops | bytes accessed | tf_op | source)
XLA Modules:
  0.0 142.1 jit_solution(17299275970124222249)
XLA Ops:
  0.6 3.6 %split_maps.1 = (bf16[3,64,1024]{2,1,0:T(8,128)(2,1)}, bf16[3,64,1024]{2,1,0:T(8,128)(2,1)}, bf16[3,64,1024]{2,1,0:T(8,128)(2,1)}, bf16[3,64,1024]{2,1,0:T(8,128)(2,1)}) custom-call(bf16[16,16,1024]{2,1,0:T(8,128)(2,1)} %q_ref.1, bf16[16,16,1024]{2,1,0:T(8,128)(2,1)} %k_ref.1, bf16[16,16,1024]{2,1,0:T(8,128)(2,1)} %v_ref.1), custom_call_target="tpu_custom_call" | custom-call | tf_op jit(solution)/shard_map/split_maps/pallas_call | solution.py:106
  4.3 0.8 collective-permute-start
  5.0 0.0 collective-permute-start.1
  5.0 3.3 %collective-permute-start.2 = (bf16[3,64,1024]{2,1,0:T(8,128)(2,1)}, bf16[3,64,1024]{2,1,0:T(8,128)(2,1)S(1)}, u32[]{:S(2)}, u32[]{:S(2)}) collective-permute-start(bf16[3,64,1024]{2,1,0:T(8,128)(2,1)} %get-tuple-element.86), channel_id=1, source_target_pairs={{0,255},{1,224},{2,225},{3,226},{4,227},{5,228},{6,229},{7,230},{8... | collective-permute-start | bytes 1179656 | tf_op jit(solution)/shard_map/ppermute | solution.py:60
  8.4 1.3 copy.23.table_ref
  9.7 3.8 %split_dropped.1 = (bf16[64,2048]{1,0:T(8,128)(2,1)}, bf16[64,2048]{1,0:T(8,128)(2,1)}, bf16[64,2048]{1,0:T(8,128)(2,1)}, bf16[64,2048]{1,0:T(8,128)(2,1)}) custom-call(bf16[16,16,2048]{2,1,0:T(8,128)(2,1)} %grad_ref.1, s32[16,16,2048]{2,1,0:T(8,128)} %keep_ref.1), custom_call_target="tpu_custom_call" | custom-call | tf_op jit(solution)/shard_map/split_dropped/pallas_call | solution.py:126
  13.5 0.0 copy-start.6
  13.6 0.0 copy-start
  13.6 6.5 %bias_blocks.1.bias_ref = f32[32,3,128,128]{3,2,1,0:T(8,128)} custom-call(f32[32,31,31]{2,1,0:T(8,128)S(1)} %copy.23.table_ref), custom_call_target="tpu_custom_call" | custom-call | flops 10000000 | bytes 8000000 | tf_op jit(solution)/shard_map/bias_blocks/pallas_call | solution.py:180
  20.0 0.1 collective-permute-start.3
  20.2 8.4 %collective-permute-start.4 = (bf16[64,2048]{1,0:T(8,128)(2,1)S(1)}, bf16[64,2048]{1,0:T(8,128)(2,1)S(1)}, u32[]{:S(2)}, u32[]{:S(2)}) collective-permute-start(bf16[64,2048]{1,0:T(8,128)(2,1)S(1)} %copy-done.4), channel_id=1, source_target_pairs={{0,31},{1,0},{2,1},{3,2},{4,3},{5,4},{6,5},{7,6},{8,7},{9,8},{10,9... | collective-permute-start | bytes 786440 | tf_op jit(solution)/shard_map/ppermute | solution.py:60
  28.5 0.1 pad_add_fusion.place_ref
  28.6 0.0 collective-permute-done.2.br_ref
  28.7 0.6 collective-permute-start.5
  29.3 9.6 %forward.1 = (bf16[1024,256]{1,0:T(8,128)(2,1)S(1)}, f32[32,256,256]{2,1,0:T(8,128)}) custom-call(f32[32]{0:T(128)S(1)} %get-tuple-element.179.scale_ref, bf16[3,64,1024]{2,1,0:T(8,128)(2,1)S(1)} %copy-done, bf16[3,64,1024]{2,1,0:T(8,128)(2,1)S(1)} %collective-permute-done.bl_ref, bf16[3,64,1024]{2,1,0:T(8,128)(2,1)S(1)} %collective-permute-done.1.tr_ref, ...), custom_call_target="tpu_custom_call" | custom-call | flops 8000000000 | bytes 16000000 | tf_op jit(solution)/shard_map/forward/pallas_call | solution.py:277
  38.9 0.0 collective-permute-done.3
  38.9 1.0 collective-permute-start.6
  40.0 0.3 collective-permute-start.7
  40.3 1.4 convolution_convert_fusion.grad_ref
  41.7 7.0 %backward.2 = (bf16[3,64,1024]{2,1,0:T(8,128)(2,1)S(1)}, bf16[3,64,1024]{2,1,0:T(8,128)(2,1)S(1)}, bf16[3,64,1024]{2,1,0:T(8,128)(2,1)S(1)}, bf16[3,64,1024]{2,1,0:T(8,128)(2,1)S(1)}, bf16[8,32,128]{2,1,0:T(8,128)(2,1)S(1)}) custom-call(f32[32]{0:T(128)S(1)} %get-tuple-element.178.scale_ref, bf16[3,64,1024]{2,1,0:T(8,128)(2,1)S(1)} %copy-done, ...), custom_call_target="tpu_custom_call" | custom-call | flops 8000000000 | bytes 10000000 | tf_op jit(solution)/shard_map/backward/pallas_call | solution.py:428
  48.8 2.2 %outer_terms.1 = (f32[128,2048]{1,0:T(8,128)S(1)}, bf16[128,2048]{1,0:T(8,128)(2,1)S(1)}, bf16[128,2048]{1,0:T(8,128)(2,1)S(1)}, bf16[128,2048]{1,0:T(8,128)(2,1)S(1)}) custom-call(s32[4]{0:T(128)S(1)} %pad_add_fusion.place_ref, bf16[1024,256]{1,0:T(8,128)(2,1)S(1)} %get-tuple-element.100.own_ref, bf16[1024,256]{1,0:T(8,128)(2,1)S(1)} %collective-permute-done.6.other_ref, ...), custom_call_target="tpu_custom_call" | custom-call | flops 1100000000 | bytes 6000000 | tf_op jit(solution)/shard_map/outer_terms/pallas_call | solution.py:468
  51.0 1.2 collective-permute-start.8
  52.2 6.1 %collective-permute-start.9 = (bf16[128,2048]{1,0:T(8,128)(2,1)S(1)}, bf16[128,2048]{1,0:T(8,128)(2,1)S(1)}, u32[]{:S(2)}, u32[]{:S(2)}) collective-permute-start(bf16[128,2048]{1,0:T(8,128)(2,1)S(1)} %get-tuple-element.123), channel_id=1, source_target_pairs={{0,192},{1,193},{2,194},{3,195},{4,196},{5,197},{6,198},{7,199},{8... | collective-permute-start | bytes 1572872 | tf_op jit(solution)/shard_map/ppermute | solution.py:50
  58.3 1.4 collective-permute-start.10
  59.7 7.0 %backward.3 = (bf16[3,64,1024]{2,1,0:T(8,128)(2,1)S(1)}, bf16[3,64,1024]{2,1,0:T(8,128)(2,1)S(1)}, bf16[3,64,1024]{2,1,0:T(8,128)(2,1)S(1)}, bf16[3,64,1024]{2,1,0:T(8,128)(2,1)S(1)}, bf16[8,32,128]{2,1,0:T(8,128)(2,1)S(1)}) custom-call(f32[32]{0:T(128)S(1)} %get-tuple-element.178.scale_ref, ...), custom_call_target="tpu_custom_call", output_to_operand_aliasing={{0}: (7, {}), {1}: (8, {}), {2}: (9, {}), {3}: (10, {}), {4... | custom-call | flops 8000000000 | bytes 10000000 | tf_op jit(solution)/shard_map/backward/pallas_call | solution.py:428
  66.7 0.1 collective-permute-start.12
  66.8 0.1 collective-permute-start.13
  66.9 4.0 %collective-permute-done.8.refs_1_ = bf16[128,2048]{1,0:T(8,128)(2,1)S(1)} collective-permute-done((bf16[128,2048]{1,0:T(8,128)(2,1)S(1)}, bf16[128,2048]{1,0:T(8,128)(2,1)S(1)}, u32[]{:S(2)}, u32[]{:S(2)}) %collective-permute-start.8) | collective-permute-done | bytes 524320 | tf_op jit(solution)/shard_map/ppermute | solution.py:50
  70.9 10.0 %collective-permute-done.9.refs_3_ = bf16[128,2048]{1,0:T(8,128)(2,1)S(1)} collective-permute-done((bf16[128,2048]{1,0:T(8,128)(2,1)S(1)}, bf16[128,2048]{1,0:T(8,128)(2,1)S(1)}, u32[]{:S(2)}, u32[]{:S(2)}) %collective-permute-start.9) | collective-permute-done | bytes 524320 | tf_op jit(solution)/shard_map/ppermute | solution.py:50
  80.9 0.0 collective-permute-start.11
  80.9 19.2 %all_to_all.15 = bf16[8,32,128]{2,1,0:T(8,128)(2,1)S(1)} all-to-all(bf16[8,32,128]{2,1,0:T(8,128)(2,1)S(1)} %get-tuple-element.152), channel_id=1, replica_groups={{0,4,8,12,16,20,24,28},{1,5,9,13,17,21,25,29},{2,6,10,14,18,22,26,30},{..., dimensions={0} | all-to-all | bytes 131072 | tf_op jit(solution)/shard_map/all_to_all | solution.py:536
  100.2 0.8 sum_for_y.1
  101.0 0.7 broadcast_in_dim.3
  101.7 11.4 %all-to-all-start.1 = ((bf16[32,32,128]{2,1,0:T(8,128)(2,1)}), bf16[32,32,128]{2,1,0:T(8,128)(2,1)S(1)}, u32[]{:S(2)}, u32[]{:S(2)}) async-start(bf16[32,32,128]{2,1,0:T(8,128)(2,1)} %broadcast_in_dim.3), calls=%async_computation.1 | async-start | bytes 524288 | tf_op jit(solution)/shard_map/all_to_all | solution.py:550
  113.1 0.3 collective-permute-start.14
  113.4 2.7 %collective-permute-start.15 = (bf16[32,2048]{1,0:T(8,128)(2,1)S(1)}, bf16[32,2048]{1,0:T(8,128)(2,1)S(1)}, u32[]{:S(2)}, u32[]{:S(2)}) collective-permute-start(bf16[32,2048]{1,0:T(8,128)(2,1)S(1)} %get-tuple-element.155), channel_id=1, source_target_pairs={{0,2},{1,3},{2,0},{3,1},{4,6},{5,7},{6,4},{7,5},{8,10},{9,11},{10,... | collective-permute-start | bytes 393224 | tf_op jit(solution)/shard_map/ppermute | solution.py:50
  116.1 4.6 %all-to-all-done.1 = bf16[32,32,128]{2,1,0:T(8,128)(2,1)S(1)} async-done(((bf16[32,32,128]{2,1,0:T(8,128)(2,1)}), bf16[32,32,128]{2,1,0:T(8,128)(2,1)S(1)}, u32[]{:S(2)}, u32[]{:S(2)}) %all-to-all-start.1) | async-done | bytes 262176 | tf_op jit(solution)/shard_map/all_to_all | solution.py:550
  120.8 0.6 collective-permute-done.14.refs_1_
  121.4 1.3 collective-permute-done.15.refs_2_
  122.7 2.1 %collective-permute-done.16.refs_3_ = bf16[32,2048]{1,0:T(8,128)(2,1)S(1)} collective-permute-done((bf16[32,2048]{1,0:T(8,128)(2,1)S(1)}, bf16[32,2048]{1,0:T(8,128)(2,1)S(1)}, u32[]{:S(2)}, u32[]{:S(2)}) %collective-permute-start.16) | collective-permute-done | bytes 131104 | tf_op jit(solution)/shard_map/ppermute | solution.py:50
  124.8 0.8 sum_for_z.1
  125.6 3.5 %all-to-all-start.2 = ((bf16[8,4,3072]{2,1,0:T(4,128)(2,1)}), bf16[8,4,3072]{2,1,0:T(4,128)(2,1)S(1)}, u32[]{:S(2)}, u32[]{:S(2)}) async-start(bf16[8,4,3072]{2,1,0:T(4,128)(2,1)} %sum_for_z.1), calls=%async_computation.2 | async-start | bytes 393216 | tf_op jit(solution)/shard_map/all_to_all | solution.py:536
  129.1 1.9 %join_maps.1 = (bf16[16,16,1024]{2,1,0:T(8,128)(2,1)}, bf16[16,16,1024]{2,1,0:T(8,128)(2,1)}, bf16[16,16,1024]{2,1,0:T(8,128)(2,1)}) custom-call(bf16[3,64,1024]{2,1,0:T(8,128)(2,1)S(1)} %collective-permute-done.11.tl_ref, bf16[3,64,1024]{2,1,0:T(8,128)(2,1)S(1)} %collective-permute-done.12.tr_ref, bf16[3,64,1024]{2,1,0:T(8,128)(2,1)S(1)} %collective-permute-done.13.bl_ref, ...), custom_call_target="tpu_custom_call" | custom-call | tf_op jit(solution)/shard_map/join_maps/pallas_call | solution.py:147
  131.0 8.7 %all-to-all-done.2.found_ref = bf16[8,4,3072]{2,1,0:T(4,128)(2,1)S(1)} async-done(((bf16[8,4,3072]{2,1,0:T(4,128)(2,1)}), bf16[8,4,3072]{2,1,0:T(4,128)(2,1)S(1)}, u32[]{:S(2)}, u32[]{:S(2)}) %all-to-all-start.2) | async-done | bytes 196640 | tf_op jit(solution)/shard_map/all_to_all | solution.py:536
  139.7 0.1 slice.3
  139.8 0.6 reshape.16
  140.4 0.7 totals.1
  141.0 1.1 copy.24
  (32 shorter events, 0.2 us)
Async XLA Ops:
  4.3 24.4 %collective-permute-start = (bf16[3,64,1024]{2,1,0:T(8,128)(2,1)}, bf16[3,64,1024]{2,1,0:T(8,128)(2,1)S(1)}, u32[]{:S(2)}, u32[]{:S(2)}) collective-permute-start(bf16[3,64,1024]{2,1,0:T(8,128)(2,1)} %get-tuple-element.84), channel_id=1, source_target_pairs={{0,224},{1,225},{2,226},{3,227},{4,228},{5,229},{6,230},{7,231},{8... | collective-permute-start | bytes 1179656 | tf_op jit(solution)/shard_map/ppermute | solution.py:60
  5.0 23.6 %collective-permute-start.1 = (bf16[3,64,1024]{2,1,0:T(8,128)(2,1)}, bf16[3,64,1024]{2,1,0:T(8,128)(2,1)S(1)}, u32[]{:S(2)}, u32[]{:S(2)}) collective-permute-start(bf16[3,64,1024]{2,1,0:T(8,128)(2,1)} %get-tuple-element.85), channel_id=1, source_target_pairs={{0,31},{1,0},{2,1},{3,2},{4,3},{5,4},{6,5},{7,6},{8,7},{9,8},{10,9... | collective-permute-start | bytes 1179656 | tf_op jit(solution)/shard_map/ppermute | solution.py:60
  5.0 23.6 %collective-permute-start.2 = (bf16[3,64,1024]{2,1,0:T(8,128)(2,1)}, bf16[3,64,1024]{2,1,0:T(8,128)(2,1)S(1)}, u32[]{:S(2)}, u32[]{:S(2)}) collective-permute-start(bf16[3,64,1024]{2,1,0:T(8,128)(2,1)} %get-tuple-element.86), channel_id=1, source_target_pairs={{0,255},{1,224},{2,225},{3,226},{4,227},{5,228},{6,229},{7,230},{8... | collective-permute-start | bytes 1179656 | tf_op jit(solution)/shard_map/ppermute | solution.py:60
  13.5 6.5 %copy-start.5 = (bf16[64,2048]{1,0:T(8,128)(2,1)S(1)}, bf16[64,2048]{1,0:T(8,128)(2,1)}, u32[]{:S(2)}) copy-start(bf16[64,2048]{1,0:T(8,128)(2,1)} %get-tuple-element.97) | copy-start | bytes 786436
  13.5 6.6 %copy-start.4 = (bf16[64,2048]{1,0:T(8,128)(2,1)S(1)}, bf16[64,2048]{1,0:T(8,128)(2,1)}, u32[]{:S(2)}) copy-start(bf16[64,2048]{1,0:T(8,128)(2,1)} %get-tuple-element.98) | copy-start | bytes 786436
  13.5 15.1 %copy-start.6 = (f32[32]{0:T(128)S(1)}, f32[32]{0:T(128)}, u32[]{:S(2)}) copy-start(f32[32]{0:T(128)} %param.13) | copy-start | bytes 388
  13.6 15.1 %copy-start.3 = (bf16[64,2048]{1,0:T(8,128)(2,1)S(1)}, bf16[64,2048]{1,0:T(8,128)(2,1)}, u32[]{:S(2)}) copy-start(bf16[64,2048]{1,0:T(8,128)(2,1)} %get-tuple-element.99) | copy-start | bytes 786436
  13.6 15.7 %copy-start = (bf16[3,64,1024]{2,1,0:T(8,128)(2,1)S(1)}, bf16[3,64,1024]{2,1,0:T(8,128)(2,1)}, u32[]{:S(2)}) copy-start(bf16[3,64,1024]{2,1,0:T(8,128)(2,1)} %get-tuple-element.88.tl_ref) | copy-start | bytes 1179652
  20.0 18.8 %collective-permute-start.3 = (bf16[64,2048]{1,0:T(8,128)(2,1)S(1)}, bf16[64,2048]{1,0:T(8,128)(2,1)S(1)}, u32[]{:S(2)}, u32[]{:S(2)}) collective-permute-start(bf16[64,2048]{1,0:T(8,128)(2,1)S(1)} %copy-done.5), channel_id=1, source_target_pairs={{0,224},{1,225},{2,226},{3,227},{4,228},{5,229},{6,230},{7,231},{8... | collective-permute-start | bytes 786440 | tf_op jit(solution)/shard_map/ppermute | solution.py:60
  20.2 18.7 %collective-permute-start.4 = (bf16[64,2048]{1,0:T(8,128)(2,1)S(1)}, bf16[64,2048]{1,0:T(8,128)(2,1)S(1)}, u32[]{:S(2)}, u32[]{:S(2)}) collective-permute-start(bf16[64,2048]{1,0:T(8,128)(2,1)S(1)} %copy-done.4), channel_id=1, source_target_pairs={{0,31},{1,0},{2,1},{3,2},{4,3},{5,4},{6,5},{7,6},{8,7},{9,8},{10,9... | collective-permute-start | bytes 786440 | tf_op jit(solution)/shard_map/ppermute | solution.py:60
  28.7 10.2 %collective-permute-start.5 = (bf16[64,2048]{1,0:T(8,128)(2,1)S(1)}, bf16[64,2048]{1,0:T(8,128)(2,1)S(1)}, u32[]{:S(2)}, u32[]{:S(2)}) collective-permute-start(bf16[64,2048]{1,0:T(8,128)(2,1)S(1)} %copy-done.3), channel_id=1, source_target_pairs={{0,255},{1,224},{2,225},{3,226},{4,227},{5,228},{6,229},{7,230},{8... | collective-permute-start | bytes 786440 | tf_op jit(solution)/shard_map/ppermute | solution.py:60
  29.3 10.6 %copy-start.1 = (bf16[64,2048]{1,0:T(8,128)(2,1)S(1)}, bf16[64,2048]{1,0:T(8,128)(2,1)}, u32[]{:S(2)}) copy-start(bf16[64,2048]{1,0:T(8,128)(2,1)} %get-tuple-element.101) | copy-start | bytes 786436
  29.3 11.0 %copy-start.2 = (bf16[1024,2048]{1,0:T(8,128)(2,1)S(1)}, bf16[1024,2048]{1,0:T(8,128)(2,1)}, u32[]{:S(2)}) copy-start(bf16[1024,2048]{1,0:T(8,128)(2,1)} %param.15) | copy-start | bytes 12582916
  38.9 9.8 %collective-permute-start.6 = (bf16[1024,256]{1,0:T(8,128)(2,1)S(1)}, bf16[1024,256]{1,0:T(8,128)(2,1)S(1)}, u32[]{:S(2)}, u32[]{:S(2)}) collective-permute-start(bf16[1024,256]{1,0:T(8,128)(2,1)S(1)} %get-tuple-element.100.own_ref), channel_id=1, source_target_pairs={{0,1},{1,0},{2,3},{3,2},{4,5},{5,4},{6,7},{7,6},{8,9},{9,8},{10,11... | collective-permute-start | bytes 1572872 | tf_op jit(solution)/shard_map/ppermute | solution.py:50
  40.0 8.8 %collective-permute-start.7 = (bf16[256,2048]{1,0:T(8,128)(2,1)S(1)}, bf16[256,2048]{1,0:T(8,128)(2,1)S(1)}, u32[]{:S(2)}, u32[]{:S(2)}) collective-permute-start(bf16[256,2048]{1,0:T(8,128)(2,1)S(1)} %constant_dynamic-update-slice_fusion.drop_ref), channel_id=1, source_target_pairs={{0,1},{1,0},{2,3},{3,2},{4,5},{5,4},{6,7},{7,6},{8,9},{9,8},{10,11... | collective-permute-start | bytes 3145736 | tf_op jit(solution)/shard_map/ppermute | solution.py:50
  51.0 19.9 %collective-permute-start.8 = (bf16[128,2048]{1,0:T(8,128)(2,1)S(1)}, bf16[128,2048]{1,0:T(8,128)(2,1)S(1)}, u32[]{:S(2)}, u32[]{:S(2)}) collective-permute-start(bf16[128,2048]{1,0:T(8,128)(2,1)S(1)} %get-tuple-element.122), channel_id=1, source_target_pairs={{0,64},{1,65},{2,66},{3,67},{4,68},{5,69},{6,70},{7,71},{8,72},{9,... | collective-permute-start | bytes 1572872 | tf_op jit(solution)/shard_map/ppermute | solution.py:50
  52.2 28.7 %collective-permute-start.9 = (bf16[128,2048]{1,0:T(8,128)(2,1)S(1)}, bf16[128,2048]{1,0:T(8,128)(2,1)S(1)}, u32[]{:S(2)}, u32[]{:S(2)}) collective-permute-start(bf16[128,2048]{1,0:T(8,128)(2,1)S(1)} %get-tuple-element.123), channel_id=1, source_target_pairs={{0,192},{1,193},{2,194},{3,195},{4,196},{5,197},{6,198},{7,199},{8... | collective-permute-start | bytes 1572872 | tf_op jit(solution)/shard_map/ppermute | solution.py:50
  58.3 41.9 %collective-permute-start.10 = (bf16[128,2048]{1,0:T(8,128)(2,1)S(1)}, bf16[128,2048]{1,0:T(8,128)(2,1)S(1)}, u32[]{:S(2)}, u32[]{:S(2)}) collective-permute-start(bf16[128,2048]{1,0:T(8,128)(2,1)S(1)} %get-tuple-element.132), channel_id=1, source_target_pairs={{0,128},{1,129},{2,130},{3,131},{4,132},{5,133},{6,134},{7,135},{8... | collective-permute-start | bytes 1572872 | tf_op jit(solution)/shard_map/ppermute | solution.py:50
  66.7 33.5 %collective-permute-start.12 = (bf16[3,64,1024]{2,1,0:T(8,128)(2,1)S(1)}, bf16[3,64,1024]{2,1,0:T(8,128)(2,1)S(1)}, u32[]{:S(2)}, u32[]{:S(2)}) collective-permute-start(bf16[3,64,1024]{2,1,0:T(8,128)(2,1)S(1)} %get-tuple-element.135), channel_id=1, source_target_pairs={{0,32},{1,33},{2,34},{3,35},{4,36},{5,37},{6,38},{7,39},{8,40},{9,... | collective-permute-start | bytes 1179656 | tf_op jit(solution)/shard_map/ppermute | solution.py:60
  66.8 33.4 %collective-permute-start.13 = (bf16[3,64,1024]{2,1,0:T(8,128)(2,1)S(1)}, bf16[3,64,1024]{2,1,0:T(8,128)(2,1)S(1)}, u32[]{:S(2)}, u32[]{:S(2)}) collective-permute-start(bf16[3,64,1024]{2,1,0:T(8,128)(2,1)S(1)} %get-tuple-element.136), channel_id=1, source_target_pairs={{0,1},{1,2},{2,3},{3,4},{4,5},{5,6},{6,7},{7,8},{8,9},{9,10},{10,1... | collective-permute-start | bytes 1179656 | tf_op jit(solution)/shard_map/ppermute | solution.py:60
  80.9 19.3 %collective-permute-start.11 = (bf16[3,64,1024]{2,1,0:T(8,128)(2,1)S(1)}, bf16[3,64,1024]{2,1,0:T(8,128)(2,1)S(1)}, u32[]{:S(2)}, u32[]{:S(2)}) collective-permute-start(bf16[3,64,1024]{2,1,0:T(8,128)(2,1)S(1)} %get-tuple-element.134), channel_id=1, source_target_pairs={{0,33},{1,34},{2,35},{3,36},{4,37},{5,38},{6,39},{7,40},{8,41},{9,... | collective-permute-start | bytes 1179656 | tf_op jit(solution)/shard_map/ppermute | solution.py:60
  101.7 19.0 %all-to-all-start.1 = ((bf16[32,32,128]{2,1,0:T(8,128)(2,1)}), bf16[32,32,128]{2,1,0:T(8,128)(2,1)S(1)}, u32[]{:S(2)}, u32[]{:S(2)}) async-start(bf16[32,32,128]{2,1,0:T(8,128)(2,1)} %broadcast_in_dim.3), calls=%async_computation.1 | async-start | bytes 524288 | tf_op jit(solution)/shard_map/all_to_all | solution.py:550
  113.1 8.3 %collective-permute-start.14 = (bf16[32,2048]{1,0:T(8,128)(2,1)S(1)}, bf16[32,2048]{1,0:T(8,128)(2,1)S(1)}, u32[]{:S(2)}, u32[]{:S(2)}) collective-permute-start(bf16[32,2048]{1,0:T(8,128)(2,1)S(1)} %get-tuple-element.154), channel_id=1, source_target_pairs={{0,32},{1,33},{2,34},{3,35},{4,36},{5,37},{6,38},{7,39},{8,40},{9,... | collective-permute-start | bytes 393224 | tf_op jit(solution)/shard_map/ppermute | solution.py:50
  113.4 9.2 %collective-permute-start.15 = (bf16[32,2048]{1,0:T(8,128)(2,1)S(1)}, bf16[32,2048]{1,0:T(8,128)(2,1)S(1)}, u32[]{:S(2)}, u32[]{:S(2)}) collective-permute-start(bf16[32,2048]{1,0:T(8,128)(2,1)S(1)} %get-tuple-element.155), channel_id=1, source_target_pairs={{0,2},{1,3},{2,0},{3,1},{4,6},{5,7},{6,4},{7,5},{8,10},{9,11},{10,... | collective-permute-start | bytes 393224 | tf_op jit(solution)/shard_map/ppermute | solution.py:50
  116.1 8.7 %collective-permute-start.16 = (bf16[32,2048]{1,0:T(8,128)(2,1)S(1)}, bf16[32,2048]{1,0:T(8,128)(2,1)S(1)}, u32[]{:S(2)}, u32[]{:S(2)}) collective-permute-start(bf16[32,2048]{1,0:T(8,128)(2,1)S(1)} %get-tuple-element.156), channel_id=1, source_target_pairs={{0,34},{1,35},{2,32},{3,33},{4,38},{5,39},{6,36},{7,37},{8,42},{9,... | collective-permute-start | bytes 393224 | tf_op jit(solution)/shard_map/ppermute | solution.py:50
  125.6 14.1 %all-to-all-start.2 = ((bf16[8,4,3072]{2,1,0:T(4,128)(2,1)}), bf16[8,4,3072]{2,1,0:T(4,128)(2,1)S(1)}, u32[]{:S(2)}, u32[]{:S(2)}) async-start(bf16[8,4,3072]{2,1,0:T(4,128)(2,1)} %sum_for_z.1), calls=%async_computation.2 | async-start | bytes 393216 | tf_op jit(solution)/shard_map/all_to_all | solution.py:536

commit v4 on v2

--- a/solution.py
+++ b/solution.py
@@ -25,7 +25,7 @@
 PER_TILE = TILE // HEAD_DIM
 GROUP = 2
 BIAS_HEADS = 8
-EARLY = 1
+EARLY = 2
 QUAD = 64
 TOKENS = 256
 
@@ -593,9 +593,8 @@
     quads = (br, move_map(tr, -1, 0), move_map(bl, 0, -1), move_map(tl, -1, -1))
     bias = bias_blocks(bias_table)
     tl, tr, bl, br = split_dropped(out_grad, keep_mask)
-    bias, tr, bl = lax.optimization_barrier((bias, tr, bl))
+    quads, tl, tr, bl = lax.optimization_barrier((quads, tl, tr, bl))
     up, left = move_map(tr, -1, 0), move_map(bl, 0, -1)
-    quads, tl = lax.optimization_barrier((quads, tl))
     attn_t, probs = forward(logit_scale * LOG2E, quads, bias)
     pieces = (br, up, left, move_map(tl, -1, -1))
     attn_t, pieces = lax.optimization_barrier((attn_t, pieces))
@@ -612,14 +611,12 @@
     g_tl, g_bl, g_tr, g_br, table_part = backward(
         logit_scale, quads, grad_attn, probs, EARLY, INNER // TILE // GROUP - EARLY, found
     )
+    arrived = (move_map(g_br, 1, 1), move_map(g_bl, 1, 0), move_map(g_tr, 0, 1))
     near = [move(terms[s], along_x(s)) for s in (1, 3)]
-    across = move(terms[2], along_x(2))
-    near, g_tl, g_bl, g_tr, g_br, table_part = lax.optimization_barrier(
-        (near, g_tl, g_bl, g_tr, g_br, table_part)
-    )
-    arrived = (move_map(g_br, 1, 1), move_map(g_bl, 1, 0), move_map(g_tr, 0, 1))
+    near, across, table_part = lax.optimization_barrier((near, terms[2], table_part))
+    across = move(across, along_x(2))
     piece = table_plane(table_pieces(table_part))
-    across, arrived = lax.optimization_barrier((across, arrived))
+    across, arrived, piece = lax.optimization_barrier((across, arrived, piece))
     terms = sum_for_y(place, (terms[0], near[0], across, near[1]))
     grads = join_maps(*arrived, g_tl)
     weight_grad, table_grad, log_grad = totals(terms, piece)

time: 153 us -> 158 us (1.033); the launches traced: 150 us -> 157 us
  waiting for transfers between devices: 28.4 us -> 43.4 us
  starting transfers between devices: 48.7 us -> 39.3 us
  local copies, waits for them, and re-layouts: 6.02 us -> 8.93 us
    ppermute x9, waiting for transfers between devices: 0.02 us -> 26.7 us  [move_map(): return lax.ppermute(value, ('row', 'col'), pairs)]
    all_to_all x2 -> x1, starting transfers between devices: 17.5 us -> 3.39 us  [along_z_exchange(): lax.all_to_all(value, 'col', 0, 0, axis_index_groups=groups, tiled=True)]
    ppermute x8, waiting for transfers between devices: 18.6 us -> 8 us  [move(): return lax.ppermute(value, ('row', 'col'), pairs)]
    all_to_all x0 -> x1, starting transfers between devices: none -> 7.29 us  [table_plane(): lax.all_to_all(same, ('row', 'col'), 0, 0, axis_index_groups=groups, tile...]
    all_to_all x2 -> x1, waiting for transfers between devices: 9.74 us -> 5.57 us  [along_z_exchange(): lax.all_to_all(value, 'col', 0, 0, axis_index_groups=groups, tiled=True)]
    all_to_all x0 -> x1, waiting for transfers between devices: none -> 3.14 us  [table_plane(): lax.all_to_all(same, ('row', 'col'), 0, 0, axis_index_groups=groups, tile...]
    ppermute x9, starting transfers between devices: 18.1 us -> 15 us  [move_map(): return lax.ppermute(value, ('row', 'col'), pairs)]
    unnamed x39 -> x41, local copies, waits for them, and re-layouts: 5.27 us -> 7.49 us
  transfers between devices with their start and end apart: 19 -> 19, of which waited for: 7 -> 10; matrix products, arithmetic and copies ran while one was open for 2% -> 2% of each run, Pallas kernels for 26% -> 24%
where the time goes in v4:
time: 158 us; the launch traced here: 157 us
  Pallas kernels  45.9 us (29%)
  waiting for transfers between devices  43.4 us (27%)
  starting transfers between devices  39.3 us (25%)
  blocking collectives  16.6 us (11%)
  local copies, waits for them, and re-layouts  8.93 us (6%)
    ppermute x9, waiting for transfers between devices, move_map(): return lax.ppermute(value, ('row', 'col'), pairs)  26.7 us
    all_to_all x1, blocking collectives, along_z_exchange(): lax.all_to_all(value, 'col', 0, 0, axis_index_groups=groups, tiled=True)  16.6 us
    ppermute x9, starting transfers between devices, move_map(): return lax.ppermute(value, ('row', 'col'), pairs)  15 us
    pallas_call x2, Pallas kernels, backward(): pl.pallas_call(functools.partial(backward_kernel, first), grid=(steps,),...  14.1 us
    ppermute x8, starting transfers between devices, move(): return lax.ppermute(value, ('row', 'col'), pairs)  13.6 us
    pallas_call x1, Pallas kernels, forward(): pl.pallas_call(forward_kernel, grid=(INNER // TILE // GROUP,), in_specs=[...  9.58 us
    ppermute x8, waiting for transfers between devices, move(): return lax.ppermute(value, ('row', 'col'), pairs)  8 us
    unnamed x41, local copies, waits for them, and re-layouts  7.49 us
  transfers between devices with their start and end apart: 19, of which 10 were waited for; matrix products, arithmetic and copies ran while one was open for 2% of the time, Pallas kernels for 24%

profile of v4, /device:TPU:24, one launch (start us, length us, event | category | flops | bytes accessed | tf_op | source)
XLA Modules:
  0.0 157.4 jit_solution(14239816149939820871)
XLA Ops:
  0.6 3.6 %split_maps.1 = (bf16[3,64,1024]{2,1,0:T(8,128)(2,1)}, bf16[3,64,1024]{2,1,0:T(8,128)(2,1)}, bf16[3,64,1024]{2,1,0:T(8,128)(2,1)}, bf16[3,64,1024]{2,1,0:T(8,128)(2,1)}) custom-call(bf16[16,16,1024]{2,1,0:T(8,128)(2,1)} %q_ref.1, bf16[16,16,1024]{2,1,0:T(8,128)(2,1)} %k_ref.1, bf16[16,16,1024]{2,1,0:T(8,128)(2,1)} %v_ref.1), custom_call_target="tpu_custom_call" | custom-call | tf_op jit(solution)/shard_map/split_maps/pallas_call | solution.py:106
  4.3 0.8 collective-permute-start
  5.0 3.3 %collective-permute-start.2 = (bf16[3,64,1024]{2,1,0:T(8,128)(2,1)}, bf16[3,64,1024]{2,1,0:T(8,128)(2,1)S(1)}, u32[]{:S(2)}, u32[]{:S(2)}) collective-permute-start(bf16[3,64,1024]{2,1,0:T(8,128)(2,1)} %get-tuple-element.79), channel_id=1, source_target_pairs={{0,255},{1,224},{2,225},{3,226},{4,227},{5,228},{6,229},{7,230},{8... | collective-permute-start | bytes 1179656 | tf_op jit(solution)/shard_map/ppermute | solution.py:60
  8.4 1.3 copy.23.table_ref
  9.7 3.8 %split_dropped.1 = (bf16[64,2048]{1,0:T(8,128)(2,1)}, bf16[64,2048]{1,0:T(8,128)(2,1)}, bf16[64,2048]{1,0:T(8,128)(2,1)}, bf16[64,2048]{1,0:T(8,128)(2,1)}) custom-call(bf16[16,16,2048]{2,1,0:T(8,128)(2,1)} %grad_ref.1, s32[16,16,2048]{2,1,0:T(8,128)} %keep_ref.1), custom_call_target="tpu_custom_call" | custom-call | tf_op jit(solution)/shard_map/split_dropped/pallas_call | solution.py:126
  13.6 6.5 %bias_blocks.1.bias_ref = f32[32,3,128,128]{3,2,1,0:T(8,128)} custom-call(f32[32,31,31]{2,1,0:T(8,128)S(1)} %copy.23.table_ref), custom_call_target="tpu_custom_call" | custom-call | flops 10000000 | bytes 8000000 | tf_op jit(solution)/shard_map/bias_blocks/pallas_call | solution.py:180
  20.2 1.9 %collective-permute-done.1.tr_ref = bf16[3,64,1024]{2,1,0:T(8,128)(2,1)S(1)} collective-permute-done((bf16[3,64,1024]{2,1,0:T(8,128)(2,1)}, bf16[3,64,1024]{2,1,0:T(8,128)(2,1)S(1)}, u32[]{:S(2)}, u32[]{:S(2)}) %collective-permute-start.1) | collective-permute-done | bytes 393248 | tf_op jit(solution)/shard_map/ppermute | solution.py:60
  22.2 1.4 collective-permute-done.2.br_ref
  23.6 2.1 %collective-permute-start.3 = (bf16[64,2048]{1,0:T(8,128)(2,1)S(1)}, bf16[64,2048]{1,0:T(8,128)(2,1)S(1)}, u32[]{:S(2)}, u32[]{:S(2)}) collective-permute-start(bf16[64,2048]{1,0:T(8,128)(2,1)S(1)} %copy-done.16), channel_id=1, source_target_pairs={{0,224},{1,225},{2,226},{3,227},{4,228},{5,229},{6,230},{7,231},{8... | collective-permute-start | bytes 786440 | tf_op jit(solution)/shard_map/ppermute | solution.py:60
  25.7 3.6 %collective-permute-start.4 = (bf16[64,2048]{1,0:T(8,128)(2,1)S(1)}, bf16[64,2048]{1,0:T(8,128)(2,1)S(1)}, u32[]{:S(2)}, u32[]{:S(2)}) collective-permute-start(bf16[64,2048]{1,0:T(8,128)(2,1)S(1)} %copy-done.15), channel_id=1, source_target_pairs={{0,31},{1,0},{2,1},{3,2},{4,3},{5,4},{6,5},{7,6},{8,7},{9,8},{10,9... | collective-permute-start | bytes 786440 | tf_op jit(solution)/shard_map/ppermute | solution.py:60
  29.2 3.7 %collective-permute-start.5 = (bf16[64,2048]{1,0:T(8,128)(2,1)S(1)}, bf16[64,2048]{1,0:T(8,128)(2,1)S(1)}, u32[]{:S(2)}, u32[]{:S(2)}) collective-permute-start(bf16[64,2048]{1,0:T(8,128)(2,1)S(1)} %copy-done.14), channel_id=1, source_target_pairs={{0,255},{1,224},{2,225},{3,226},{4,227},{5,228},{6,229},{7,230},{8... | collective-permute-start | bytes 786440 | tf_op jit(solution)/shard_map/ppermute | solution.py:60
  32.9 9.6 %forward.1 = (bf16[1024,256]{1,0:T(8,128)(2,1)S(1)}, f32[32,256,256]{2,1,0:T(8,128)}) custom-call(f32[32]{0:T(128)S(1)} %get-tuple-element.165.scale_ref, bf16[3,64,1024]{2,1,0:T(8,128)(2,1)S(1)} %copy-done.2, bf16[3,64,1024]{2,1,0:T(8,128)(2,1)S(1)} %collective-permute-done.bl_ref, bf16[3,64,1024]{2,1,0:T(8,128)(2,1)S(1)} %collective-permute-done.1.tr_ref, ...), custom_call_target="tpu_custom_call" | custom-call | flops 8000000000 | bytes 16000000 | tf_op jit(solution)/shard_map/forward/pallas_call | solution.py:277
  42.8 0.8 collective-permute-start.7
  43.5 1.3 convolution_convert_fusion.grad_ref
  44.9 7.0 %backward.2 = (bf16[3,64,1024]{2,1,0:T(8,128)(2,1)S(1)}, bf16[3,64,1024]{2,1,0:T(8,128)(2,1)S(1)}, bf16[3,64,1024]{2,1,0:T(8,128)(2,1)S(1)}, bf16[3,64,1024]{2,1,0:T(8,128)(2,1)S(1)}, bf16[8,32,128]{2,1,0:T(8,128)(2,1)S(1)}) custom-call(f32[32]{0:T(128)S(1)} %get-tuple-element.164.scale_ref, bf16[3,64,1024]{2,1,0:T(8,128)(2,1)S(1)} %copy-done.2, ...), custom_call_target="tpu_custom_call" | custom-call | flops 8000000000 | bytes 10000000 | tf_op jit(solution)/shard_map/backward/pallas_call | solution.py:428
  51.9 2.6 %outer_terms.1 = (f32[128,2048]{1,0:T(8,128)S(1)}, bf16[128,2048]{1,0:T(8,128)(2,1)S(1)}, bf16[128,2048]{1,0:T(8,128)(2,1)}, bf16[128,2048]{1,0:T(8,128)(2,1)S(1)}) custom-call(s32[4]{0:T(128)S(1)} %pad_add_fusion.place_ref, bf16[1024,256]{1,0:T(8,128)(2,1)S(1)} %get-tuple-element.92.own_ref, bf16[1024,256]{1,0:T(8,128)(2,1)S(1)} %collective-permute-done.6.other_ref, ...), custom_call_target="tpu_custom_call" | custom-call | flops 1100000000 | bytes 6000000 | tf_op jit(solution)/shard_map/outer_terms/pallas_call | solution.py:468
  54.6 3.2 %collective-permute-start.9 = (bf16[128,2048]{1,0:T(8,128)(2,1)S(1)}, bf16[128,2048]{1,0:T(8,128)(2,1)S(1)}, u32[]{:S(2)}, u32[]{:S(2)}) collective-permute-start(bf16[128,2048]{1,0:T(8,128)(2,1)S(1)} %get-tuple-element.115), channel_id=1, source_target_pairs={{0,192},{1,193},{2,194},{3,195},{4,196},{5,197},{6,198},{7,199},{8... | collective-permute-start | bytes 1572872 | tf_op jit(solution)/shard_map/ppermute | solution.py:50
  57.8 1.0 copy-done.4
  58.8 7.0 %backward.3 = (bf16[3,64,1024]{2,1,0:T(8,128)(2,1)S(1)}, bf16[3,64,1024]{2,1,0:T(8,128)(2,1)S(1)}, bf16[3,64,1024]{2,1,0:T(8,128)(2,1)S(1)}, bf16[3,64,1024]{2,1,0:T(8,128)(2,1)S(1)}, bf16[8,32,128]{2,1,0:T(8,128)(2,1)S(1)}) custom-call(f32[32]{0:T(128)S(1)} %get-tuple-element.164.scale_ref, ...), custom_call_target="tpu_custom_call", output_to_operand_aliasing={{0}: (7, {}), {1}: (8, {}), {2}: (9, {}), {3}: (10, {}), {4... | custom-call | flops 8000000000 | bytes 10000000 | tf_op jit(solution)/shard_map/backward/pallas_call | solution.py:428
  65.8 0.7 copy-done
  66.6 0.7 copy-done.9
  67.3 0.7 copy-done.10
  68.1 0.7 copy-done.11
  68.8 0.8 collective-permute-done.8.refs_1_
  69.6 16.6 %all_to_all.15 = bf16[8,32,128]{2,1,0:T(8,128)(2,1)S(1)} all-to-all(bf16[8,32,128]{2,1,0:T(8,128)(2,1)S(1)} %get-tuple-element.127), channel_id=1, replica_groups={{0,4,8,12,16,20,24,28},{1,5,9,13,17,21,25,29},{2,6,10,14,18,22,26,30},{..., dimensions={0} | all-to-all | bytes 131072 | tf_op jit(solution)/shard_map/all_to_all | solution.py:536
  86.3 0.7 broadcast_in_dim.3
  87.0 7.3 %all-to-all-start.1 = ((bf16[32,32,128]{2,1,0:T(8,128)(2,1)}), bf16[32,32,128]{2,1,0:T(8,128)(2,1)}, u32[]{:S(2)}, u32[]{:S(2)}) async-start(bf16[32,32,128]{2,1,0:T(8,128)(2,1)} %broadcast_in_dim.3), calls=%async_computation.1 | async-start | bytes 524288 | tf_op jit(solution)/shard_map/all_to_all | solution.py:550
  94.3 3.1 %collective-permute-start.10 = (bf16[128,2048]{1,0:T(8,128)(2,1)}, bf16[128,2048]{1,0:T(8,128)(2,1)S(1)}, u32[]{:S(2)}, u32[]{:S(2)}) collective-permute-start(bf16[128,2048]{1,0:T(8,128)(2,1)} %get-tuple-element.123), channel_id=1, source_target_pairs={{0,128},{1,129},{2,130},{3,131},{4,132},{5,133},{6,134},{7,135},{8... | collective-permute-start | bytes 1572872 | tf_op jit(solution)/shard_map/ppermute | solution.py:50
  97.4 0.4 collective-permute-start.11
  97.7 1.2 collective-permute-start.12
  98.9 3.1 %all-to-all-done.1 = bf16[32,32,128]{2,1,0:T(8,128)(2,1)} async-done(((bf16[32,32,128]{2,1,0:T(8,128)(2,1)}), bf16[32,32,128]{2,1,0:T(8,128)(2,1)}, u32[]{:S(2)}, u32[]{:S(2)}) %all-to-all-start.1) | async-done | bytes 262176 | tf_op jit(solution)/shard_map/all_to_all | solution.py:550
  102.1 1.0 convert_reduce_fusion
  103.1 19.1 %collective-permute-done.11.tl_ref = bf16[3,64,1024]{2,1,0:T(8,128)(2,1)S(1)} collective-permute-done((bf16[3,64,1024]{2,1,0:T(8,128)(2,1)}, bf16[3,64,1024]{2,1,0:T(8,128)(2,1)S(1)}, u32[]{:S(2)}, u32[]{:S(2)}) %collective-permute-start.11) | collective-permute-done | bytes 393248 | tf_op jit(solution)/shard_map/ppermute | solution.py:60
  122.2 4.2 %collective-permute-done.12.tr_ref = bf16[3,64,1024]{2,1,0:T(8,128)(2,1)S(1)} collective-permute-done((bf16[3,64,1024]{2,1,0:T(8,128)(2,1)}, bf16[3,64,1024]{2,1,0:T(8,128)(2,1)S(1)}, u32[]{:S(2)}, u32[]{:S(2)}) %collective-permute-start.12) | collective-permute-done | bytes 393248 | tf_op jit(solution)/shard_map/ppermute | solution.py:60
  126.5 0.8 sum_for_y.1
  127.3 4.3 %collective-permute-start.14 = (bf16[32,2048]{1,0:T(8,128)(2,1)S(1)}, bf16[32,2048]{1,0:T(8,128)(2,1)S(1)}, u32[]{:S(2)}, u32[]{:S(2)}) collective-permute-start(bf16[32,2048]{1,0:T(8,128)(2,1)S(1)} %get-tuple-element.140), channel_id=1, source_target_pairs={{0,32},{1,33},{2,34},{3,35},{4,36},{5,37},{6,38},{7,39},{8,40},{9,... | collective-permute-start | bytes 393224 | tf_op jit(solution)/shard_map/ppermute | solution.py:50
  131.6 2.1 %collective-permute-start.15 = (bf16[32,2048]{1,0:T(8,128)(2,1)S(1)}, bf16[32,2048]{1,0:T(8,128)(2,1)S(1)}, u32[]{:S(2)}, u32[]{:S(2)}) collective-permute-start(bf16[32,2048]{1,0:T(8,128)(2,1)S(1)} %get-tuple-element.141), channel_id=1, source_target_pairs={{0,2},{1,3},{2,0},{3,1},{4,6},{5,7},{6,4},{7,5},{8,10},{9,11},{10,... | collective-permute-start | bytes 393224 | tf_op jit(solution)/shard_map/ppermute | solution.py:50
  133.7 3.8 %collective-permute-done.14.refs_1_ = bf16[32,2048]{1,0:T(8,128)(2,1)S(1)} collective-permute-done((bf16[32,2048]{1,0:T(8,128)(2,1)S(1)}, bf16[32,2048]{1,0:T(8,128)(2,1)S(1)}, u32[]{:S(2)}, u32[]{:S(2)}) %collective-permute-start.14) | collective-permute-done | bytes 131104 | tf_op jit(solution)/shard_map/ppermute | solution.py:50
  137.5 2.0 %collective-permute-done.15.refs_2_ = bf16[32,2048]{1,0:T(8,128)(2,1)S(1)} collective-permute-done((bf16[32,2048]{1,0:T(8,128)(2,1)S(1)}, bf16[32,2048]{1,0:T(8,128)(2,1)S(1)}, u32[]{:S(2)}, u32[]{:S(2)}) %collective-permute-start.15) | collective-permute-done | bytes 131104 | tf_op jit(solution)/shard_map/ppermute | solution.py:50
  139.5 1.4 collective-permute-done.16.refs_3_
  140.8 0.8 sum_for_z.1
  141.6 3.4 %all-to-all-start.2 = ((bf16[8,4,3072]{2,1,0:T(4,128)(2,1)}), bf16[8,4,3072]{2,1,0:T(4,128)(2,1)S(1)}, u32[]{:S(2)}, u32[]{:S(2)}) async-start(bf16[8,4,3072]{2,1,0:T(4,128)(2,1)} %sum_for_z.1), calls=%async_computation.2 | async-start | bytes 393216 | tf_op jit(solution)/shard_map/all_to_all | solution.py:536
  145.0 1.0 copy-done.1
  146.0 3.4 %join_maps.1 = (bf16[16,16,1024]{2,1,0:T(8,128)(2,1)}, bf16[16,16,1024]{2,1,0:T(8,128)(2,1)}, bf16[16,16,1024]{2,1,0:T(8,128)(2,1)}) custom-call(bf16[3,64,1024]{2,1,0:T(8,128)(2,1)S(1)} %collective-permute-done.11.tl_ref, bf16[3,64,1024]{2,1,0:T(8,128)(2,1)S(1)} %collective-permute-done.12.tr_ref, bf16[3,64,1024]{2,1,0:T(8,128)(2,1)} %collective-permute-done.13.bl_ref, ...), custom_call_target="tpu_custom_call" | custom-call | tf_op jit(solution)/shard_map/join_maps/pallas_call | solution.py:147
  149.4 5.6 %all-to-all-done.2.found_ref = bf16[8,4,3072]{2,1,0:T(4,128)(2,1)S(1)} async-done(((bf16[8,4,3072]{2,1,0:T(4,128)(2,1)}), bf16[8,4,3072]{2,1,0:T(4,128)(2,1)S(1)}, u32[]{:S(2)}, u32[]{:S(2)}) %all-to-all-start.2) | async-done | bytes 196640 | tf_op jit(solution)/shard_map/all_to_all | solution.py:536
  155.1 0.6 reshape.16
  155.7 0.7 totals.1
  156.4 1.1 copy.24
  (54 shorter events, 0.5 us)
Async XLA Ops:
  4.3 15.9 %collective-permute-start = (bf16[3,64,1024]{2,1,0:T(8,128)(2,1)}, bf16[3,64,1024]{2,1,0:T(8,128)(2,1)S(1)}, u32[]{:S(2)}, u32[]{:S(2)}) collective-permute-start(bf16[3,64,1024]{2,1,0:T(8,128)(2,1)} %get-tuple-element.77), channel_id=1, source_target_pairs={{0,224},{1,225},{2,226},{3,227},{4,228},{5,229},{6,230},{7,231},{8... | collective-permute-start | bytes 1179656 | tf_op jit(solution)/shard_map/ppermute | solution.py:60
  5.0 17.2 %collective-permute-start.1 = (bf16[3,64,1024]{2,1,0:T(8,128)(2,1)}, bf16[3,64,1024]{2,1,0:T(8,128)(2,1)S(1)}, u32[]{:S(2)}, u32[]{:S(2)}) collective-permute-start(bf16[3,64,1024]{2,1,0:T(8,128)(2,1)} %get-tuple-element.78), channel_id=1, source_target_pairs={{0,31},{1,0},{2,1},{3,2},{4,3},{5,4},{6,5},{7,6},{8,7},{9,8},{10,9... | collective-permute-start | bytes 1179656 | tf_op jit(solution)/shard_map/ppermute | solution.py:60
  5.0 18.5 %collective-permute-start.2 = (bf16[3,64,1024]{2,1,0:T(8,128)(2,1)}, bf16[3,64,1024]{2,1,0:T(8,128)(2,1)S(1)}, u32[]{:S(2)}, u32[]{:S(2)}) collective-permute-start(bf16[3,64,1024]{2,1,0:T(8,128)(2,1)} %get-tuple-element.79), channel_id=1, source_target_pairs={{0,255},{1,224},{2,225},{3,226},{4,227},{5,228},{6,229},{7,230},{8... | collective-permute-start | bytes 1179656 | tf_op jit(solution)/shard_map/ppermute | solution.py:60
  13.6 6.6 %copy-start.17 = (f32[32]{0:T(128)S(1)}, f32[32]{0:T(128)}, u32[]{:S(2)}) copy-start(f32[32]{0:T(128)} %param.13) | copy-start | bytes 388
  13.6 10.0 %copy-start.16 = (bf16[64,2048]{1,0:T(8,128)(2,1)S(1)}, bf16[64,2048]{1,0:T(8,128)(2,1)}, u32[]{:S(2)}) copy-start(bf16[64,2048]{1,0:T(8,128)(2,1)} %get-tuple-element.89) | copy-start | bytes 786436
  13.6 12.1 %copy-start.15 = (bf16[64,2048]{1,0:T(8,128)(2,1)S(1)}, bf16[64,2048]{1,0:T(8,128)(2,1)}, u32[]{:S(2)}) copy-start(bf16[64,2048]{1,0:T(8,128)(2,1)} %get-tuple-element.90) | copy-start | bytes 786436
  13.6 15.6 %copy-start.14 = (bf16[64,2048]{1,0:T(8,128)(2,1)S(1)}, bf16[64,2048]{1,0:T(8,128)(2,1)}, u32[]{:S(2)}) copy-start(bf16[64,2048]{1,0:T(8,128)(2,1)} %get-tuple-element.91) | copy-start | bytes 786436
  13.6 19.3 %copy-start.2 = (bf16[3,64,1024]{2,1,0:T(8,128)(2,1)S(1)}, bf16[3,64,1024]{2,1,0:T(8,128)(2,1)}, u32[]{:S(2)}) copy-start(bf16[3,64,1024]{2,1,0:T(8,128)(2,1)} %get-tuple-element.83.tl_ref) | copy-start | bytes 1179652
  20.2 24.6 %copy-start.3 = (bf16[3,64,1024]{2,1,0:T(8,128)(2,1)}, bf16[3,64,1024]{2,1,0:T(8,128)(2,1)S(1)}, u32[]{:S(2)}) copy-start(bf16[3,64,1024]{2,1,0:T(8,128)(2,1)S(1)} %collective-permute-done.bl_ref) | copy-start | bytes 1179652
  22.2 20.3 %copy-start.5 = (bf16[3,64,1024]{2,1,0:T(8,128)(2,1)}, bf16[3,64,1024]{2,1,0:T(8,128)(2,1)S(1)}, u32[]{:S(2)}) copy-start(bf16[3,64,1024]{2,1,0:T(8,128)(2,1)S(1)} %collective-permute-done.1.tr_ref) | copy-start | bytes 1179652
  23.5 19.0 %copy-start.7 = (bf16[3,64,1024]{2,1,0:T(8,128)(2,1)}, bf16[3,64,1024]{2,1,0:T(8,128)(2,1)S(1)}, u32[]{:S(2)}) copy-start(bf16[3,64,1024]{2,1,0:T(8,128)(2,1)S(1)} %collective-permute-done.2.br_ref) | copy-start | bytes 1179652
  23.6 19.0 %collective-permute-start.3 = (bf16[64,2048]{1,0:T(8,128)(2,1)S(1)}, bf16[64,2048]{1,0:T(8,128)(2,1)S(1)}, u32[]{:S(2)}, u32[]{:S(2)}) collective-permute-start(bf16[64,2048]{1,0:T(8,128)(2,1)S(1)} %copy-done.16), channel_id=1, source_target_pairs={{0,224},{1,225},{2,226},{3,227},{4,228},{5,229},{6,230},{7,231},{8... | collective-permute-start | bytes 786440 | tf_op jit(solution)/shard_map/ppermute | solution.py:60
  25.7 16.9 %collective-permute-start.4 = (bf16[64,2048]{1,0:T(8,128)(2,1)S(1)}, bf16[64,2048]{1,0:T(8,128)(2,1)S(1)}, u32[]{:S(2)}, u32[]{:S(2)}) collective-permute-start(bf16[64,2048]{1,0:T(8,128)(2,1)S(1)} %copy-done.15), channel_id=1, source_target_pairs={{0,31},{1,0},{2,1},{3,2},{4,3},{5,4},{6,5},{7,6},{8,7},{9,8},{10,9... | collective-permute-start | bytes 786440 | tf_op jit(solution)/shard_map/ppermute | solution.py:60
  29.2 13.3 %collective-permute-start.5 = (bf16[64,2048]{1,0:T(8,128)(2,1)S(1)}, bf16[64,2048]{1,0:T(8,128)(2,1)S(1)}, u32[]{:S(2)}, u32[]{:S(2)}) collective-permute-start(bf16[64,2048]{1,0:T(8,128)(2,1)S(1)} %copy-done.14), channel_id=1, source_target_pairs={{0,255},{1,224},{2,225},{3,226},{4,227},{5,228},{6,229},{7,230},{8... | collective-permute-start | bytes 786440 | tf_op jit(solution)/shard_map/ppermute | solution.py:60
  32.9 9.7 %copy-start.12 = (bf16[64,2048]{1,0:T(8,128)(2,1)S(1)}, bf16[64,2048]{1,0:T(8,128)(2,1)}, u32[]{:S(2)}) copy-start(bf16[64,2048]{1,0:T(8,128)(2,1)} %get-tuple-element.93) | copy-start | bytes 786436
  32.9 10.6 %copy-start.13 = (bf16[1024,2048]{1,0:T(8,128)(2,1)S(1)}, bf16[1024,2048]{1,0:T(8,128)(2,1)}, u32[]{:S(2)}) copy-start(bf16[1024,2048]{1,0:T(8,128)(2,1)} %param.15) | copy-start | bytes 12582916
  42.5 9.4 %collective-permute-start.6 = (bf16[1024,256]{1,0:T(8,128)(2,1)S(1)}, bf16[1024,256]{1,0:T(8,128)(2,1)S(1)}, u32[]{:S(2)}, u32[]{:S(2)}) collective-permute-start(bf16[1024,256]{1,0:T(8,128)(2,1)S(1)} %get-tuple-element.92.own_ref), channel_id=1, source_target_pairs={{0,1},{1,0},{2,3},{3,2},{4,5},{5,4},{6,7},{7,6},{8,9},{9,8},{10,11... | collective-permute-start | bytes 1572872 | tf_op jit(solution)/shard_map/ppermute | solution.py:50
  42.7 2.1 %copy-start.6 = (bf16[3,64,1024]{2,1,0:T(8,128)(2,1)S(1)}, bf16[3,64,1024]{2,1,0:T(8,128)(2,1)}, u32[]{:S(2)}) copy-start(bf16[3,64,1024]{2,1,0:T(8,128)(2,1)} %copy-done.5) | copy-start | bytes 1179652
  42.7 2.1 %copy-start.8 = (bf16[3,64,1024]{2,1,0:T(8,128)(2,1)S(1)}, bf16[3,64,1024]{2,1,0:T(8,128)(2,1)}, u32[]{:S(2)}) copy-start(bf16[3,64,1024]{2,1,0:T(8,128)(2,1)} %copy-done.7) | copy-start | bytes 1179652
  42.8 9.1 %collective-permute-start.7 = (bf16[256,2048]{1,0:T(8,128)(2,1)S(1)}, bf16[256,2048]{1,0:T(8,128)(2,1)S(1)}, u32[]{:S(2)}, u32[]{:S(2)}) collective-permute-start(bf16[256,2048]{1,0:T(8,128)(2,1)S(1)} %constant_dynamic-update-slice_fusion.drop_ref), channel_id=1, source_target_pairs={{0,1},{1,0},{2,3},{3,2},{4,5},{5,4},{6,7},{7,6},{8,9},{9,8},{10,11... | collective-permute-start | bytes 3145736 | tf_op jit(solution)/shard_map/ppermute | solution.py:50
  54.6 15.1 %collective-permute-start.8 = (bf16[128,2048]{1,0:T(8,128)(2,1)S(1)}, bf16[128,2048]{1,0:T(8,128)(2,1)S(1)}, u32[]{:S(2)}, u32[]{:S(2)}) collective-permute-start(bf16[128,2048]{1,0:T(8,128)(2,1)S(1)} %get-tuple-element.114), channel_id=1, source_target_pairs={{0,64},{1,65},{2,66},{3,67},{4,68},{5,69},{6,70},{7,71},{8,72},{9,... | collective-permute-start | bytes 1572872 | tf_op jit(solution)/shard_map/ppermute | solution.py:50
  54.6 15.1 %collective-permute-start.9 = (bf16[128,2048]{1,0:T(8,128)(2,1)S(1)}, bf16[128,2048]{1,0:T(8,128)(2,1)S(1)}, u32[]{:S(2)}, u32[]{:S(2)}) collective-permute-start(bf16[128,2048]{1,0:T(8,128)(2,1)S(1)} %get-tuple-element.115), channel_id=1, source_target_pairs={{0,192},{1,193},{2,194},{3,195},{4,196},{5,197},{6,198},{7,199},{8... | collective-permute-start | bytes 1572872 | tf_op jit(solution)/shard_map/ppermute | solution.py:50
  57.8 1.0 copy-start.4
  65.8 0.8 copy-start
  66.6 0.7 copy-start.9
  67.3 0.7 copy-start.10
  68.1 0.7 copy-start.11
  87.0 15.1 %all-to-all-start.1 = ((bf16[32,32,128]{2,1,0:T(8,128)(2,1)}), bf16[32,32,128]{2,1,0:T(8,128)(2,1)}, u32[]{:S(2)}, u32[]{:S(2)}) async-start(bf16[32,32,128]{2,1,0:T(8,128)(2,1)} %broadcast_in_dim.3), calls=%async_computation.1 | async-start | bytes 524288 | tf_op jit(solution)/shard_map/all_to_all | solution.py:550
  94.3 32.2 %collective-permute-start.10 = (bf16[128,2048]{1,0:T(8,128)(2,1)}, bf16[128,2048]{1,0:T(8,128)(2,1)S(1)}, u32[]{:S(2)}, u32[]{:S(2)}) collective-permute-start(bf16[128,2048]{1,0:T(8,128)(2,1)} %get-tuple-element.123), channel_id=1, source_target_pairs={{0,128},{1,129},{2,130},{3,131},{4,132},{5,133},{6,134},{7,135},{8... | collective-permute-start | bytes 1572872 | tf_op jit(solution)/shard_map/ppermute | solution.py:50
  97.4 24.9 %collective-permute-start.11 = (bf16[3,64,1024]{2,1,0:T(8,128)(2,1)}, bf16[3,64,1024]{2,1,0:T(8,128)(2,1)S(1)}, u32[]{:S(2)}, u32[]{:S(2)}) collective-permute-start(bf16[3,64,1024]{2,1,0:T(8,128)(2,1)} %copy-done.11), channel_id=1, source_target_pairs={{0,33},{1,34},{2,35},{3,36},{4,37},{5,38},{6,39},{7,40},{8,41},{9,... | collective-permute-start | bytes 1179656 | tf_op jit(solution)/shard_map/ppermute | solution.py:60
  97.7 28.7 %collective-permute-start.12 = (bf16[3,64,1024]{2,1,0:T(8,128)(2,1)}, bf16[3,64,1024]{2,1,0:T(8,128)(2,1)S(1)}, u32[]{:S(2)}, u32[]{:S(2)}) collective-permute-start(bf16[3,64,1024]{2,1,0:T(8,128)(2,1)} %copy-done.9), channel_id=1, source_target_pairs={{0,32},{1,33},{2,34},{3,35},{4,36},{5,37},{6,38},{7,39},{8,40},{9,... | collective-permute-start | bytes 1179656 | tf_op jit(solution)/shard_map/ppermute | solution.py:60
  98.9 27.5 %collective-permute-start.13 = (bf16[3,64,1024]{2,1,0:T(8,128)(2,1)}, bf16[3,64,1024]{2,1,0:T(8,128)(2,1)}, u32[]{:S(2)}, u32[]{:S(2)}) collective-permute-start(bf16[3,64,1024]{2,1,0:T(8,128)(2,1)} %copy-done.10), channel_id=1, source_target_pairs={{0,1},{1,2},{2,3},{3,4},{4,5},{5,6},{6,7},{7,8},{8,9},{9,10},{10,1... | collective-permute-start | bytes 1179656 | tf_op jit(solution)/shard_map/ppermute | solution.py:60
  127.3 10.2 %collective-permute-start.14 = (bf16[32,2048]{1,0:T(8,128)(2,1)S(1)}, bf16[32,2048]{1,0:T(8,128)(2,1)S(1)}, u32[]{:S(2)}, u32[]{:S(2)}) collective-permute-start(bf16[32,2048]{1,0:T(8,128)(2,1)S(1)} %get-tuple-element.140), channel_id=1, source_target_pairs={{0,32},{1,33},{2,34},{3,35},{4,36},{5,37},{6,38},{7,39},{8,40},{9,... | collective-permute-start | bytes 393224 | tf_op jit(solution)/shard_map/ppermute | solution.py:50
  131.6 7.9 %collective-permute-start.15 = (bf16[32,2048]{1,0:T(8,128)(2,1)S(1)}, bf16[32,2048]{1,0:T(8,128)(2,1)S(1)}, u32[]{:S(2)}, u32[]{:S(2)}) collective-permute-start(bf16[32,2048]{1,0:T(8,128)(2,1)S(1)} %get-tuple-element.141), channel_id=1, source_target_pairs={{0,2},{1,3},{2,0},{3,1},{4,6},{5,7},{6,4},{7,5},{8,10},{9,11},{10,... | collective-permute-start | bytes 393224 | tf_op jit(solution)/shard_map/ppermute | solution.py:50
  133.7 7.2 %collective-permute-start.16 = (bf16[32,2048]{1,0:T(8,128)(2,1)S(1)}, bf16[32,2048]{1,0:T(8,128)(2,1)S(1)}, u32[]{:S(2)}, u32[]{:S(2)}) collective-permute-start(bf16[32,2048]{1,0:T(8,128)(2,1)S(1)} %get-tuple-element.142), channel_id=1, source_target_pairs={{0,34},{1,35},{2,32},{3,33},{4,38},{5,39},{6,36},{7,37},{8,42},{9,... | collective-permute-start | bytes 393224 | tf_op jit(solution)/shard_map/ppermute | solution.py:50
  141.6 13.4 %all-to-all-start.2 = ((bf16[8,4,3072]{2,1,0:T(4,128)(2,1)}), bf16[8,4,3072]{2,1,0:T(4,128)(2,1)S(1)}, u32[]{:S(2)}, u32[]{:S(2)}) async-start(bf16[8,4,3072]{2,1,0:T(4,128)(2,1)} %sum_for_z.1), calls=%async_computation.2 | async-start | bytes 393216 | tf_op jit(solution)/shard_map/all_to_all | solution.py:536
  145.0 1.0 copy-start.1

commit v5 on v4

--- a/solution.py
+++ b/solution.py
@@ -615,9 +615,11 @@
     near = [move(terms[s], along_x(s)) for s in (1, 3)]
     near, across, table_part = lax.optimization_barrier((near, terms[2], table_part))
     across = move(across, along_x(2))
-    piece = table_plane(table_pieces(table_part))
-    across, arrived, piece = lax.optimization_barrier((across, arrived, piece))
+    piece = table_pieces(table_part)
+    across, arrived = lax.optimization_barrier((across, arrived))
     terms = sum_for_y(place, (terms[0], near[0], across, near[1]))
+    terms, piece = lax.optimization_barrier((terms, piece))
+    piece = table_plane(piece)
     grads = join_maps(*arrived, g_tl)
     weight_grad, table_grad, log_grad = totals(terms, piece)
     return (*grads, weight_grad, table_grad, log_grad)

time: 158 us -> 145 us (0.918)
  waiting for transfers between devices: 43.4 us -> 33.1 us
  local copies, waits for them, and re-layouts: 8.93 us -> 3.95 us
  starting transfers between devices: 39.3 us -> 44.2 us
  Pallas kernels: 45.9 us -> 43.7 us
    ppermute x9, waiting for transfers between devices: 26.7 us -> 11.1 us  [move_map(): return lax.ppermute(value, ('row', 'col'), pairs)]
    unnamed x41 -> x19, local copies, waits for them, and re-layouts: 7.49 us -> 2.5 us
    all_to_all x1, starting transfers between devices: 3.39 us -> 7.73 us  [along_z_exchange(): lax.all_to_all(value, 'col', 0, 0, axis_index_groups=groups, tiled=True)]
    ppermute x8, starting transfers between devices: 13.6 us -> 9.64 us  [move(): return lax.ppermute(value, ('row', 'col'), pairs)]
    ppermute x9, starting transfers between devices: 15 us -> 18.3 us  [move_map(): return lax.ppermute(value, ('row', 'col'), pairs)]
    all_to_all x1, waiting for transfers between devices: 5.57 us -> 8.58 us  [along_z_exchange(): lax.all_to_all(value, 'col', 0, 0, axis_index_groups=groups, tiled=True)]
  transfers between devices with their start and end apart: 19 -> 19, of which waited for: 10 -> 10; matrix products, arithmetic and copies ran while one was open for 2% -> 2% of each run, Pallas kernels for 24% -> 25%
where the time goes in v5:
time: 145 us; the launch traced here: 143 us
  starting transfers between devices  44.2 us (30%)
  Pallas kernels  43.7 us (30%)
  waiting for transfers between devices  33.1 us (23%)
  blocking collectives  15.6 us (11%)
  local copies, waits for them, and re-layouts  3.95 us (3%)
    ppermute x9, starting transfers between devices, move_map(): return lax.ppermute(value, ('row', 'col'), pairs)  18.3 us
    all_to_all x1, blocking collectives, along_z_exchange(): lax.all_to_all(value, 'col', 0, 0, axis_index_groups=groups, tiled=True)  15.6 us
    pallas_call x2, Pallas kernels, backward(): pl.pallas_call(functools.partial(backward_kernel, first), grid=(steps,),...  14.1 us
    ppermute x9, waiting for transfers between devices, move_map(): return lax.ppermute(value, ('row', 'col'), pairs)  11.1 us
    ppermute x8, starting transfers between devices, move(): return lax.ppermute(value, ('row', 'col'), pairs)  9.64 us
    pallas_call x1, Pallas kernels, forward(): pl.pallas_call(forward_kernel, grid=(INNER // TILE // GROUP,), in_specs=[...  9.58 us
    ppermute x8, waiting for transfers between devices, move(): return lax.ppermute(value, ('row', 'col'), pairs)  8.89 us
    all_to_all x1, waiting for transfers between devices, along_z_exchange(): lax.all_to_all(value, 'col', 0, 0, axis_index_groups=groups, tiled=True)  8.58 us
  transfers between devices with their start and end apart: 19, of which 10 were waited for; matrix products, arithmetic and copies ran while one was open for 2% of the time, Pallas kernels for 25%

profile of v5, /device:TPU:24, one launch (start us, length us, event | category | flops | bytes accessed | tf_op | source)
XLA Modules:
  0.0 142.9 jit_solution(7316830951456153037)
XLA Ops:
  0.6 3.6 %split_maps.1 = (bf16[3,64,1024]{2,1,0:T(8,128)(2,1)}, bf16[3,64,1024]{2,1,0:T(8,128)(2,1)}, bf16[3,64,1024]{2,1,0:T(8,128)(2,1)}, bf16[3,64,1024]{2,1,0:T(8,128)(2,1)}) custom-call(bf16[16,16,1024]{2,1,0:T(8,128)(2,1)} %q_ref.1, bf16[16,16,1024]{2,1,0:T(8,128)(2,1)} %k_ref.1, bf16[16,16,1024]{2,1,0:T(8,128)(2,1)} %v_ref.1), custom_call_target="tpu_custom_call" | custom-call | tf_op jit(solution)/shard_map/split_maps/pallas_call | solution.py:106
  4.3 0.8 collective-permute-start
  5.0 0.0 collective-permute-start.1
  5.0 3.3 %collective-permute-start.2 = (bf16[3,64,1024]{2,1,0:T(8,128)(2,1)}, bf16[3,64,1024]{2,1,0:T(8,128)(2,1)S(1)}, u32[]{:S(2)}, u32[]{:S(2)}) collective-permute-start(bf16[3,64,1024]{2,1,0:T(8,128)(2,1)} %get-tuple-element.83), channel_id=1, source_target_pairs={{0,255},{1,224},{2,225},{3,226},{4,227},{5,228},{6,229},{7,230},{8... | collective-permute-start | bytes 1179656 | tf_op jit(solution)/shard_map/ppermute | solution.py:60
  8.4 1.3 copy.23.table_ref
  9.7 3.8 %split_dropped.1 = (bf16[64,2048]{1,0:T(8,128)(2,1)}, bf16[64,2048]{1,0:T(8,128)(2,1)}, bf16[64,2048]{1,0:T(8,128)(2,1)}, bf16[64,2048]{1,0:T(8,128)(2,1)}) custom-call(bf16[16,16,2048]{2,1,0:T(8,128)(2,1)} %grad_ref.1, s32[16,16,2048]{2,1,0:T(8,128)} %keep_ref.1), custom_call_target="tpu_custom_call" | custom-call | tf_op jit(solution)/shard_map/split_dropped/pallas_call | solution.py:126
  13.6 0.0 copy-start
  13.6 6.5 %bias_blocks.1.bias_ref = f32[32,3,128,128]{3,2,1,0:T(8,128)} custom-call(f32[32,31,31]{2,1,0:T(8,128)S(1)} %copy.23.table_ref), custom_call_target="tpu_custom_call" | custom-call | flops 10000000 | bytes 8000000 | tf_op jit(solution)/shard_map/bias_blocks/pallas_call | solution.py:180
  20.1 0.1 pad_add_fusion.place_ref
  20.2 0.0 collective-permute-done.bl_ref
  20.2 2.0 %collective-permute-done.1.tr_ref = bf16[3,64,1024]{2,1,0:T(8,128)(2,1)S(1)} collective-permute-done((bf16[3,64,1024]{2,1,0:T(8,128)(2,1)}, bf16[3,64,1024]{2,1,0:T(8,128)(2,1)S(1)}, u32[]{:S(2)}, u32[]{:S(2)}) %collective-permute-start.1) | collective-permute-done | bytes 393248 | tf_op jit(solution)/shard_map/ppermute | solution.py:60
  22.2 1.4 collective-permute-done.2.br_ref
  23.6 2.1 %collective-permute-start.3 = (bf16[64,2048]{1,0:T(8,128)(2,1)S(1)}, bf16[64,2048]{1,0:T(8,128)(2,1)S(1)}, u32[]{:S(2)}, u32[]{:S(2)}) collective-permute-start(bf16[64,2048]{1,0:T(8,128)(2,1)S(1)} %copy-done.5), channel_id=1, source_target_pairs={{0,224},{1,225},{2,226},{3,227},{4,228},{5,229},{6,230},{7,231},{8... | collective-permute-start | bytes 786440 | tf_op jit(solution)/shard_map/ppermute | solution.py:60
  25.7 3.6 %collective-permute-start.4 = (bf16[64,2048]{1,0:T(8,128)(2,1)S(1)}, bf16[64,2048]{1,0:T(8,128)(2,1)S(1)}, u32[]{:S(2)}, u32[]{:S(2)}) collective-permute-start(bf16[64,2048]{1,0:T(8,128)(2,1)S(1)} %copy-done.4), channel_id=1, source_target_pairs={{0,31},{1,0},{2,1},{3,2},{4,3},{5,4},{6,5},{7,6},{8,7},{9,8},{10,9... | collective-permute-start | bytes 786440 | tf_op jit(solution)/shard_map/ppermute | solution.py:60
  29.2 3.7 %collective-permute-start.5 = (bf16[64,2048]{1,0:T(8,128)(2,1)S(1)}, bf16[64,2048]{1,0:T(8,128)(2,1)S(1)}, u32[]{:S(2)}, u32[]{:S(2)}) collective-permute-start(bf16[64,2048]{1,0:T(8,128)(2,1)S(1)} %copy-done.3), channel_id=1, source_target_pairs={{0,255},{1,224},{2,225},{3,226},{4,227},{5,228},{6,229},{7,230},{8... | collective-permute-start | bytes 786440 | tf_op jit(solution)/shard_map/ppermute | solution.py:60
  32.9 9.6 %forward.1 = (bf16[1024,256]{1,0:T(8,128)(2,1)S(1)}, f32[32,256,256]{2,1,0:T(8,128)}) custom-call(f32[32]{0:T(128)S(1)} %get-tuple-element.173.scale_ref, bf16[3,64,1024]{2,1,0:T(8,128)(2,1)S(1)} %copy-done, bf16[3,64,1024]{2,1,0:T(8,128)(2,1)S(1)} %collective-permute-done.bl_ref, bf16[3,64,1024]{2,1,0:T(8,128)(2,1)S(1)} %collective-permute-done.1.tr_ref, ...), custom_call_target="tpu_custom_call" | custom-call | flops 8000000000 | bytes 16000000 | tf_op jit(solution)/shard_map/forward/pallas_call | solution.py:277
  42.5 0.1 collective-permute-start.6
  42.7 0.8 collective-permute-start.7
  43.5 1.3 convolution_convert_fusion.grad_ref
  44.8 7.0 %backward.2 = (bf16[3,64,1024]{2,1,0:T(8,128)(2,1)S(1)}, bf16[3,64,1024]{2,1,0:T(8,128)(2,1)S(1)}, bf16[3,64,1024]{2,1,0:T(8,128)(2,1)S(1)}, bf16[3,64,1024]{2,1,0:T(8,128)(2,1)S(1)}, bf16[8,32,128]{2,1,0:T(8,128)(2,1)S(1)}) custom-call(f32[32]{0:T(128)S(1)} %get-tuple-element.172.scale_ref, bf16[3,64,1024]{2,1,0:T(8,128)(2,1)S(1)} %copy-done, ...), custom_call_target="tpu_custom_call" | custom-call | flops 8000000000 | bytes 10000000 | tf_op jit(solution)/shard_map/backward/pallas_call | solution.py:428
  51.9 2.1 %outer_terms.1 = (f32[128,2048]{1,0:T(8,128)S(1)}, bf16[128,2048]{1,0:T(8,128)(2,1)S(1)}, bf16[128,2048]{1,0:T(8,128)(2,1)S(1)}, bf16[128,2048]{1,0:T(8,128)(2,1)S(1)}) custom-call(s32[4]{0:T(128)S(1)} %pad_add_fusion.place_ref, bf16[1024,256]{1,0:T(8,128)(2,1)S(1)} %get-tuple-element.96.own_ref, bf16[1024,256]{1,0:T(8,128)(2,1)S(1)} %collective-permute-done.6.other_ref, ...), custom_call_target="tpu_custom_call" | custom-call | flops 1100000000 | bytes 6000000 | tf_op jit(solution)/shard_map/outer_terms/pallas_call | solution.py:468
  54.0 0.1 collective-permute-start.8
  54.0 3.2 %collective-permute-start.9 = (bf16[128,2048]{1,0:T(8,128)(2,1)S(1)}, bf16[128,2048]{1,0:T(8,128)(2,1)S(1)}, u32[]{:S(2)}, u32[]{:S(2)}) collective-permute-start(bf16[128,2048]{1,0:T(8,128)(2,1)S(1)} %get-tuple-element.119), channel_id=1, source_target_pairs={{0,192},{1,193},{2,194},{3,195},{4,196},{5,197},{6,198},{7,199},{8... | collective-permute-start | bytes 1572872 | tf_op jit(solution)/shard_map/ppermute | solution.py:50
  57.3 7.0 %backward.3 = (bf16[3,64,1024]{2,1,0:T(8,128)(2,1)S(1)}, bf16[3,64,1024]{2,1,0:T(8,128)(2,1)S(1)}, bf16[3,64,1024]{2,1,0:T(8,128)(2,1)S(1)}, bf16[3,64,1024]{2,1,0:T(8,128)(2,1)S(1)}, bf16[8,32,128]{2,1,0:T(8,128)(2,1)S(1)}) custom-call(f32[32]{0:T(128)S(1)} %get-tuple-element.172.scale_ref, ...), custom_call_target="tpu_custom_call", output_to_operand_aliasing={{0}: (7, {}), {1}: (8, {}), {2}: (9, {}), {3}: (10, {}), {4... | custom-call | flops 8000000000 | bytes 10000000 | tf_op jit(solution)/shard_map/backward/pallas_call | solution.py:428
  64.3 4.8 %collective-permute-done.8.refs_1_ = bf16[128,2048]{1,0:T(8,128)(2,1)S(1)} collective-permute-done((bf16[128,2048]{1,0:T(8,128)(2,1)S(1)}, bf16[128,2048]{1,0:T(8,128)(2,1)S(1)}, u32[]{:S(2)}, u32[]{:S(2)}) %collective-permute-start.8) | collective-permute-done | bytes 524320 | tf_op jit(solution)/shard_map/ppermute | solution.py:50
  69.1 2.5 %collective-permute-start.10 = (bf16[128,2048]{1,0:T(8,128)(2,1)S(1)}, bf16[128,2048]{1,0:T(8,128)(2,1)S(1)}, u32[]{:S(2)}, u32[]{:S(2)}) collective-permute-start(bf16[128,2048]{1,0:T(8,128)(2,1)S(1)} %get-tuple-element.127), channel_id=1, source_target_pairs={{0,128},{1,129},{2,130},{3,131},{4,132},{5,133},{6,134},{7,135},{8... | collective-permute-start | bytes 1572872 | tf_op jit(solution)/shard_map/ppermute | solution.py:50
  71.6 1.0 collective-permute-start.12
  72.6 3.8 %collective-permute-start.13 = (bf16[3,64,1024]{2,1,0:T(8,128)(2,1)S(1)}, bf16[3,64,1024]{2,1,0:T(8,128)(2,1)S(1)}, u32[]{:S(2)}, u32[]{:S(2)}) collective-permute-start(bf16[3,64,1024]{2,1,0:T(8,128)(2,1)S(1)} %get-tuple-element.130), channel_id=1, source_target_pairs={{0,1},{1,2},{2,3},{3,4},{4,5},{5,6},{6,7},{7,8},{8,9},{9,10},{10,1... | collective-permute-start | bytes 1179656 | tf_op jit(solution)/shard_map/ppermute | solution.py:60
  76.4 15.6 %all_to_all.15 = bf16[8,32,128]{2,1,0:T(8,128)(2,1)S(1)} all-to-all(bf16[8,32,128]{2,1,0:T(8,128)(2,1)S(1)} %get-tuple-element.146), channel_id=1, replica_groups={{0,4,8,12,16,20,24,28},{1,5,9,13,17,21,25,29},{2,6,10,14,18,22,26,30},{..., dimensions={0} | all-to-all | bytes 131072 | tf_op jit(solution)/shard_map/all_to_all | solution.py:536
  92.0 3.5 %collective-permute-done.11.tl_ref = bf16[3,64,1024]{2,1,0:T(8,128)(2,1)S(1)} collective-permute-done((bf16[3,64,1024]{2,1,0:T(8,128)(2,1)S(1)}, bf16[3,64,1024]{2,1,0:T(8,128)(2,1)S(1)}, u32[]{:S(2)}, u32[]{:S(2)}) %collective-permute-start.11) | collective-permute-done | bytes 393248 | tf_op jit(solution)/shard_map/ppermute | solution.py:60
  95.4 4.2 %collective-permute-done.12.tr_ref = bf16[3,64,1024]{2,1,0:T(8,128)(2,1)S(1)} collective-permute-done((bf16[3,64,1024]{2,1,0:T(8,128)(2,1)S(1)}, bf16[3,64,1024]{2,1,0:T(8,128)(2,1)S(1)}, u32[]{:S(2)}, u32[]{:S(2)}) %collective-permute-start.12) | collective-permute-done | bytes 393248 | tf_op jit(solution)/shard_map/ppermute | solution.py:60
  99.7 0.8 sum_for_y.1
  100.4 0.7 broadcast_in_dim.3
  101.2 8.5 %all-to-all-start.1 = ((bf16[32,32,128]{2,1,0:T(8,128)(2,1)}), bf16[32,32,128]{2,1,0:T(8,128)(2,1)S(1)}, u32[]{:S(2)}, u32[]{:S(2)}) async-start(bf16[32,32,128]{2,1,0:T(8,128)(2,1)} %broadcast_in_dim.3), calls=%async_computation.1 | async-start | bytes 524288 | tf_op jit(solution)/shard_map/all_to_all | solution.py:550
  109.7 0.3 collective-permute-start.14
  110.0 2.7 %collective-permute-start.15 = (bf16[32,2048]{1,0:T(8,128)(2,1)S(1)}, bf16[32,2048]{1,0:T(8,128)(2,1)S(1)}, u32[]{:S(2)}, u32[]{:S(2)}) collective-permute-start(bf16[32,2048]{1,0:T(8,128)(2,1)S(1)} %get-tuple-element.149), channel_id=1, source_target_pairs={{0,2},{1,3},{2,0},{3,1},{4,6},{5,7},{6,4},{7,5},{8,10},{9,11},{10,... | collective-permute-start | bytes 393224 | tf_op jit(solution)/shard_map/ppermute | solution.py:50
  112.7 4.6 %all-to-all-done.1 = bf16[32,32,128]{2,1,0:T(8,128)(2,1)S(1)} async-done(((bf16[32,32,128]{2,1,0:T(8,128)(2,1)}), bf16[32,32,128]{2,1,0:T(8,128)(2,1)S(1)}, u32[]{:S(2)}, u32[]{:S(2)}) %all-to-all-start.1) | async-done | bytes 262176 | tf_op jit(solution)/shard_map/all_to_all | solution.py:550
  117.4 0.6 collective-permute-done.14.refs_1_
  118.0 1.3 collective-permute-done.15.refs_2_
  119.3 2.1 %collective-permute-done.16.refs_3_ = bf16[32,2048]{1,0:T(8,128)(2,1)S(1)} collective-permute-done((bf16[32,2048]{1,0:T(8,128)(2,1)S(1)}, bf16[32,2048]{1,0:T(8,128)(2,1)S(1)}, u32[]{:S(2)}, u32[]{:S(2)}) %collective-permute-start.16) | collective-permute-done | bytes 131104 | tf_op jit(solution)/shard_map/ppermute | solution.py:50
  121.4 0.8 sum_for_z.1
  122.2 7.7 %all-to-all-start.2 = ((bf16[8,4,3072]{2,1,0:T(4,128)(2,1)}), bf16[8,4,3072]{2,1,0:T(4,128)(2,1)S(1)}, u32[]{:S(2)}, u32[]{:S(2)}) async-start(bf16[8,4,3072]{2,1,0:T(4,128)(2,1)} %sum_for_z.1), calls=%async_computation.2 | async-start | bytes 393216 | tf_op jit(solution)/shard_map/all_to_all | solution.py:536
  129.9 1.9 %join_maps.1 = (bf16[16,16,1024]{2,1,0:T(8,128)(2,1)}, bf16[16,16,1024]{2,1,0:T(8,128)(2,1)}, bf16[16,16,1024]{2,1,0:T(8,128)(2,1)}) custom-call(bf16[3,64,1024]{2,1,0:T(8,128)(2,1)S(1)} %collective-permute-done.11.tl_ref, bf16[3,64,1024]{2,1,0:T(8,128)(2,1)S(1)} %collective-permute-done.12.tr_ref, bf16[3,64,1024]{2,1,0:T(8,128)(2,1)S(1)} %collective-permute-done.13.bl_ref, ...), custom_call_target="tpu_custom_call" | custom-call | tf_op jit(solution)/shard_map/join_maps/pallas_call | solution.py:147
  131.8 8.6 %all-to-all-done.2.found_ref = bf16[8,4,3072]{2,1,0:T(4,128)(2,1)S(1)} async-done(((bf16[8,4,3072]{2,1,0:T(4,128)(2,1)}), bf16[8,4,3072]{2,1,0:T(4,128)(2,1)S(1)}, u32[]{:S(2)}, u32[]{:S(2)}) %all-to-all-start.2) | async-done | bytes 196640 | tf_op jit(solution)/shard_map/all_to_all | solution.py:536
  140.4 0.1 slice.3
  140.5 0.6 reshape.16
  141.1 0.7 totals.1
  141.8 1.1 copy.24
  (32 shorter events, 0.2 us)
Async XLA Ops:
  4.3 15.9 %collective-permute-start = (bf16[3,64,1024]{2,1,0:T(8,128)(2,1)}, bf16[3,64,1024]{2,1,0:T(8,128)(2,1)S(1)}, u32[]{:S(2)}, u32[]{:S(2)}) collective-permute-start(bf16[3,64,1024]{2,1,0:T(8,128)(2,1)} %get-tuple-element.81), channel_id=1, source_target_pairs={{0,224},{1,225},{2,226},{3,227},{4,228},{5,229},{6,230},{7,231},{8... | collective-permute-start | bytes 1179656 | tf_op jit(solution)/shard_map/ppermute | solution.py:60
  5.0 17.2 %collective-permute-start.1 = (bf16[3,64,1024]{2,1,0:T(8,128)(2,1)}, bf16[3,64,1024]{2,1,0:T(8,128)(2,1)S(1)}, u32[]{:S(2)}, u32[]{:S(2)}) collective-permute-start(bf16[3,64,1024]{2,1,0:T(8,128)(2,1)} %get-tuple-element.82), channel_id=1, source_target_pairs={{0,31},{1,0},{2,1},{3,2},{4,3},{5,4},{6,5},{7,6},{8,7},{9,8},{10,9... | collective-permute-start | bytes 1179656 | tf_op jit(solution)/shard_map/ppermute | solution.py:60
  5.0 18.5 %collective-permute-start.2 = (bf16[3,64,1024]{2,1,0:T(8,128)(2,1)}, bf16[3,64,1024]{2,1,0:T(8,128)(2,1)S(1)}, u32[]{:S(2)}, u32[]{:S(2)}) collective-permute-start(bf16[3,64,1024]{2,1,0:T(8,128)(2,1)} %get-tuple-element.83), channel_id=1, source_target_pairs={{0,255},{1,224},{2,225},{3,226},{4,227},{5,228},{6,229},{7,230},{8... | collective-permute-start | bytes 1179656 | tf_op jit(solution)/shard_map/ppermute | solution.py:60
  13.6 6.6 %copy-start.6 = (f32[32]{0:T(128)S(1)}, f32[32]{0:T(128)}, u32[]{:S(2)}) copy-start(f32[32]{0:T(128)} %param.13) | copy-start | bytes 388
  13.6 10.0 %copy-start.5 = (bf16[64,2048]{1,0:T(8,128)(2,1)S(1)}, bf16[64,2048]{1,0:T(8,128)(2,1)}, u32[]{:S(2)}) copy-start(bf16[64,2048]{1,0:T(8,128)(2,1)} %get-tuple-element.93) | copy-start | bytes 786436
  13.6 12.1 %copy-start.4 = (bf16[64,2048]{1,0:T(8,128)(2,1)S(1)}, bf16[64,2048]{1,0:T(8,128)(2,1)}, u32[]{:S(2)}) copy-start(bf16[64,2048]{1,0:T(8,128)(2,1)} %get-tuple-element.94) | copy-start | bytes 786436
  13.6 15.6 %copy-start.3 = (bf16[64,2048]{1,0:T(8,128)(2,1)S(1)}, bf16[64,2048]{1,0:T(8,128)(2,1)}, u32[]{:S(2)}) copy-start(bf16[64,2048]{1,0:T(8,128)(2,1)} %get-tuple-element.95) | copy-start | bytes 786436
  13.6 19.3 %copy-start = (bf16[3,64,1024]{2,1,0:T(8,128)(2,1)S(1)}, bf16[3,64,1024]{2,1,0:T(8,128)(2,1)}, u32[]{:S(2)}) copy-start(bf16[3,64,1024]{2,1,0:T(8,128)(2,1)} %get-tuple-element.87.tl_ref) | copy-start | bytes 1179652
  23.6 18.9 %collective-permute-start.3 = (bf16[64,2048]{1,0:T(8,128)(2,1)S(1)}, bf16[64,2048]{1,0:T(8,128)(2,1)S(1)}, u32[]{:S(2)}, u32[]{:S(2)}) collective-permute-start(bf16[64,2048]{1,0:T(8,128)(2,1)S(1)} %copy-done.5), channel_id=1, source_target_pairs={{0,224},{1,225},{2,226},{3,227},{4,228},{5,229},{6,230},{7,231},{8... | collective-permute-start | bytes 786440 | tf_op jit(solution)/shard_map/ppermute | solution.py:60
  25.7 16.9 %collective-permute-start.4 = (bf16[64,2048]{1,0:T(8,128)(2,1)S(1)}, bf16[64,2048]{1,0:T(8,128)(2,1)S(1)}, u32[]{:S(2)}, u32[]{:S(2)}) collective-permute-start(bf16[64,2048]{1,0:T(8,128)(2,1)S(1)} %copy-done.4), channel_id=1, source_target_pairs={{0,31},{1,0},{2,1},{3,2},{4,3},{5,4},{6,5},{7,6},{8,7},{9,8},{10,9... | collective-permute-start | bytes 786440 | tf_op jit(solution)/shard_map/ppermute | solution.py:60
  29.2 13.3 %collective-permute-start.5 = (bf16[64,2048]{1,0:T(8,128)(2,1)S(1)}, bf16[64,2048]{1,0:T(8,128)(2,1)S(1)}, u32[]{:S(2)}, u32[]{:S(2)}) collective-permute-start(bf16[64,2048]{1,0:T(8,128)(2,1)S(1)} %copy-done.3), channel_id=1, source_target_pairs={{0,255},{1,224},{2,225},{3,226},{4,227},{5,228},{6,229},{7,230},{8... | collective-permute-start | bytes 786440 | tf_op jit(solution)/shard_map/ppermute | solution.py:60
  32.9 9.7 %copy-start.1 = (bf16[64,2048]{1,0:T(8,128)(2,1)S(1)}, bf16[64,2048]{1,0:T(8,128)(2,1)}, u32[]{:S(2)}) copy-start(bf16[64,2048]{1,0:T(8,128)(2,1)} %get-tuple-element.97) | copy-start | bytes 786436
  32.9 10.6 %copy-start.2 = (bf16[1024,2048]{1,0:T(8,128)(2,1)S(1)}, bf16[1024,2048]{1,0:T(8,128)(2,1)}, u32[]{:S(2)}) copy-start(bf16[1024,2048]{1,0:T(8,128)(2,1)} %param.15) | copy-start | bytes 12582916
  42.5 9.3 %collective-permute-start.6 = (bf16[1024,256]{1,0:T(8,128)(2,1)S(1)}, bf16[1024,256]{1,0:T(8,128)(2,1)S(1)}, u32[]{:S(2)}, u32[]{:S(2)}) collective-permute-start(bf16[1024,256]{1,0:T(8,128)(2,1)S(1)} %get-tuple-element.96.own_ref), channel_id=1, source_target_pairs={{0,1},{1,0},{2,3},{3,2},{4,5},{5,4},{6,7},{7,6},{8,9},{9,8},{10,11... | collective-permute-start | bytes 1572872 | tf_op jit(solution)/shard_map/ppermute | solution.py:50
  42.7 9.1 %collective-permute-start.7 = (bf16[256,2048]{1,0:T(8,128)(2,1)S(1)}, bf16[256,2048]{1,0:T(8,128)(2,1)S(1)}, u32[]{:S(2)}, u32[]{:S(2)}) collective-permute-start(bf16[256,2048]{1,0:T(8,128)(2,1)S(1)} %constant_dynamic-update-slice_fusion.drop_ref), channel_id=1, source_target_pairs={{0,1},{1,0},{2,3},{3,2},{4,5},{5,4},{6,7},{7,6},{8,9},{9,8},{10,11... | collective-permute-start | bytes 3145736 | tf_op jit(solution)/shard_map/ppermute | solution.py:50
  54.0 15.2 %collective-permute-start.8 = (bf16[128,2048]{1,0:T(8,128)(2,1)S(1)}, bf16[128,2048]{1,0:T(8,128)(2,1)S(1)}, u32[]{:S(2)}, u32[]{:S(2)}) collective-permute-start(bf16[128,2048]{1,0:T(8,128)(2,1)S(1)} %get-tuple-element.118), channel_id=1, source_target_pairs={{0,64},{1,65},{2,66},{3,67},{4,68},{5,69},{6,70},{7,71},{8,72},{9,... | collective-permute-start | bytes 1572872 | tf_op jit(solution)/shard_map/ppermute | solution.py:50
  54.0 15.1 %collective-permute-start.9 = (bf16[128,2048]{1,0:T(8,128)(2,1)S(1)}, bf16[128,2048]{1,0:T(8,128)(2,1)S(1)}, u32[]{:S(2)}, u32[]{:S(2)}) collective-permute-start(bf16[128,2048]{1,0:T(8,128)(2,1)S(1)} %get-tuple-element.119), channel_id=1, source_target_pairs={{0,192},{1,193},{2,194},{3,195},{4,196},{5,197},{6,198},{7,199},{8... | collective-permute-start | bytes 1572872 | tf_op jit(solution)/shard_map/ppermute | solution.py:50
  69.1 30.5 %collective-permute-start.10 = (bf16[128,2048]{1,0:T(8,128)(2,1)S(1)}, bf16[128,2048]{1,0:T(8,128)(2,1)S(1)}, u32[]{:S(2)}, u32[]{:S(2)}) collective-permute-start(bf16[128,2048]{1,0:T(8,128)(2,1)S(1)} %get-tuple-element.127), channel_id=1, source_target_pairs={{0,128},{1,129},{2,130},{3,131},{4,132},{5,133},{6,134},{7,135},{8... | collective-permute-start | bytes 1572872 | tf_op jit(solution)/shard_map/ppermute | solution.py:50
  71.6 23.8 %collective-permute-start.11 = (bf16[3,64,1024]{2,1,0:T(8,128)(2,1)S(1)}, bf16[3,64,1024]{2,1,0:T(8,128)(2,1)S(1)}, u32[]{:S(2)}, u32[]{:S(2)}) collective-permute-start(bf16[3,64,1024]{2,1,0:T(8,128)(2,1)S(1)} %get-tuple-element.128), channel_id=1, source_target_pairs={{0,33},{1,34},{2,35},{3,36},{4,37},{5,38},{6,39},{7,40},{8,41},{9,... | collective-permute-start | bytes 1179656 | tf_op jit(solution)/shard_map/ppermute | solution.py:60
  71.6 28.1 %collective-permute-start.12 = (bf16[3,64,1024]{2,1,0:T(8,128)(2,1)S(1)}, bf16[3,64,1024]{2,1,0:T(8,128)(2,1)S(1)}, u32[]{:S(2)}, u32[]{:S(2)}) collective-permute-start(bf16[3,64,1024]{2,1,0:T(8,128)(2,1)S(1)} %get-tuple-element.129), channel_id=1, source_target_pairs={{0,32},{1,33},{2,34},{3,35},{4,36},{5,37},{6,38},{7,39},{8,40},{9,... | collective-permute-start | bytes 1179656 | tf_op jit(solution)/shard_map/ppermute | solution.py:60
  72.6 27.1 %collective-permute-start.13 = (bf16[3,64,1024]{2,1,0:T(8,128)(2,1)S(1)}, bf16[3,64,1024]{2,1,0:T(8,128)(2,1)S(1)}, u32[]{:S(2)}, u32[]{:S(2)}) collective-permute-start(bf16[3,64,1024]{2,1,0:T(8,128)(2,1)S(1)} %get-tuple-element.130), channel_id=1, source_target_pairs={{0,1},{1,2},{2,3},{3,4},{4,5},{5,6},{6,7},{7,8},{8,9},{9,10},{10,1... | collective-permute-start | bytes 1179656 | tf_op jit(solution)/shard_map/ppermute | solution.py:60
  101.2 16.1 %all-to-all-start.1 = ((bf16[32,32,128]{2,1,0:T(8,128)(2,1)}), bf16[32,32,128]{2,1,0:T(8,128)(2,1)S(1)}, u32[]{:S(2)}, u32[]{:S(2)}) async-start(bf16[32,32,128]{2,1,0:T(8,128)(2,1)} %broadcast_in_dim.3), calls=%async_computation.1 | async-start | bytes 524288 | tf_op jit(solution)/shard_map/all_to_all | solution.py:550
  109.7 8.3 %collective-permute-start.14 = (bf16[32,2048]{1,0:T(8,128)(2,1)S(1)}, bf16[32,2048]{1,0:T(8,128)(2,1)S(1)}, u32[]{:S(2)}, u32[]{:S(2)}) collective-permute-start(bf16[32,2048]{1,0:T(8,128)(2,1)S(1)} %get-tuple-element.148), channel_id=1, source_target_pairs={{0,32},{1,33},{2,34},{3,35},{4,36},{5,37},{6,38},{7,39},{8,40},{9,... | collective-permute-start | bytes 393224 | tf_op jit(solution)/shard_map/ppermute | solution.py:50
  110.0 9.2 %collective-permute-start.15 = (bf16[32,2048]{1,0:T(8,128)(2,1)S(1)}, bf16[32,2048]{1,0:T(8,128)(2,1)S(1)}, u32[]{:S(2)}, u32[]{:S(2)}) collective-permute-start(bf16[32,2048]{1,0:T(8,128)(2,1)S(1)} %get-tuple-element.149), channel_id=1, source_target_pairs={{0,2},{1,3},{2,0},{3,1},{4,6},{5,7},{6,4},{7,5},{8,10},{9,11},{10,... | collective-permute-start | bytes 393224 | tf_op jit(solution)/shard_map/ppermute | solution.py:50
  112.7 8.7 %collective-permute-start.16 = (bf16[32,2048]{1,0:T(8,128)(2,1)S(1)}, bf16[32,2048]{1,0:T(8,128)(2,1)S(1)}, u32[]{:S(2)}, u32[]{:S(2)}) collective-permute-start(bf16[32,2048]{1,0:T(8,128)(2,1)S(1)} %get-tuple-element.150), channel_id=1, source_target_pairs={{0,34},{1,35},{2,32},{3,33},{4,38},{5,39},{6,36},{7,37},{8,42},{9,... | collective-permute-start | bytes 393224 | tf_op jit(solution)/shard_map/ppermute | solution.py:50
  122.2 18.2 %all-to-all-start.2 = ((bf16[8,4,3072]{2,1,0:T(4,128)(2,1)}), bf16[8,4,3072]{2,1,0:T(4,128)(2,1)S(1)}, u32[]{:S(2)}, u32[]{:S(2)}) async-start(bf16[8,4,3072]{2,1,0:T(4,128)(2,1)} %sum_for_z.1), calls=%async_computation.2 | async-start | bytes 393216 | tf_op jit(solution)/shard_map/all_to_all | solution.py:536

commit v6 on v3

--- a/solution.py
+++ b/solution.py
@@ -593,9 +593,8 @@
     quads = (br, move_map(tr, -1, 0), move_map(bl, 0, -1), move_map(tl, -1, -1))
     bias = bias_blocks(bias_table)
     tl, tr, bl, br = split_dropped(out_grad, keep_mask)
-    bias, tr, bl = lax.optimization_barrier((bias, tr, bl))
+    quads, tl, tr, bl = lax.optimization_barrier((quads, tl, tr, bl))
     up, left = move_map(tr, -1, 0), move_map(bl, 0, -1)
-    quads, tl = lax.optimization_barrier((quads, tl))
     attn_t, probs = forward(logit_scale * LOG2E, quads, bias)
     pieces = (br, up, left, move_map(tl, -1, -1))
     attn_t, pieces = lax.optimization_barrier((attn_t, pieces))

time: 144 us -> 141 us (0.979)
  starting transfers between devices: 41.3 us -> 36.2 us
  waiting for transfers between devices: 31.3 us -> 36.1 us
  blocking collectives: 19.2 us -> 16.9 us
    ppermute x8, starting transfers between devices: 13 us -> 8.2 us  [move(): return lax.ppermute(value, ('row', 'col'), pairs)]
    ppermute x9, waiting for transfers between devices: 0.02 us -> 3.4 us  [move_map(): return lax.ppermute(value, ('row', 'col'), pairs)]
    all_to_all x1, starting transfers between devices: 11.4 us -> 8.46 us  [table_plane(): lax.all_to_all(same, ('row', 'col'), 0, 0, axis_index_groups=groups, tile...]
    all_to_all x1, starting transfers between devices: 3.5 us -> 5.9 us  [along_z_exchange(): lax.all_to_all(value, 'col', 0, 0, axis_index_groups=groups, tiled=True)]
    all_to_all x1, blocking collectives: 19.2 us -> 16.9 us  [along_z_exchange(): lax.all_to_all(value, 'col', 0, 0, axis_index_groups=groups, tiled=True)]
    ppermute x8, waiting for transfers between devices: 18.1 us -> 19.5 us  [move(): return lax.ppermute(value, ('row', 'col'), pairs)]
  transfers between devices with their start and end apart: 19 -> 19, of which waited for: 7 -> 8; matrix products, arithmetic and copies ran while one was open for 2% -> 2% of each run, Pallas kernels for 25% -> 26%
where the time goes in v6:
time: 141 us; the launch traced here: 139 us
  Pallas kernels  43.8 us (31%)
  starting transfers between devices  36.2 us (26%)
  waiting for transfers between devices  36.1 us (26%)
  blocking collectives  16.9 us (12%)
  local copies, waits for them, and re-layouts  3.95 us (3%)
    ppermute x8, waiting for transfers between devices, move(): return lax.ppermute(value, ('row', 'col'), pairs)  19.5 us
    all_to_all x1, blocking collectives, along_z_exchange(): lax.all_to_all(value, 'col', 0, 0, axis_index_groups=groups, tiled=True)  16.9 us
    pallas_call x2, Pallas kernels, backward(): pl.pallas_call(functools.partial(backward_kernel, first), grid=(steps,),...  14 us
    ppermute x9, starting transfers between devices, move_map(): return lax.ppermute(value, ('row', 'col'), pairs)  13.6 us
    pallas_call x1, Pallas kernels, forward(): pl.pallas_call(forward_kernel, grid=(INNER // TILE // GROUP,), in_specs=[...  9.58 us
    all_to_all x1, waiting for transfers between devices, along_z_exchange(): lax.all_to_all(value, 'col', 0, 0, axis_index_groups=groups, tiled=True)  8.58 us
    all_to_all x1, starting transfers between devices, table_plane(): lax.all_to_all(same, ('row', 'col'), 0, 0, axis_index_groups=groups, tile...  8.46 us
    ppermute x8, starting transfers between devices, move(): return lax.ppermute(value, ('row', 'col'), pairs)  8.2 us
  transfers between devices with their start and end apart: 19, of which 8 were waited for; matrix products, arithmetic and copies ran while one was open for 2% of the time, Pallas kernels for 26%

profile of v6, /device:TPU:24, one launch (start us, length us, event | category | flops | bytes accessed | tf_op | source)
XLA Modules:
  0.0 139.3 jit_solution(2979142803843670882)
XLA Ops:
  0.6 3.6 %split_maps.1 = (bf16[3,64,1024]{2,1,0:T(8,128)(2,1)}, bf16[3,64,1024]{2,1,0:T(8,128)(2,1)}, bf16[3,64,1024]{2,1,0:T(8,128)(2,1)}, bf16[3,64,1024]{2,1,0:T(8,128)(2,1)}) custom-call(bf16[16,16,1024]{2,1,0:T(8,128)(2,1)} %q_ref.1, bf16[16,16,1024]{2,1,0:T(8,128)(2,1)} %k_ref.1, bf16[16,16,1024]{2,1,0:T(8,128)(2,1)} %v_ref.1), custom_call_target="tpu_custom_call" | custom-call | tf_op jit(solution)/shard_map/split_maps/pallas_call | solution.py:106
  4.3 0.8 collective-permute-start
  5.0 0.0 collective-permute-start.1
  5.0 3.3 %collective-permute-start.2 = (bf16[3,64,1024]{2,1,0:T(8,128)(2,1)}, bf16[3,64,1024]{2,1,0:T(8,128)(2,1)S(1)}, u32[]{:S(2)}, u32[]{:S(2)}) collective-permute-start(bf16[3,64,1024]{2,1,0:T(8,128)(2,1)} %get-tuple-element.85), channel_id=1, source_target_pairs={{0,255},{1,224},{2,225},{3,226},{4,227},{5,228},{6,229},{7,230},{8... | collective-permute-start | bytes 1179656 | tf_op jit(solution)/shard_map/ppermute | solution.py:60
  8.4 1.3 copy.23.table_ref
  9.7 3.8 %split_dropped.1 = (bf16[64,2048]{1,0:T(8,128)(2,1)}, bf16[64,2048]{1,0:T(8,128)(2,1)}, bf16[64,2048]{1,0:T(8,128)(2,1)}, bf16[64,2048]{1,0:T(8,128)(2,1)}) custom-call(bf16[16,16,2048]{2,1,0:T(8,128)(2,1)} %grad_ref.1, s32[16,16,2048]{2,1,0:T(8,128)} %keep_ref.1), custom_call_target="tpu_custom_call" | custom-call | tf_op jit(solution)/shard_map/split_dropped/pallas_call | solution.py:126
  13.6 0.0 copy-start
  13.6 6.5 %bias_blocks.1.bias_ref = f32[32,3,128,128]{3,2,1,0:T(8,128)} custom-call(f32[32,31,31]{2,1,0:T(8,128)S(1)} %copy.23.table_ref), custom_call_target="tpu_custom_call" | custom-call | flops 10000000 | bytes 8000000 | tf_op jit(solution)/shard_map/bias_blocks/pallas_call | solution.py:180
  20.1 0.1 pad_add_fusion.place_ref
  20.2 0.0 collective-permute-done.bl_ref
  20.2 2.0 %collective-permute-done.1.tr_ref = bf16[3,64,1024]{2,1,0:T(8,128)(2,1)S(1)} collective-permute-done((bf16[3,64,1024]{2,1,0:T(8,128)(2,1)}, bf16[3,64,1024]{2,1,0:T(8,128)(2,1)S(1)}, u32[]{:S(2)}, u32[]{:S(2)}) %collective-permute-start.1) | collective-permute-done | bytes 393248 | tf_op jit(solution)/shard_map/ppermute | solution.py:60
  22.2 1.4 collective-permute-done.2.br_ref
  23.6 2.1 %collective-permute-start.3 = (bf16[64,2048]{1,0:T(8,128)(2,1)S(1)}, bf16[64,2048]{1,0:T(8,128)(2,1)S(1)}, u32[]{:S(2)}, u32[]{:S(2)}) collective-permute-start(bf16[64,2048]{1,0:T(8,128)(2,1)S(1)} %copy-done.5), channel_id=1, source_target_pairs={{0,224},{1,225},{2,226},{3,227},{4,228},{5,229},{6,230},{7,231},{8... | collective-permute-start | bytes 786440 | tf_op jit(solution)/shard_map/ppermute | solution.py:60
  25.7 3.6 %collective-permute-start.4 = (bf16[64,2048]{1,0:T(8,128)(2,1)S(1)}, bf16[64,2048]{1,0:T(8,128)(2,1)S(1)}, u32[]{:S(2)}, u32[]{:S(2)}) collective-permute-start(bf16[64,2048]{1,0:T(8,128)(2,1)S(1)} %copy-done.4), channel_id=1, source_target_pairs={{0,31},{1,0},{2,1},{3,2},{4,3},{5,4},{6,5},{7,6},{8,7},{9,8},{10,9... | collective-permute-start | bytes 786440 | tf_op jit(solution)/shard_map/ppermute | solution.py:60
  29.2 3.7 %collective-permute-start.5 = (bf16[64,2048]{1,0:T(8,128)(2,1)S(1)}, bf16[64,2048]{1,0:T(8,128)(2,1)S(1)}, u32[]{:S(2)}, u32[]{:S(2)}) collective-permute-start(bf16[64,2048]{1,0:T(8,128)(2,1)S(1)} %copy-done.3), channel_id=1, source_target_pairs={{0,255},{1,224},{2,225},{3,226},{4,227},{5,228},{6,229},{7,230},{8... | collective-permute-start | bytes 786440 | tf_op jit(solution)/shard_map/ppermute | solution.py:60
  32.9 9.6 %forward.1 = (bf16[1024,256]{1,0:T(8,128)(2,1)S(1)}, f32[32,256,256]{2,1,0:T(8,128)}) custom-call(f32[32]{0:T(128)S(1)} %get-tuple-element.177.scale_ref, bf16[3,64,1024]{2,1,0:T(8,128)(2,1)S(1)} %copy-done, bf16[3,64,1024]{2,1,0:T(8,128)(2,1)S(1)} %collective-permute-done.bl_ref, bf16[3,64,1024]{2,1,0:T(8,128)(2,1)S(1)} %collective-permute-done.1.tr_ref, ...), custom_call_target="tpu_custom_call" | custom-call | flops 8000000000 | bytes 16000000 | tf_op jit(solution)/shard_map/forward/pallas_call | solution.py:277
  42.5 0.0 collective-permute-done.5
  42.5 0.1 collective-permute-start.6
  42.7 0.8 collective-permute-start.7
  43.5 1.3 convolution_convert_fusion.grad_ref
  44.8 7.0 %backward.2 = (bf16[3,64,1024]{2,1,0:T(8,128)(2,1)S(1)}, bf16[3,64,1024]{2,1,0:T(8,128)(2,1)S(1)}, bf16[3,64,1024]{2,1,0:T(8,128)(2,1)S(1)}, bf16[3,64,1024]{2,1,0:T(8,128)(2,1)S(1)}, bf16[8,32,128]{2,1,0:T(8,128)(2,1)S(1)}) custom-call(f32[32]{0:T(128)S(1)} %get-tuple-element.176.scale_ref, bf16[3,64,1024]{2,1,0:T(8,128)(2,1)S(1)} %copy-done, ...), custom_call_target="tpu_custom_call" | custom-call | flops 8000000000 | bytes 10000000 | tf_op jit(solution)/shard_map/backward/pallas_call | solution.py:428
  51.8 2.2 %outer_terms.1 = (f32[128,2048]{1,0:T(8,128)S(1)}, bf16[128,2048]{1,0:T(8,128)(2,1)S(1)}, bf16[128,2048]{1,0:T(8,128)(2,1)S(1)}, bf16[128,2048]{1,0:T(8,128)(2,1)S(1)}) custom-call(s32[4]{0:T(128)S(1)} %pad_add_fusion.place_ref, bf16[1024,256]{1,0:T(8,128)(2,1)S(1)} %get-tuple-element.98.own_ref, bf16[1024,256]{1,0:T(8,128)(2,1)S(1)} %collective-permute-done.6.other_ref, ...), custom_call_target="tpu_custom_call" | custom-call | flops 1100000000 | bytes 6000000 | tf_op jit(solution)/shard_map/outer_terms/pallas_call | solution.py:468
  54.0 0.1 collective-permute-start.8
  54.1 3.2 %collective-permute-start.9 = (bf16[128,2048]{1,0:T(8,128)(2,1)S(1)}, bf16[128,2048]{1,0:T(8,128)(2,1)S(1)}, u32[]{:S(2)}, u32[]{:S(2)}) collective-permute-start(bf16[128,2048]{1,0:T(8,128)(2,1)S(1)} %get-tuple-element.121), channel_id=1, source_target_pairs={{0,192},{1,193},{2,194},{3,195},{4,196},{5,197},{6,198},{7,199},{8... | collective-permute-start | bytes 1572872 | tf_op jit(solution)/shard_map/ppermute | solution.py:50
  57.4 1.0 collective-permute-start.10
  58.4 7.0 %backward.3 = (bf16[3,64,1024]{2,1,0:T(8,128)(2,1)S(1)}, bf16[3,64,1024]{2,1,0:T(8,128)(2,1)S(1)}, bf16[3,64,1024]{2,1,0:T(8,128)(2,1)S(1)}, bf16[3,64,1024]{2,1,0:T(8,128)(2,1)S(1)}, bf16[8,32,128]{2,1,0:T(8,128)(2,1)S(1)}) custom-call(f32[32]{0:T(128)S(1)} %get-tuple-element.176.scale_ref, ...), custom_call_target="tpu_custom_call", output_to_operand_aliasing={{0}: (7, {}), {1}: (8, {}), {2}: (9, {}), {3}: (10, {}), {4... | custom-call | flops 8000000000 | bytes 10000000 | tf_op jit(solution)/shard_map/backward/pallas_call | solution.py:428
  65.4 0.1 collective-permute-start.12
  65.5 0.1 collective-permute-start.13
  65.6 15.5 %collective-permute-done.8.refs_1_ = bf16[128,2048]{1,0:T(8,128)(2,1)S(1)} collective-permute-done((bf16[128,2048]{1,0:T(8,128)(2,1)S(1)}, bf16[128,2048]{1,0:T(8,128)(2,1)S(1)}, u32[]{:S(2)}, u32[]{:S(2)}) %collective-permute-start.8) | collective-permute-done | bytes 524320 | tf_op jit(solution)/shard_map/ppermute | solution.py:50
  81.1 0.0 collective-permute-start.11
  81.1 16.9 %all_to_all.15 = bf16[8,32,128]{2,1,0:T(8,128)(2,1)S(1)} all-to-all(bf16[8,32,128]{2,1,0:T(8,128)(2,1)S(1)} %get-tuple-element.150), channel_id=1, replica_groups={{0,4,8,12,16,20,24,28},{1,5,9,13,17,21,25,29},{2,6,10,14,18,22,26,30},{..., dimensions={0} | all-to-all | bytes 131072 | tf_op jit(solution)/shard_map/all_to_all | solution.py:536
  98.0 0.8 sum_for_y.1
  98.8 0.7 broadcast_in_dim.3
  99.6 8.5 %all-to-all-start.1 = ((bf16[32,32,128]{2,1,0:T(8,128)(2,1)}), bf16[32,32,128]{2,1,0:T(8,128)(2,1)S(1)}, u32[]{:S(2)}, u32[]{:S(2)}) async-start(bf16[32,32,128]{2,1,0:T(8,128)(2,1)} %broadcast_in_dim.3), calls=%async_computation.1 | async-start | bytes 524288 | tf_op jit(solution)/shard_map/all_to_all | solution.py:550
  108.0 0.3 collective-permute-start.14
  108.3 2.7 %collective-permute-start.15 = (bf16[32,2048]{1,0:T(8,128)(2,1)S(1)}, bf16[32,2048]{1,0:T(8,128)(2,1)S(1)}, u32[]{:S(2)}, u32[]{:S(2)}) collective-permute-start(bf16[32,2048]{1,0:T(8,128)(2,1)S(1)} %get-tuple-element.153), channel_id=1, source_target_pairs={{0,2},{1,3},{2,0},{3,1},{4,6},{5,7},{6,4},{7,5},{8,10},{9,11},{10,... | collective-permute-start | bytes 393224 | tf_op jit(solution)/shard_map/ppermute | solution.py:50
  111.0 4.6 %all-to-all-done.1 = bf16[32,32,128]{2,1,0:T(8,128)(2,1)S(1)} async-done(((bf16[32,32,128]{2,1,0:T(8,128)(2,1)}), bf16[32,32,128]{2,1,0:T(8,128)(2,1)S(1)}, u32[]{:S(2)}, u32[]{:S(2)}) %all-to-all-start.1) | async-done | bytes 262176 | tf_op jit(solution)/shard_map/all_to_all | solution.py:550
  115.7 0.6 collective-permute-done.14.refs_1_
  116.3 1.3 collective-permute-done.15.refs_2_
  117.6 2.1 %collective-permute-done.16.refs_3_ = bf16[32,2048]{1,0:T(8,128)(2,1)S(1)} collective-permute-done((bf16[32,2048]{1,0:T(8,128)(2,1)S(1)}, bf16[32,2048]{1,0:T(8,128)(2,1)S(1)}, u32[]{:S(2)}, u32[]{:S(2)}) %collective-permute-start.16) | collective-permute-done | bytes 131104 | tf_op jit(solution)/shard_map/ppermute | solution.py:50
  119.7 0.8 sum_for_z.1
  120.5 5.9 %all-to-all-start.2 = ((bf16[8,4,3072]{2,1,0:T(4,128)(2,1)}), bf16[8,4,3072]{2,1,0:T(4,128)(2,1)S(1)}, u32[]{:S(2)}, u32[]{:S(2)}) async-start(bf16[8,4,3072]{2,1,0:T(4,128)(2,1)} %sum_for_z.1), calls=%async_computation.2 | async-start | bytes 393216 | tf_op jit(solution)/shard_map/all_to_all | solution.py:536
  126.4 1.9 %join_maps.1 = (bf16[16,16,1024]{2,1,0:T(8,128)(2,1)}, bf16[16,16,1024]{2,1,0:T(8,128)(2,1)}, bf16[16,16,1024]{2,1,0:T(8,128)(2,1)}) custom-call(bf16[3,64,1024]{2,1,0:T(8,128)(2,1)S(1)} %collective-permute-done.11.tl_ref, bf16[3,64,1024]{2,1,0:T(8,128)(2,1)S(1)} %collective-permute-done.12.tr_ref, bf16[3,64,1024]{2,1,0:T(8,128)(2,1)S(1)} %collective-permute-done.13.bl_ref, ...), custom_call_target="tpu_custom_call" | custom-call | tf_op jit(solution)/shard_map/join_maps/pallas_call | solution.py:147
  128.3 8.6 %all-to-all-done.2.found_ref = bf16[8,4,3072]{2,1,0:T(4,128)(2,1)S(1)} async-done(((bf16[8,4,3072]{2,1,0:T(4,128)(2,1)}), bf16[8,4,3072]{2,1,0:T(4,128)(2,1)S(1)}, u32[]{:S(2)}, u32[]{:S(2)}) %all-to-all-start.2) | async-done | bytes 196640 | tf_op jit(solution)/shard_map/all_to_all | solution.py:536
  136.9 0.1 slice.3
  137.0 0.6 reshape.16
  137.6 0.7 totals.1
  138.3 1.1 copy.24
  (32 shorter events, 0.2 us)
Async XLA Ops:
  4.3 15.9 %collective-permute-start = (bf16[3,64,1024]{2,1,0:T(8,128)(2,1)}, bf16[3,64,1024]{2,1,0:T(8,128)(2,1)S(1)}, u32[]{:S(2)}, u32[]{:S(2)}) collective-permute-start(bf16[3,64,1024]{2,1,0:T(8,128)(2,1)} %get-tuple-element.83), channel_id=1, source_target_pairs={{0,224},{1,225},{2,226},{3,227},{4,228},{5,229},{6,230},{7,231},{8... | collective-permute-start | bytes 1179656 | tf_op jit(solution)/shard_map/ppermute | solution.py:60
  5.0 17.2 %collective-permute-start.1 = (bf16[3,64,1024]{2,1,0:T(8,128)(2,1)}, bf16[3,64,1024]{2,1,0:T(8,128)(2,1)S(1)}, u32[]{:S(2)}, u32[]{:S(2)}) collective-permute-start(bf16[3,64,1024]{2,1,0:T(8,128)(2,1)} %get-tuple-element.84), channel_id=1, source_target_pairs={{0,31},{1,0},{2,1},{3,2},{4,3},{5,4},{6,5},{7,6},{8,7},{9,8},{10,9... | collective-permute-start | bytes 1179656 | tf_op jit(solution)/shard_map/ppermute | solution.py:60
  5.0 18.5 %collective-permute-start.2 = (bf16[3,64,1024]{2,1,0:T(8,128)(2,1)}, bf16[3,64,1024]{2,1,0:T(8,128)(2,1)S(1)}, u32[]{:S(2)}, u32[]{:S(2)}) collective-permute-start(bf16[3,64,1024]{2,1,0:T(8,128)(2,1)} %get-tuple-element.85), channel_id=1, source_target_pairs={{0,255},{1,224},{2,225},{3,226},{4,227},{5,228},{6,229},{7,230},{8... | collective-permute-start | bytes 1179656 | tf_op jit(solution)/shard_map/ppermute | solution.py:60
  13.6 6.6 %copy-start.6 = (f32[32]{0:T(128)S(1)}, f32[32]{0:T(128)}, u32[]{:S(2)}) copy-start(f32[32]{0:T(128)} %param.13) | copy-start | bytes 388
  13.6 10.0 %copy-start.5 = (bf16[64,2048]{1,0:T(8,128)(2,1)S(1)}, bf16[64,2048]{1,0:T(8,128)(2,1)}, u32[]{:S(2)}) copy-start(bf16[64,2048]{1,0:T(8,128)(2,1)} %get-tuple-element.95) | copy-start | bytes 786436
  13.6 12.1 %copy-start.4 = (bf16[64,2048]{1,0:T(8,128)(2,1)S(1)}, bf16[64,2048]{1,0:T(8,128)(2,1)}, u32[]{:S(2)}) copy-start(bf16[64,2048]{1,0:T(8,128)(2,1)} %get-tuple-element.96) | copy-start | bytes 786436
  13.6 15.6 %copy-start.3 = (bf16[64,2048]{1,0:T(8,128)(2,1)S(1)}, bf16[64,2048]{1,0:T(8,128)(2,1)}, u32[]{:S(2)}) copy-start(bf16[64,2048]{1,0:T(8,128)(2,1)} %get-tuple-element.97) | copy-start | bytes 786436
  13.6 19.3 %copy-start = (bf16[3,64,1024]{2,1,0:T(8,128)(2,1)S(1)}, bf16[3,64,1024]{2,1,0:T(8,128)(2,1)}, u32[]{:S(2)}) copy-start(bf16[3,64,1024]{2,1,0:T(8,128)(2,1)} %get-tuple-element.89.tl_ref) | copy-start | bytes 1179652
  23.6 18.9 %collective-permute-start.3 = (bf16[64,2048]{1,0:T(8,128)(2,1)S(1)}, bf16[64,2048]{1,0:T(8,128)(2,1)S(1)}, u32[]{:S(2)}, u32[]{:S(2)}) collective-permute-start(bf16[64,2048]{1,0:T(8,128)(2,1)S(1)} %copy-done.5), channel_id=1, source_target_pairs={{0,224},{1,225},{2,226},{3,227},{4,228},{5,229},{6,230},{7,231},{8... | collective-permute-start | bytes 786440 | tf_op jit(solution)/shard_map/ppermute | solution.py:60
  25.7 16.9 %collective-permute-start.4 = (bf16[64,2048]{1,0:T(8,128)(2,1)S(1)}, bf16[64,2048]{1,0:T(8,128)(2,1)S(1)}, u32[]{:S(2)}, u32[]{:S(2)}) collective-permute-start(bf16[64,2048]{1,0:T(8,128)(2,1)S(1)} %copy-done.4), channel_id=1, source_target_pairs={{0,31},{1,0},{2,1},{3,2},{4,3},{5,4},{6,5},{7,6},{8,7},{9,8},{10,9... | collective-permute-start | bytes 786440 | tf_op jit(solution)/shard_map/ppermute | solution.py:60
  29.2 13.3 %collective-permute-start.5 = (bf16[64,2048]{1,0:T(8,128)(2,1)S(1)}, bf16[64,2048]{1,0:T(8,128)(2,1)S(1)}, u32[]{:S(2)}, u32[]{:S(2)}) collective-permute-start(bf16[64,2048]{1,0:T(8,128)(2,1)S(1)} %copy-done.3), channel_id=1, source_target_pairs={{0,255},{1,224},{2,225},{3,226},{4,227},{5,228},{6,229},{7,230},{8... | collective-permute-start | bytes 786440 | tf_op jit(solution)/shard_map/ppermute | solution.py:60
  32.9 9.7 %copy-start.1 = (bf16[64,2048]{1,0:T(8,128)(2,1)S(1)}, bf16[64,2048]{1,0:T(8,128)(2,1)}, u32[]{:S(2)}) copy-start(bf16[64,2048]{1,0:T(8,128)(2,1)} %get-tuple-element.99) | copy-start | bytes 786436
  32.9 10.6 %copy-start.2 = (bf16[1024,2048]{1,0:T(8,128)(2,1)S(1)}, bf16[1024,2048]{1,0:T(8,128)(2,1)}, u32[]{:S(2)}) copy-start(bf16[1024,2048]{1,0:T(8,128)(2,1)} %param.15) | copy-start | bytes 12582916
  42.5 9.3 %collective-permute-start.6 = (bf16[1024,256]{1,0:T(8,128)(2,1)S(1)}, bf16[1024,256]{1,0:T(8,128)(2,1)S(1)}, u32[]{:S(2)}, u32[]{:S(2)}) collective-permute-start(bf16[1024,256]{1,0:T(8,128)(2,1)S(1)} %get-tuple-element.98.own_ref), channel_id=1, source_target_pairs={{0,1},{1,0},{2,3},{3,2},{4,5},{5,4},{6,7},{7,6},{8,9},{9,8},{10,11... | collective-permute-start | bytes 1572872 | tf_op jit(solution)/shard_map/ppermute | solution.py:50
  42.7 9.1 %collective-permute-start.7 = (bf16[256,2048]{1,0:T(8,128)(2,1)S(1)}, bf16[256,2048]{1,0:T(8,128)(2,1)S(1)}, u32[]{:S(2)}, u32[]{:S(2)}) collective-permute-start(bf16[256,2048]{1,0:T(8,128)(2,1)S(1)} %constant_dynamic-update-slice_fusion.drop_ref), channel_id=1, source_target_pairs={{0,1},{1,0},{2,3},{3,2},{4,5},{5,4},{6,7},{7,6},{8,9},{9,8},{10,11... | collective-permute-start | bytes 3145736 | tf_op jit(solution)/shard_map/ppermute | solution.py:50
  54.0 27.0 %collective-permute-start.8 = (bf16[128,2048]{1,0:T(8,128)(2,1)S(1)}, bf16[128,2048]{1,0:T(8,128)(2,1)S(1)}, u32[]{:S(2)}, u32[]{:S(2)}) collective-permute-start(bf16[128,2048]{1,0:T(8,128)(2,1)S(1)} %get-tuple-element.120), channel_id=1, source_target_pairs={{0,64},{1,65},{2,66},{3,67},{4,68},{5,69},{6,70},{7,71},{8,72},{9,... | collective-permute-start | bytes 1572872 | tf_op jit(solution)/shard_map/ppermute | solution.py:50
  54.1 26.9 %collective-permute-start.9 = (bf16[128,2048]{1,0:T(8,128)(2,1)S(1)}, bf16[128,2048]{1,0:T(8,128)(2,1)S(1)}, u32[]{:S(2)}, u32[]{:S(2)}) collective-permute-start(bf16[128,2048]{1,0:T(8,128)(2,1)S(1)} %get-tuple-element.121), channel_id=1, source_target_pairs={{0,192},{1,193},{2,194},{3,195},{4,196},{5,197},{6,198},{7,199},{8... | collective-permute-start | bytes 1572872 | tf_op jit(solution)/shard_map/ppermute | solution.py:50
  57.4 40.7 %collective-permute-start.10 = (bf16[128,2048]{1,0:T(8,128)(2,1)S(1)}, bf16[128,2048]{1,0:T(8,128)(2,1)S(1)}, u32[]{:S(2)}, u32[]{:S(2)}) collective-permute-start(bf16[128,2048]{1,0:T(8,128)(2,1)S(1)} %get-tuple-element.130), channel_id=1, source_target_pairs={{0,128},{1,129},{2,130},{3,131},{4,132},{5,133},{6,134},{7,135},{8... | collective-permute-start | bytes 1572872 | tf_op jit(solution)/shard_map/ppermute | solution.py:50
  65.4 32.6 %collective-permute-start.12 = (bf16[3,64,1024]{2,1,0:T(8,128)(2,1)S(1)}, bf16[3,64,1024]{2,1,0:T(8,128)(2,1)S(1)}, u32[]{:S(2)}, u32[]{:S(2)}) collective-permute-start(bf16[3,64,1024]{2,1,0:T(8,128)(2,1)S(1)} %get-tuple-element.133), channel_id=1, source_target_pairs={{0,32},{1,33},{2,34},{3,35},{4,36},{5,37},{6,38},{7,39},{8,40},{9,... | collective-permute-start | bytes 1179656 | tf_op jit(solution)/shard_map/ppermute | solution.py:60
  65.5 32.5 %collective-permute-start.13 = (bf16[3,64,1024]{2,1,0:T(8,128)(2,1)S(1)}, bf16[3,64,1024]{2,1,0:T(8,128)(2,1)S(1)}, u32[]{:S(2)}, u32[]{:S(2)}) collective-permute-start(bf16[3,64,1024]{2,1,0:T(8,128)(2,1)S(1)} %get-tuple-element.134), channel_id=1, source_target_pairs={{0,1},{1,2},{2,3},{3,4},{4,5},{5,6},{6,7},{7,8},{8,9},{9,10},{10,1... | collective-permute-start | bytes 1179656 | tf_op jit(solution)/shard_map/ppermute | solution.py:60
  81.1 16.9 %collective-permute-start.11 = (bf16[3,64,1024]{2,1,0:T(8,128)(2,1)S(1)}, bf16[3,64,1024]{2,1,0:T(8,128)(2,1)S(1)}, u32[]{:S(2)}, u32[]{:S(2)}) collective-permute-start(bf16[3,64,1024]{2,1,0:T(8,128)(2,1)S(1)} %get-tuple-element.132), channel_id=1, source_target_pairs={{0,33},{1,34},{2,35},{3,36},{4,37},{5,38},{6,39},{7,40},{8,41},{9,... | collective-permute-start | bytes 1179656 | tf_op jit(solution)/shard_map/ppermute | solution.py:60
  99.6 16.0 %all-to-all-start.1 = ((bf16[32,32,128]{2,1,0:T(8,128)(2,1)}), bf16[32,32,128]{2,1,0:T(8,128)(2,1)S(1)}, u32[]{:S(2)}, u32[]{:S(2)}) async-start(bf16[32,32,128]{2,1,0:T(8,128)(2,1)} %broadcast_in_dim.3), calls=%async_computation.1 | async-start | bytes 524288 | tf_op jit(solution)/shard_map/all_to_all | solution.py:550
  108.0 8.3 %collective-permute-start.14 = (bf16[32,2048]{1,0:T(8,128)(2,1)S(1)}, bf16[32,2048]{1,0:T(8,128)(2,1)S(1)}, u32[]{:S(2)}, u32[]{:S(2)}) collective-permute-start(bf16[32,2048]{1,0:T(8,128)(2,1)S(1)} %get-tuple-element.152), channel_id=1, source_target_pairs={{0,32},{1,33},{2,34},{3,35},{4,36},{5,37},{6,38},{7,39},{8,40},{9,... | collective-permute-start | bytes 393224 | tf_op jit(solution)/shard_map/ppermute | solution.py:50
  108.3 9.2 %collective-permute-start.15 = (bf16[32,2048]{1,0:T(8,128)(2,1)S(1)}, bf16[32,2048]{1,0:T(8,128)(2,1)S(1)}, u32[]{:S(2)}, u32[]{:S(2)}) collective-permute-start(bf16[32,2048]{1,0:T(8,128)(2,1)S(1)} %get-tuple-element.153), channel_id=1, source_target_pairs={{0,2},{1,3},{2,0},{3,1},{4,6},{5,7},{6,4},{7,5},{8,10},{9,11},{10,... | collective-permute-start | bytes 393224 | tf_op jit(solution)/shard_map/ppermute | solution.py:50
  111.0 8.7 %collective-permute-start.16 = (bf16[32,2048]{1,0:T(8,128)(2,1)S(1)}, bf16[32,2048]{1,0:T(8,128)(2,1)S(1)}, u32[]{:S(2)}, u32[]{:S(2)}) collective-permute-start(bf16[32,2048]{1,0:T(8,128)(2,1)S(1)} %get-tuple-element.154), channel_id=1, source_target_pairs={{0,34},{1,35},{2,32},{3,33},{4,38},{5,39},{6,36},{7,37},{8,42},{9,... | collective-permute-start | bytes 393224 | tf_op jit(solution)/shard_map/ppermute | solution.py:50
  120.5 16.4 %all-to-all-start.2 = ((bf16[8,4,3072]{2,1,0:T(4,128)(2,1)}), bf16[8,4,3072]{2,1,0:T(4,128)(2,1)S(1)}, u32[]{:S(2)}, u32[]{:S(2)}) async-start(bf16[8,4,3072]{2,1,0:T(4,128)(2,1)} %sum_for_z.1), calls=%async_computation.2 | async-start | bytes 393216 | tf_op jit(solution)/shard_map/all_to_all | solution.py:536
